TPU v7x, 32 devices: a whole 2x2x4 slice. The times are simulated.
32 devices in a mesh: dp: 2 (over x), expert: 16 (over z, y, core).
Axes of the slice: x: 2, y: 2, z: 4, core: 2. Of those that a mesh axis runs over, the one named last changes fastest.
Arguments:
- tokens: bfloat16 [1024, 3584], P('expert'), may hold values from -6 to 6
- routes: int32 [1024, 8], P('expert'), may hold values from 0 to 31, all different within a row; in each aligned block of 64 rows (0 to 63, 64 to 127, ...) at most 24 rows name the same one
- gate_quant: int32 [1024, 8], P('expert'), may hold values from 1 to 65535
- swap_codes: int32 [8], replicated, may hold values from 0 to 4
- expert_gate_up: bfloat16 [32, 2, 3584, 1024], P('expert', None, None, 'dp'), may hold values from -0.09375 to 0.09375
- expert_down: bfloat16 [32, 1024, 3584], P('expert', 'dp'), may hold values from -0.1875 to 0.1875
- shared_gate_up: bfloat16 [1024, 2, 3584], P(('dp', 'expert')), may hold values from -0.09375 to 0.09375
- shared_down: bfloat16 [1024, 3584], P(('dp', 'expert')), may hold values from -0.1875 to 0.1875
Outputs:
- layer_out: bfloat16 [1024, 3584], P('expert', 'dp')
Inputs may be any that keep to these rules, and one draw needn't show every extreme that they name: `routes`: in each aligned block of 64 rows (the rows of one index of expert) no slot id is named by more than 24 rows, a bound that some block reaches.
All inputs are finite; a program needn't handle non-finite values.
Results may differ from a plain program's by a relative error of at most 0.007.
Values may be sent and summed in bfloat16 or wider, within the bound.
No kernel may reach another device: no remote copies, remote signals or barrier semaphores. Data moves between devices by JAX's collectives and lax.ppermute only.
A program may use at most 192 MiB of HBM per device.

v0:
```python
import jax
import jax.numpy as jnp
from jax import lax
from jax.sharding import PartitionSpec as P

routed_scale = 2.5


def shifted(x, axis, by):
    peers = lax.axis_size(axis)
    return lax.ppermute(x, axis, [(i, (i + by) % peers) for i in range(peers)])


def local(
    tokens, routes, gate_quant, swap_codes, expert_gate_up, expert_down, shared_gate_up, shared_down
):
    axis_width = lax.axis_size("expert")
    half_width = axis_width // 2
    per_device = expert_down.shape[0]
    tok_rows = tokens.shape[0]
    model_dim = tokens.shape[1]
    top_count = routes.shape[1]
    experts = per_device * axis_width
    capacity = 3 * tok_rows * top_count // (2 * experts)
    my_index = lax.axis_index("expert")
    expert_ids = jnp.arange(experts, dtype=jnp.int32)
    rows_gate_up = lax.all_gather(shared_gate_up, "expert", axis=0, tiled=True)
    rows_down = lax.all_gather(shared_down, "expert", axis=0, tiled=True)
    projected = jnp.einsum("td,rgd->gtr", tokens, rows_gate_up, preferred_element_type=jnp.float32)
    activated = (jax.nn.silu(projected[0]) * projected[1]).astype(jnp.bfloat16)
    shared_part = jnp.dot(activated, rows_down, preferred_element_type=jnp.float32)
    pair_ids = jnp.arange(half_width, dtype=jnp.int32)
    my_code = jnp.sum(jnp.where(pair_ids == my_index % half_width, swap_codes, 0))
    give_slot = jnp.where(
        my_index < half_width, (my_code - 1) // per_device, (my_code - 1) % per_device
    )
    give_slot = jnp.clip(give_slot, 0, per_device - 1)
    block_gate_up = lax.dynamic_index_in_dim(expert_gate_up, give_slot, 0, keepdims=False)
    block_down = lax.dynamic_index_in_dim(expert_down, give_slot, 0, keepdims=False)
    traded_gate_up, traded_down = shifted((block_gate_up, block_down), "expert", half_width)
    take_new = (my_code > 0) & (jnp.arange(per_device, dtype=jnp.int32) == give_slot)
    resident_gate_up = jnp.where(
        take_new[:, None, None, None], traded_gate_up[None], expert_gate_up
    )
    resident_down = jnp.where(take_new[:, None, None], traded_down[None], expert_down)
    flat_target = routes.reshape(-1)
    assign_count = flat_target.shape[0]
    onehot = (flat_target[:, None] == expert_ids[None, :]).astype(jnp.int32)
    rank_in = jnp.sum((jnp.cumsum(onehot, axis=0) - 1) * onehot, axis=1)
    slot_place = flat_target * capacity + rank_in
    source = (
        jnp.zeros((experts * capacity,), jnp.int32)
        .at[slot_place]
        .set(jnp.arange(1, assign_count + 1, dtype=jnp.int32))
    )
    filled = source > 0
    picked_rows = jnp.take(tokens, jnp.maximum(source - 1, 0) // top_count, axis=0)
    outgoing = jnp.where(filled[:, None], picked_rows, jnp.zeros_like(picked_rows))
    outgoing = outgoing.reshape(axis_width, per_device, capacity, model_dim)
    projected = jnp.einsum(
        "nemd,egdh->gnemh",
        lax.all_to_all(outgoing, "expert", split_axis=0, concat_axis=0, tiled=True),
        resident_gate_up,
        preferred_element_type=jnp.float32,
    )
    activated = (jax.nn.silu(projected[0]) * projected[1]).astype(jnp.bfloat16)
    partial_out = jnp.einsum(
        "nemh,ehd->nemd", activated, resident_down, preferred_element_type=jnp.float32
    ).astype(jnp.bfloat16)
    returned = lax.all_to_all(partial_out, "expert", split_axis=0, concat_axis=0, tiled=True)
    out_width = returned.shape[3]
    per_slot = returned.reshape(experts * capacity, out_width)
    gathered = jnp.take(per_slot, slot_place, axis=0).reshape(tok_rows, top_count, out_width)
    quant_float = gate_quant.astype(jnp.float32)
    gate_weights = routed_scale * quant_float / jnp.sum(quant_float, axis=1, keepdims=True)
    routed = jnp.einsum("tk,tkd->td", gate_weights, gathered.astype(jnp.float32))
    local_term = routed + shared_part
    total = lax.psum_scatter(local_term, "dp", scatter_dimension=1, tiled=True)
    return total.astype(jnp.bfloat16)


def solution(mesh):
    in_specs = (
        P("expert", None),
        P("expert", None),
        P("expert", None),
        P(),
        P("expert", None, None, "dp"),
        P("expert", "dp", None),
        P(("dp", "expert"), None, None),
        P(("dp", "expert"), None),
    )
    out_specs = P("expert", "dp")
    return jax.shard_map(local, mesh=mesh, in_specs=in_specs, out_specs=out_specs, check_vma=False)
```

profile of v0, /device:TPU:0, one launch (start us, length us, event | category | flops | bytes accessed | tf_op | source)
XLA Modules:
  0.0 873.0 jit_solution(12615954827809064467)
XLA Ops:
  6.5 0.0 copy-start
  6.5 0.8 copy.30
  7.4 0.1 eq.49
  7.5 0.1 reshape.98
  7.5 0.7 broadcast_multiply_fusion
  8.3 1.2 reduce-window.6
  9.4 0.2 slice_reduce_fusion
  9.7 0.1 copy.35
  9.8 0.1 mul.47
  9.9 0.1 fusion.34
  10.0 2.4 scatter_custom_fusion
  12.5 0.1 broadcast_in_dim.87
  12.6 0.1 broadcast_in_dim.89
  12.7 0.0 copy-done
  12.7 5.4 gather_fusion
  18.1 5.7 select_select_fusion
  23.8 0.0 copy-start.4
  23.8 7.6 all-to-all-start
  31.4 0.0 all-gather.3.cloned.1.call-start
  31.4 0.0 copy-done.4
  31.4 0.6 fusion.40
  32.8 6.5 dynamic-slice_bitcast_fusion
  39.3 0.0 copy-start.1
  39.3 2.8 collective-permute-start.1
  42.0 4.1 dynamic-slice_bitcast_fusion.1
  46.1 0.2 collective-permute-start
  46.3 0.0 copy-done.1
  46.3 0.8 copy.39
  47.1 0.0 all-gather.3.cloned.1.call-update
  47.8 543.7 %collective-permute-done.1 = bf16[2,3584,512]{2,1,0:T(8,128)(2,1)} collective-permute-done((bf16[2,3584,512]{2,1,0:T(8,128)(2,1)}, bf16[2,3584,512]{2,1,0:T(8,128)(2,1)}, u32[]{:S(2)}, u32[]{:S(2)}) %collective-permute-start.1) | collective-permute-done | bytes 7340064 | tf_op jit(solution)/shard_map/ppermute | solution.py:11
  591.5 0.0 all-to-all-done
  591.5 14.0 %fusion.19 = f32[2,16,2,24,512]{4,3,1,0,2:T(8,128)} fusion(bf16[2,2,3584,512]{3,2,1,0:T(8,128)(2,1)} %param.12, pred[2]{0:T(512)(128)(4,1)S(1)} %compare_and_fusion.2, bf16[2,3584,512]{2,1,0:T(8,128)(2,1)} %collective-permute-done.1, bf16[16,2,24,3584]{3,2,1,0:T(8,128)(2,1)} %all-to-all-done), kind=kOutput, calls=%fused_computation.23 | convolution fusion | flops 5644484608 | bytes 30670850 | tf_op jit(solution)/shard_map/nemd,egdh->gnemh/dot_general | solution.py:60
  605.5 64.2 %collective-permute-done = bf16[512,3584]{1,0:T(8,128)(2,1)} collective-permute-done((bf16[512,3584]{1,0:T(8,128)(2,1)}, bf16[512,3584]{1,0:T(8,128)(2,1)}, u32[]{:S(2)}, u32[]{:S(2)}) %collective-permute-start) | collective-permute-done | bytes 3670048 | tf_op jit(solution)/shard_map/ppermute | solution.py:11
  669.6 7.4 fusion.12
  677.1 3.0 copy.38
  680.1 0.0 copy-start.2
  680.1 0.0 copy-start.3
  680.1 4.7 all-to-all-start.1
  684.8 0.0 all-gather.5.cloned.1.call-start
  684.9 0.7 all-gather.5.cloned.1.call-update
  685.6 0.2 reduce-scatter.2.cloned.1.call-start
  685.8 0.1 reduce_sum.33
  685.9 0.1 copy.33
  686.0 0.0 copy-done.2
  686.0 0.1 copy.34
  686.1 0.0 copy-done.3
  686.1 0.1 copy.43
  686.3 0.0 all-gather.3.cloned.1.call-done
  686.3 5.4 convolution_bitcast_fusion
  691.7 115.7 %all-to-all-done.1 = bf16[16,2,24,3584]{3,2,1,0:T(8,128)(2,1)} async-done(((bf16[16,2,24,3584]{3,2,1,0:T(8,128)(2,1)}), bf16[16,2,24,3584]{3,2,1,0:T(8,128)(2,1)}, u32[]{:S(2)}, u32[]{:S(2)}) %all-to-all-start.1) | async-done | bytes 5505056 | tf_op jit(solution)/shard_map/all_to_all | solution.py:70
  807.4 11.2 %gather_fusion.1 = bf16[512,3584]{1,0:T(8,128)(2,1)} fusion(bf16[768,3584]{1,0:T(8,128)(2,1)} %bitcast.16, s32[1024]{0:T(1024)S(1)} %pad_clamp_fusion), kind=kCustom, calls=%fused_computation.1 | custom fusion | bytes 7342080 | tf_op jit(solution)/shard_map/jit(_take)/gather | solution.py:73
  818.5 3.2 fusion.16
  821.8 0.0 all-gather.5.cloned.1.call-done
  821.8 3.7 convolution_add_fusion
  825.5 0.0 reduce-scatter.2.cloned.1.call-update
  825.5 39.2 %reduce-scatter.2.cloned.1.call-done = f32[64,1792]{1,0:T(8,128)} async-done(((f32[64,3584]{1,0:T(8,128)}), f32[64,1792]{1,0:T(8,128)}) %reduce-scatter.2.cloned.1.call-update) | async-done | bytes 458768 | tf_op jit(solution)/shard_map/reduce_scatter | solution.py:78
  864.7 1.7 convert_element_type.30
  (12 shorter events, 0.1 us)
Async XLA Ops:
  6.5 6.1 copy-start
  23.8 7.6 copy-start.4
  23.8 567.7 %all-to-all-start = ((bf16[16,2,24,3584]{3,2,1,0:T(8,128)(2,1)}), bf16[16,2,24,3584]{3,2,1,0:T(8,128)(2,1)}, u32[]{:S(2)}, u32[]{:S(2)}) async-start(bf16[16,2,24,3584]{3,2,1,0:T(8,128)(2,1)} %select_select_fusion), calls=%async_computation | async-start | bytes 11010048 | tf_op jit(solution)/shard_map/all_to_all | solution.py:62
  31.4 654.9 %all-gather.3.cloned.1.call-start = ((), (), s32[]{:S(2)}) async-start(), calls=%async_computation.3 | async-start | bytes 7798784 | tf_op jit(solution)/shard_map/all_gather | solution.py:27
  39.3 7.0 copy-start.1
  39.3 552.2 %collective-permute-start.1 = (bf16[2,3584,512]{2,1,0:T(8,128)(2,1)}, bf16[2,3584,512]{2,1,0:T(8,128)(2,1)}, u32[]{:S(2)}, u32[]{:S(2)}) collective-permute-start(bf16[2,3584,512]{2,1,0:T(8,128)(2,1)} %dynamic-slice_bitcast_fusion), channel_id=1, source_target_pairs={{0,8},{1,9},{2,10},{3,11},{4,12},{5,13},{6,14},{7,15},{8,0},{9,1},... | collective-permute-start | bytes 22020104 | tf_op jit(solution)/shard_map/ppermute | solution.py:11
  46.1 623.6 %collective-permute-start = (bf16[512,3584]{1,0:T(8,128)(2,1)}, bf16[512,3584]{1,0:T(8,128)(2,1)}, u32[]{:S(2)}, u32[]{:S(2)}) collective-permute-start(bf16[512,3584]{1,0:T(8,128)(2,1)} %dynamic-slice_bitcast_fusion.1), channel_id=1, source_target_pairs={{0,8},{1,9},{2,10},{3,11},{4,12},{5,13},{6,14},{7,15},{8,0},{9,1},... | collective-permute-start | bytes 11010056 | tf_op jit(solution)/shard_map/ppermute | solution.py:11
  680.1 5.9 copy-start.2
  680.1 6.0 copy-start.3
  680.1 127.3 %all-to-all-start.1 = ((bf16[16,2,24,3584]{3,2,1,0:T(8,128)(2,1)}), bf16[16,2,24,3584]{3,2,1,0:T(8,128)(2,1)}, u32[]{:S(2)}, u32[]{:S(2)}) async-start(bf16[16,2,24,3584]{3,2,1,0:T(8,128)(2,1)} %copy.38), calls=%async_computation.1 | async-start | bytes 11010048 | tf_op jit(solution)/shard_map/all_to_all | solution.py:70
  684.8 137.0 %all-gather.5.cloned.1.call-start = ((), (), s32[]{:S(2)}) async-start(), calls=%async_computation.4 | async-start | bytes 3899392 | tf_op jit(solution)/shard_map/all_gather | solution.py:28
  685.6 179.1 %reduce-scatter.2.cloned.1.call-start = ((), (), s32[]{:S(2)}) async-start(), calls=%async_computation.5 | async-start | bytes 1376256 | tf_op jit(solution)/shard_map/reduce_scatter | solution.py:78
Sparse Core Ops, SparseCore 0:
  47.2 357.4 all-gather.2
  688.0 108.8 all-gather.4
  825.7 39.0 reduce-scatter.1
where the time goes:
time: 874 us; the launch traced here: 873 us
  waiting for transfers between devices  764 us (87%)
  local copies, waits for them, and re-layouts  35.4 us (4%)
  matrix products  33.7 us (4%)
  starting transfers between devices  15.5 us (2%)
  between operations  14.6 us (2%)
  other arithmetic  10.1 us (1%)
    ppermute x2, waiting for transfers between devices, shifted(): return lax.ppermute(x, axis, [(i, (i + by) % peers) for i in range(peers)])  608 us
    all_to_all x1, waiting for transfers between devices, local(): lax.all_to_all(partial_out, 'expert', split_axis=0, concat_axis=0, tiled=...  116 us
    reduce_scatter x1, waiting for transfers between devices, local(): total = lax.psum_scatter(local_term, 'dp', scatter_dimension=1, tiled=True)  39.2 us
  transfers between devices with their start and end apart: 7, of which 4 were waited for; matrix products, arithmetic and copies ran while one was open for 6% of the time, Pallas kernels for 0%

commit v1 on v0

--- a/solution.py
+++ b/solution.py
@@ -6,9 +6,23 @@
 routed_scale = 2.5
 
 
-def shifted(x, axis, by):
-    peers = lax.axis_size(axis)
-    return lax.ppermute(x, axis, [(i, (i + by) % peers) for i in range(peers)])
+def remapped(routes, swap_codes, per_device, half_width):
+    owner = routes // per_device
+    slot = routes % per_device
+    pair_ids = jnp.arange(half_width, dtype=jnp.int32)
+    code = jnp.sum(
+        jnp.where((owner % half_width)[..., None] == pair_ids, swap_codes, 0), axis=-1
+    )
+    lower = owner < half_width
+    low_slot = (code - 1) // per_device
+    high_slot = (code - 1) % per_device
+    traded = (code > 0) & (slot == jnp.where(lower, low_slot, high_slot))
+    partner = jnp.where(
+        lower,
+        (owner + half_width) * per_device + high_slot,
+        (owner - half_width) * per_device + low_slot,
+    )
+    return jnp.where(traded, partner, routes)
 
 
 def local(
@@ -22,28 +36,13 @@
     top_count = routes.shape[1]
     experts = per_device * axis_width
     capacity = 3 * tok_rows * top_count // (2 * experts)
-    my_index = lax.axis_index("expert")
     expert_ids = jnp.arange(experts, dtype=jnp.int32)
     rows_gate_up = lax.all_gather(shared_gate_up, "expert", axis=0, tiled=True)
     rows_down = lax.all_gather(shared_down, "expert", axis=0, tiled=True)
     projected = jnp.einsum("td,rgd->gtr", tokens, rows_gate_up, preferred_element_type=jnp.float32)
     activated = (jax.nn.silu(projected[0]) * projected[1]).astype(jnp.bfloat16)
     shared_part = jnp.dot(activated, rows_down, preferred_element_type=jnp.float32)
-    pair_ids = jnp.arange(half_width, dtype=jnp.int32)
-    my_code = jnp.sum(jnp.where(pair_ids == my_index % half_width, swap_codes, 0))
-    give_slot = jnp.where(
-        my_index < half_width, (my_code - 1) // per_device, (my_code - 1) % per_device
-    )
-    give_slot = jnp.clip(give_slot, 0, per_device - 1)
-    block_gate_up = lax.dynamic_index_in_dim(expert_gate_up, give_slot, 0, keepdims=False)
-    block_down = lax.dynamic_index_in_dim(expert_down, give_slot, 0, keepdims=False)
-    traded_gate_up, traded_down = shifted((block_gate_up, block_down), "expert", half_width)
-    take_new = (my_code > 0) & (jnp.arange(per_device, dtype=jnp.int32) == give_slot)
-    resident_gate_up = jnp.where(
-        take_new[:, None, None, None], traded_gate_up[None], expert_gate_up
-    )
-    resident_down = jnp.where(take_new[:, None, None], traded_down[None], expert_down)
-    flat_target = routes.reshape(-1)
+    flat_target = remapped(routes, swap_codes, per_device, half_width).reshape(-1)
     assign_count = flat_target.shape[0]
     onehot = (flat_target[:, None] == expert_ids[None, :]).astype(jnp.int32)
     rank_in = jnp.sum((jnp.cumsum(onehot, axis=0) - 1) * onehot, axis=1)
@@ -60,12 +59,12 @@
     projected = jnp.einsum(
         "nemd,egdh->gnemh",
         lax.all_to_all(outgoing, "expert", split_axis=0, concat_axis=0, tiled=True),
-        resident_gate_up,
+        expert_gate_up,
         preferred_element_type=jnp.float32,
     )
     activated = (jax.nn.silu(projected[0]) * projected[1]).astype(jnp.bfloat16)
     partial_out = jnp.einsum(
-        "nemh,ehd->nemd", activated, resident_down, preferred_element_type=jnp.float32
+        "nemh,ehd->nemd", activated, expert_down, preferred_element_type=jnp.float32
     ).astype(jnp.bfloat16)
     returned = lax.all_to_all(partial_out, "expert", split_axis=0, concat_axis=0, tiled=True)
     out_width = returned.shape[3]

time: 874 us -> 411 us (0.47)
  waiting for transfers between devices: 764 us -> 300 us
  starting transfers between devices: 15.5 us -> 32.9 us
  local copies, waits for them, and re-layouts: 35.4 us -> 24 us
    ppermute x2 -> x0, waiting for transfers between devices: 608 us -> none  [shifted(): return lax.ppermute(x, axis, [(i, (i + by) % peers) for i in range(peers)])]
    all_to_all x1, waiting for transfers between devices: 0.01 us -> 144 us  [local(): lax.all_to_all(outgoing, 'expert', split_axis=0, concat_axis=0, tiled=True)]
    all_to_all x1, starting transfers between devices: 4.74 us -> 25.1 us  [local(): lax.all_to_all(partial_out, 'expert', split_axis=0, concat_axis=0, tiled=...]
    squeeze x2 -> x0, local copies, waits for them, and re-layouts: 10.6 us -> none  [the longest x1 6.5 us: local(): lax.dynamic_index_in_dim(expert_gate_up, give_slot, 0, keepdims=False)]
  transfers between devices with their start and end apart: 7 -> 5, of which waited for: 4 -> 3; matrix products, arithmetic and copies ran while one was open for 6% -> 10% of each run, Pallas kernels for 0% -> 0%
where the time goes in v1:
time: 411 us; the launch traced here: 410 us
  waiting for transfers between devices  300 us (73%)
  starting transfers between devices  32.9 us (8%)
  matrix products  29.6 us (7%)
  local copies, waits for them, and re-layouts  24 us (6%)
  between operations  13.3 us (3%)
  other arithmetic  11 us (3%)
    all_to_all x1, waiting for transfers between devices, local(): lax.all_to_all(outgoing, 'expert', split_axis=0, concat_axis=0, tiled=True)  144 us
    all_to_all x1, waiting for transfers between devices, local(): lax.all_to_all(partial_out, 'expert', split_axis=0, concat_axis=0, tiled=...  116 us
    reduce_scatter x1, waiting for transfers between devices, local(): total = lax.psum_scatter(local_term, 'dp', scatter_dimension=1, tiled=True)  39.2 us
    all_to_all x1, starting transfers between devices, local(): lax.all_to_all(partial_out, 'expert', split_axis=0, concat_axis=0, tiled=...  25.1 us
    gather x1, local copies, waits for them, and re-layouts, local(): jnp.take(per_slot, slot_place, axis=0)  11.2 us
    dot_general x1, matrix products, local(): jnp.einsum('nemd,egdh->gnemh', lax.all_to_all(outgoing, 'expert', split_a...  10.8 us
  transfers between devices with their start and end apart: 5, of which 3 were waited for; matrix products, arithmetic and copies ran while one was open for 10% of the time, Pallas kernels for 0%

profile of v1, /device:TPU:0, one launch (start us, length us, event | category | flops | bytes accessed | tf_op | source)
XLA Modules:
  0.0 410.4 jit_solution(8325245481699456807)
XLA Ops:
  6.5 0.0 copy-start
  6.5 0.8 add_select_fusion.4
  7.3 0.7 select_reduce_fusion
  8.0 0.7 broadcast_multiply_fusion
  8.7 0.1 copy.35
  8.8 0.1 eq.50
  8.9 0.1 reshape.87
  9.0 1.2 reduce-window.6
  10.2 0.2 slice_reduce_fusion
  10.5 0.1 copy.40
  10.6 0.1 mul.55
  10.7 0.1 fusion.28
  10.8 2.4 scatter_custom_fusion
  13.3 0.1 broadcast_in_dim.54
  13.4 0.1 broadcast_in_dim.56
  13.5 0.0 copy-done
  13.5 5.4 %gather_fusion = bf16[768,3584]{1,0:T(8,128)(2,1)} fusion(bf16[64,3584]{1,0:T(8,128)(2,1)S(1)} %copy-done, s32[1024]{0:T(1024)S(1)} %pad_clamp_fusion.1), kind=kCustom, calls=%fused_computation | custom fusion | bytes 11013120 | tf_op jit(solution)/shard_map/jit(_take)/gather | solution.py:56
  18.9 5.6 %select_select_fusion = bf16[16,2,24,3584]{3,2,1,0:T(8,128)(2,1)} fusion(bf16[16,2,24,3584]{3,2,1,0:T(8,128)(2,1)} %bitcast.84, pred[16,2,24]{2,1,0:T(4,128)(4,1)S(1)} %broadcast_in_dim.56, pred[16,2,24]{2,1,0:T(4,128)(4,1)S(1)} %broadcast_in_dim.54), kind=kLoop, calls=%fused_computation.10 | loop fusion | flops 5505024 | bytes 11011584 | tf_op jit(solution)/shard_map/jit(_where)/select_n | solution.py:57
  24.5 0.0 copy-start.1
  24.5 7.6 %all-to-all-start = ((bf16[16,2,24,3584]{3,2,1,0:T(8,128)(2,1)}), bf16[16,2,24,3584]{3,2,1,0:T(8,128)(2,1)}, u32[]{:S(2)}, u32[]{:S(2)}) async-start(bf16[16,2,24,3584]{3,2,1,0:T(8,128)(2,1)} %select_select_fusion), calls=%async_computation | async-start | bytes 11010048 | tf_op jit(solution)/shard_map/all_to_all | solution.py:61
  32.1 0.0 all-gather.3.cloned.1.call-start
  32.2 0.0 copy-done.1
  32.2 0.8 copy.44
  33.0 0.0 all-gather.3.cloned.1.call-update
  33.0 143.8 %all-to-all-done = bf16[16,2,24,3584]{3,2,1,0:T(8,128)(2,1)} async-done(((bf16[16,2,24,3584]{3,2,1,0:T(8,128)(2,1)}), bf16[16,2,24,3584]{3,2,1,0:T(8,128)(2,1)}, u32[]{:S(2)}, u32[]{:S(2)}) %all-to-all-start) | async-done | bytes 5505056 | tf_op jit(solution)/shard_map/all_to_all | solution.py:61
  176.8 10.8 %fusion.13 = f32[2,16,2,24,512]{4,3,0,1,2:T(8,128)S(1)} fusion(bf16[2,2,3584,512]{3,2,1,0:T(8,128)(2,1)} %param.12, bf16[16,2,24,3584]{3,2,1,0:T(8,128)(2,1)} %all-to-all-done), kind=kOutput, calls=%fused_computation.15 | convolution fusion | flops 5637144576 | bytes 23330816 | tf_op jit(solution)/shard_map/nemd,egdh->gnemh/dot_general | solution.py:59
  187.7 6.5 %fusion.7 = bf16[16,2,24,3584]{3,2,0,1:T(8,128)(2,1)S(1)} fusion(bf16[2,512,3584]{2,1,0:T(8,128)(2,1)} %param.13, f32[2,16,2,24,512]{4,3,0,1,2:T(8,128)S(1)} %fusion.13), kind=kOutput, calls=%fused_computation.8 | convolution fusion | flops 2823684096 | bytes 15990784 | tf_op jit(solution)/shard_map/nemh,ehd->nemd/dot_general | solution.py:66
  194.2 2.9 copy.43
  197.1 0.0 copy-start.2
  197.1 25.1 %all-to-all-start.1 = ((bf16[16,2,24,3584]{3,2,1,0:T(8,128)(2,1)}), bf16[16,2,24,3584]{3,2,1,0:T(8,128)(2,1)}, u32[]{:S(2)}, u32[]{:S(2)}) async-start(bf16[16,2,24,3584]{3,2,1,0:T(8,128)(2,1)} %copy.43), calls=%async_computation.1 | async-start | bytes 11010048 | tf_op jit(solution)/shard_map/all_to_all | solution.py:69
  222.2 0.0 all-gather.5.cloned.1.call-start
  222.2 0.7 all-gather.5.cloned.1.call-update
  222.9 0.2 reduce-scatter.2.cloned.1.call-start
  223.2 0.1 reduce_sum.34
  223.3 0.1 copy.38
  223.3 0.1 copy.39
  223.4 0.0 copy-done.2
  223.5 0.1 copy.48
  223.6 0.0 all-gather.3.cloned.1.call-done
  223.6 5.4 %convolution_bitcast_fusion = f32[2,64,512]{2,1,0:T(8,128)S(1)} fusion(bf16[512,2,3584]{2,0,1:T(8,128)(2,1)} %all-gather.3.cloned.1.call-done, bf16[64,3584]{1,0:T(8,128)(2,1)S(1)} %copy-done), kind=kOutput, calls=%fused_computation.21 | convolution fusion | flops 469762048 | bytes 8060928 | tf_op jit(solution)/shard_map/td,rgd->gtr/dot_general | solution.py:42
  229.0 115.8 %all-to-all-done.1 = bf16[16,2,24,3584]{3,2,1,0:T(8,128)(2,1)} async-done(((bf16[16,2,24,3584]{3,2,1,0:T(8,128)(2,1)}), bf16[16,2,24,3584]{3,2,1,0:T(8,128)(2,1)}, u32[]{:S(2)}, u32[]{:S(2)}) %all-to-all-start.1) | async-done | bytes 5505056 | tf_op jit(solution)/shard_map/all_to_all | solution.py:69
  344.8 11.2 %gather_fusion.1 = bf16[512,3584]{1,0:T(8,128)(2,1)} fusion(bf16[768,3584]{1,0:T(8,128)(2,1)} %bitcast.14, s32[1024]{0:T(1024)S(1)} %pad_clamp_fusion), kind=kCustom, calls=%fused_computation.1 | custom fusion | bytes 7342080 | tf_op jit(solution)/shard_map/jit(_take)/gather | solution.py:72
  356.0 3.2 fusion.11
  359.2 0.0 all-gather.5.cloned.1.call-done
  359.2 3.7 convolution_add_fusion
  362.9 0.0 reduce-scatter.2.cloned.1.call-update
  362.9 39.2 %reduce-scatter.2.cloned.1.call-done = f32[64,1792]{1,0:T(8,128)} async-done(((f32[64,3584]{1,0:T(8,128)}), f32[64,1792]{1,0:T(8,128)}) %reduce-scatter.2.cloned.1.call-update) | async-done | bytes 458768 | tf_op jit(solution)/shard_map/reduce_scatter | solution.py:77
  402.2 1.7 convert_element_type.30
  (11 shorter events, 0.1 us)
Async XLA Ops:
  6.5 6.9 %copy-start = (bf16[64,3584]{1,0:T(8,128)(2,1)S(1)}, bf16[64,3584]{1,0:T(8,128)(2,1)}, u32[]{:S(2)}) copy-start(bf16[64,3584]{1,0:T(8,128)(2,1)} %param.8) | copy-start | bytes 1376260
  24.5 7.6 %copy-start.1 = (bf16[32,2,3584]{2,1,0:T(2,128)(2,1)S(1)}, bf16[32,2,3584]{2,1,0:T(2,128)(2,1)}, u32[]{:S(2)}) copy-start(bf16[32,2,3584]{2,1,0:T(2,128)(2,1)} %param.14) | copy-start | bytes 1376260
  24.5 152.3 %all-to-all-start = ((bf16[16,2,24,3584]{3,2,1,0:T(8,128)(2,1)}), bf16[16,2,24,3584]{3,2,1,0:T(8,128)(2,1)}, u32[]{:S(2)}, u32[]{:S(2)}) async-start(bf16[16,2,24,3584]{3,2,1,0:T(8,128)(2,1)} %select_select_fusion), calls=%async_computation | async-start | bytes 11010048 | tf_op jit(solution)/shard_map/all_to_all | solution.py:61
  32.1 191.5 %all-gather.3.cloned.1.call-start = ((), (), s32[]{:S(2)}) async-start(), calls=%async_computation.3 | async-start | bytes 7798784 | tf_op jit(solution)/shard_map/all_gather | solution.py:40
  197.1 26.4 %copy-start.2 = (s32[64,8]{0,1:T(8,128)S(1)}, s32[64,8]{0,1:T(8,128)}, u32[]{:S(2)}) copy-start(s32[64,8]{0,1:T(8,128)} %param.10) | copy-start | bytes 6148
  197.1 147.7 %all-to-all-start.1 = ((bf16[16,2,24,3584]{3,2,1,0:T(8,128)(2,1)}), bf16[16,2,24,3584]{3,2,1,0:T(8,128)(2,1)}, u32[]{:S(2)}, u32[]{:S(2)}) async-start(bf16[16,2,24,3584]{3,2,1,0:T(8,128)(2,1)} %copy.43), calls=%async_computation.1 | async-start | bytes 11010048 | tf_op jit(solution)/shard_map/all_to_all | solution.py:69
  222.2 137.0 %all-gather.5.cloned.1.call-start = ((), (), s32[]{:S(2)}) async-start(), calls=%async_computation.4 | async-start | bytes 3899392 | tf_op jit(solution)/shard_map/all_gather | solution.py:41
  222.9 179.2 %reduce-scatter.2.cloned.1.call-start = ((), (), s32[]{:S(2)}) async-start(), calls=%async_computation.5 | async-start | bytes 1376256 | tf_op jit(solution)/shard_map/reduce_scatter | solution.py:77
Sparse Core Ops, SparseCore 0:
  35.2 132.9 all-gather.2
  225.3 108.9 all-gather.4
  363.1 39.0 reduce-scatter.1

commit v2 on v1

v2 whole, which is shorter than its diff:
```python
import jax
import jax.numpy as jnp
from jax import lax
from jax.sharding import PartitionSpec as P

routed_scale = 2.5
f32 = jnp.float32
bf16 = jnp.bfloat16


def remapped(routes, swap_codes, per_device, half_width):
    owner = routes // per_device
    slot = routes % per_device
    pair_ids = jnp.arange(half_width, dtype=jnp.int32)
    code = jnp.sum(
        jnp.where((owner % half_width)[..., None] == pair_ids, swap_codes, 0), axis=-1
    )
    lower = owner < half_width
    low_slot = (code - 1) // per_device
    high_slot = (code - 1) % per_device
    traded = (code > 0) & (slot == jnp.where(lower, low_slot, high_slot))
    partner = jnp.where(
        lower,
        (owner + half_width) * per_device + high_slot,
        (owner - half_width) * per_device + low_slot,
    )
    return jnp.where(traded, partner, routes)


def hop(x, by):
    return lax.ppermute(x, "expert", [(i, i ^ by) for i in range(lax.axis_size("expert"))])


def hop_x(x, by):
    return lax.ppermute(x, "dp", [(i, i ^ by) for i in range(lax.axis_size("dp"))])


def local(
    tokens, routes, gate_quant, swap_codes, expert_gate_up, expert_down, shared_gate_up, shared_down
):
    axis_width = lax.axis_size("expert")
    nx = lax.axis_size("dp")
    ny = nx
    nz = axis_width // (2 * ny)
    zs = 2 * ny
    per_device = expert_down.shape[0]
    tok_rows, model_dim = tokens.shape
    experts = per_device * axis_width
    me = lax.axis_index("expert")
    mx = lax.axis_index("dp")
    part = tok_rows // nx
    width = model_dim // nx

    target = remapped(routes, swap_codes, per_device, axis_width // 2)
    quant = gate_quant.astype(f32)
    gates = routed_scale * quant / jnp.sum(quant, axis=1, keepdims=True)
    expert_ids = jnp.arange(experts, dtype=jnp.int32)
    table = jnp.sum(jnp.where(target[:, :, None] == expert_ids, gates[:, :, None], 0.0), axis=1)
    every = lax.all_gather(table, "expert", axis=0, tiled=False)
    mine = lax.dynamic_slice_in_dim(every, me * per_device, per_device, axis=2)
    weight = jnp.take(mine, jnp.arange(axis_width) ^ me, axis=0)

    def canonical(parts):
        stacked = jnp.stack(parts)
        return jnp.take(stacked, jnp.arange(nx) ^ mx, axis=0).reshape(tok_rows, model_dim)

    own_part = lax.dynamic_slice_in_dim(tokens, mx * part, part, axis=0)
    by_z = {k: hop(own_part, k * zs) for k in range(1, nz)}
    blocks = {(0, 0): tokens}
    for j in range(1, ny):
        blocks[0, j] = hop(tokens, 2 * j)
    for k in range(1, nz):
        for j in range(ny):
            first = by_z[k] if j == 0 else hop(by_z[k], 2 * j)
            blocks[k, j] = canonical([first] + [hop_x(first, h) for h in range(1, nx)])

    sg = shared_gate_up[:, 0, :]
    su = shared_gate_up[:, 1, :]

    def layer(rows, scale):
        total = None
        for e in range(per_device):
            g = jnp.dot(rows, expert_gate_up[e, 0], preferred_element_type=f32)
            u = jnp.dot(rows, expert_gate_up[e, 1], preferred_element_type=f32)
            act = (jax.nn.silu(g) * u * scale[:, e : e + 1]).astype(bf16)
            out = jnp.dot(act, expert_down[e], preferred_element_type=f32)
            total = out if total is None else total + out
        g = lax.dot_general(rows, sg, (((1,), (1,)), ((), ())), preferred_element_type=f32)
        u = lax.dot_general(rows, su, (((1,), (1,)), ((), ())), preferred_element_type=f32)
        act = (jax.nn.silu(g) * u).astype(bf16)
        return total + jnp.dot(act, shared_down, preferred_element_type=f32)

    def feature_part(v, h):
        return lax.dynamic_slice_in_dim(v, (mx ^ h) * width, width, axis=v.ndim - 1)

    def added(own, others):
        total = own.astype(f32)
        for other in others:
            total = total + other.astype(f32)
        return total

    done = {}
    for k in range(nz):
        own_rows = jnp.concatenate([blocks[k, j] for j in range(ny)], axis=0)
        rows = jnp.concatenate([own_rows, hop(own_rows, 1)], axis=0)
        scale = weight[k * zs : (k + 1) * zs].reshape(ny, 2, tok_rows, per_device)
        scale = scale.transpose(1, 0, 2, 3).reshape(-1, per_device)
        out = layer(rows, scale)
        half = ny * tok_rows
        from_core = hop(out[half:].astype(bf16), 1)
        chip = added(out[:half], [from_core]).astype(bf16).reshape(ny, tok_rows, model_dim)
        if k % 2:
            got = [hop_x(feature_part(chip, h), h) for h in range(1, nx)]
            chip = added(feature_part(chip, 0), got).astype(bf16)
            got = [hop(chip[j], 2 * j) for j in range(1, ny)]
            plane = added(chip[0], got)
        else:
            got = [hop(chip[j], 2 * j) for j in range(1, ny)]
            chip = added(chip[0], got).astype(bf16)
            got = [hop_x(feature_part(chip, h), h) for h in range(1, nx)]
            plane = added(feature_part(chip, 0), got)
        done[k] = plane if k == 0 else hop(plane.astype(bf16), k * zs)
    return added(done[0], [done[k] for k in range(1, nz)]).astype(bf16)


def solution(mesh):
    in_specs = (
        P("expert", None),
        P("expert", None),
        P("expert", None),
        P(),
        P("expert", None, None, "dp"),
        P("expert", "dp", None),
        P(("dp", "expert"), None, None),
        P(("dp", "expert"), None),
    )
    out_specs = P("expert", "dp")
    return jax.shard_map(local, mesh=mesh, in_specs=in_specs, out_specs=out_specs, check_vma=False)
```

time: 411 us -> 286 us (0.70)
  waiting for transfers between devices: 300 us -> 46.2 us
  matrix products: 29.6 us -> 129 us
  blocking collectives: 0 us -> 22.4 us
  between operations: 13.3 us -> 0.4 us
  other arithmetic: 11 us -> 21.4 us
  local copies, waits for them, and re-layouts: 24 us -> 29.2 us
    all_to_all x2 -> x0, waiting for transfers between devices: 260 us -> none  [the longest x1 144 us: local(): lax.all_to_all(outgoing, 'expert', split_axis=0, concat_axis=0, tiled=True)]
    dot_general x5 -> x24, matrix products: 29.6 us -> 129 us  [the longest x8 65.2 us: layer(): out = jnp.dot(act, expert_down[e], preferred_element_type=f32)]
    ppermute x0 -> x32, waiting for transfers between devices: none -> 46.2 us  [the longest x22 30.6 us: hop(): lax.ppermute(x, 'expert', [(i, i ^ by) for i in range(lax.axis_size('expe...]
    reduce_scatter x1 -> x0, waiting for transfers between devices: 39.2 us -> none  [local(): total = lax.psum_scatter(local_term, 'dp', scatter_dimension=1, tiled=True)]
    ppermute x0 -> x32, starting transfers between devices: none -> 36.3 us  [the longest x22 25.9 us: hop(): lax.ppermute(x, 'expert', [(i, i ^ by) for i in range(lax.axis_size('expe...]
    all_to_all x2 -> x0, starting transfers between devices: 32.6 us -> none  [the longest x1 25.1 us: local(): lax.all_to_all(partial_out, 'expert', split_axis=0, concat_axis=0, tiled=...]
    all_gather x0 -> x1, blocking collectives: none -> 22.4 us  [local(): every = lax.all_gather(table, 'expert', axis=0, tiled=False)]
    slice x1 -> x12, local copies, waits for them, and re-layouts: 0.22 us -> 12.3 us  [the longest x4 9.34 us: local(): from_core = hop(out[half:].astype(bf16), 1)]
  transfers between devices with their start and end apart: 5 -> 32, of which waited for: 3 -> 11; matrix products, arithmetic and copies ran while one was open for 10% -> 62% of each run, Pallas kernels for 0% -> 0%
where the time goes in v2:
time: 286 us; the launch traced here: 285 us
  matrix products  129 us (45%)
  waiting for transfers between devices  46.2 us (16%)
  starting transfers between devices  36.3 us (13%)
  local copies, waits for them, and re-layouts  29.2 us (10%)
  blocking collectives  22.4 us (8%)
  other arithmetic  21.4 us (7%)
    dot_general x8, matrix products, layer(): out = jnp.dot(act, expert_down[e], preferred_element_type=f32)  65.2 us
    dot_general x8, matrix products, layer(): u = jnp.dot(rows, expert_gate_up[e, 1], preferred_element_type=f32)  32.8 us
    ppermute x22, waiting for transfers between devices, hop(): lax.ppermute(x, 'expert', [(i, i ^ by) for i in range(lax.axis_size('expe...  30.6 us
    ppermute x22, starting transfers between devices, hop(): lax.ppermute(x, 'expert', [(i, i ^ by) for i in range(lax.axis_size('expe...  25.9 us
    dot_general x4, matrix products, layer(): return total + jnp.dot(act, shared_down, preferred_element_type=f32)  25.3 us
    all_gather x1, blocking collectives, local(): every = lax.all_gather(table, 'expert', axis=0, tiled=False)  22.4 us
    ppermute x10, waiting for transfers between devices, hop_x(): lax.ppermute(x, 'dp', [(i, i ^ by) for i in range(lax.axis_size('dp'))])  15.5 us
    ppermute x10, starting transfers between devices, hop_x(): lax.ppermute(x, 'dp', [(i, i ^ by) for i in range(lax.axis_size('dp'))])  10.5 us
  transfers between devices with their start and end apart: 32, of which 11 were waited for; matrix products, arithmetic and copies ran while one was open for 62% of the time, Pallas kernels for 0%

profile of v2, /device:TPU:0, one launch (start us, length us, event | category | flops | bytes accessed | tf_op | source)
XLA Modules:
  0.0 285.1 jit_solution(6608589926656029741)
XLA Ops:
  0.0 1.7 constant_dynamic-slice_fusion.3
  1.7 3.0 %collective-permute-start.5 = (bf16[32,3584]{1,0:T(8,128)(2,1)}, bf16[32,3584]{1,0:T(8,128)(2,1)}, u32[]{:S(2)}, u32[]{:S(2)}) collective-permute-start(bf16[32,3584]{1,0:T(8,128)(2,1)} %constant_dynamic-slice_fusion.3), channel_id=1, source_target_pairs={{0,4},{1,5},{2,6},{3,7},{4,0},{5,1},{6,2},{7,3},{8,12},{9,13},{10,... | collective-permute-start | bytes 688136 | tf_op jit(solution)/shard_map/ppermute | solution.py:31
  4.7 2.6 collective-permute-start.14
  7.3 1.7 collective-permute-start
  13.7 22.4 %all-gather.1 = f32[16,64,32]{1,2,0:T(8,128)S(1)} all-gather(f32[1,64,32]{1,2,0:T(8,128)S(1)} %bitcast.223), channel_id=2, replica_groups=mesh['dp'=2,'expert'=16] {'expert'}, dimensions={0}, use_global_device_ids=true | all-gather | bytes 139264 | tf_op jit(solution)/shard_map/all_gather | solution.py:59
  36.9 2.9 %fusion.152 = (bf16[32,1,3584]{2,1,0:T(2,128)(2,1)}, bf16[32,1,3584]{2,1,0:T(2,128)(2,1)}) fusion(bf16[32,2,3584]{2,1,0:T(2,128)(2,1)} %param.16), kind=kLoop, calls=%fused_computation.227 | loop fusion | bytes 917504 | tf_op jit(solution)/shard_map/slice | solution.py:77
  40.0 1.2 copy_bitcast_fusion
  41.4 1.5 collective-permute-start.6
  44.2 1.3 collective-permute-start.16
  45.5 1.5 collective-permute-start.24
  48.0 2.1 collective-permute-done.6
  51.8 3.1 %collective-permute-done.15 = bf16[32,3584]{1,0:T(8,128)(2,1)S(1)} collective-permute-done((bf16[32,3584]{1,0:T(8,128)(2,1)}, bf16[32,3584]{1,0:T(8,128)(2,1)S(1)}, u32[]{:S(2)}, u32[]{:S(2)}) %collective-permute-start.15) | collective-permute-done | bytes 229408 | tf_op jit(solution)/shard_map/ppermute | solution.py:35
  55.0 1.8 pad_maximum_fusion.9
  56.7 2.6 collective-permute-done.24
  59.3 1.7 pad_maximum_fusion.11
  61.1 1.5 collective-permute-start.8
  62.6 1.3 gather_fusion.1
  63.9 2.4 gather_fusion.3
  66.3 2.4 gather_fusion.5
  69.2 1.5 collective-permute-start.26
  71.8 5.6 %collective-permute-done.17 = bf16[32,3584]{1,0:T(8,128)(2,1)S(1)} collective-permute-done((bf16[32,3584]{1,0:T(8,128)(2,1)}, bf16[32,3584]{1,0:T(8,128)(2,1)S(1)}, u32[]{:S(2)}, u32[]{:S(2)}) %collective-permute-start.17) | collective-permute-done | bytes 229408 | tf_op jit(solution)/shard_map/ppermute | solution.py:35
  78.4 1.3 gather_fusion.2
  79.8 1.4 gather_fusion.4
  82.2 1.3 gather_fusion.6
  83.6 2.0 broadcast_select_fusion.5
  89.3 1.2 constant_dynamic-update-slice_fusion
  90.6 3.9 %fusion.34 = f32[256,512]{1,0:T(8,128)} fusion(bf16[256,3584]{1,0:T(8,128)(2,1)S(1)} %constant_dynamic-update-slice_fusion, bf16[2,2,3584,512]{3,2,1,0:T(8,128)(2,1)} %param.14), kind=kOutput, calls=%fused_computation.49 | convolution fusion | flops 939524096 | bytes 6029312 | tf_op jit(solution)/shard_map/dot_general | solution.py:84
  94.5 4.0 %fusion.10 = f32[256,512]{1,0:T(8,128)} fusion(bf16[256,3584]{1,0:T(8,128)(2,1)S(1)} %constant_dynamic-update-slice_fusion, bf16[2,2,3584,512]{3,2,1,0:T(8,128)(2,1)} %param.14), kind=kOutput, calls=%fused_computation.25 | convolution fusion | flops 939524096 | bytes 6029312 | tf_op jit(solution)/shard_map/dot_general | solution.py:84
  98.5 7.4 %fusion.26 = f32[256,3584]{1,0:T(8,128)} fusion(bf16[2,512,3584]{2,1,0:T(8,128)(2,1)} %param.15, f32[256,512]{1,0:T(8,128)} %fusion.34, bf16[256,3584]{1,0:T(8,128)(2,1)S(1)} %constant_dynamic-update-slice_fusion, bf16[2,2,3584,512]{3,2,1,0:T(8,128)(2,1)} %param.14, f32[256]{0:T(256)S(1)} %bitcast.235), kind=kOutput, calls=%fused_computation.41 | convolution fusion | flops 1879965696 | bytes 13370368 | tf_op jit(solution)/shard_map/dot_general | solution.py:86
  105.9 8.5 %convolution_add_fusion.7 = f32[256,3584]{1,0:T(8,128)} fusion(f32[256,3584]{1,0:T(8,128)} %fusion.26, bf16[2,512,3584]{2,1,0:T(8,128)(2,1)} %param.15, f32[256,512]{1,0:T(8,128)} %fusion.10, bf16[256,3584]{1,0:T(8,128)(2,1)S(1)} %constant_dynamic-update-slice_fusion, bf16[2,2,3584,512]{3,2,1,0:T(8,128)(2,1)} %param.14, f32[256]{0:T(256)S(1)} %bitcast.234), kind=kOutput, calls=%fused_computation.14 | convolution fusion | flops 1880883200 | bytes 17040384 | tf_op jit(solution)/shard_map/dot_general | solution.py:86
  115.0 6.1 %convolution_add_fusion.6 = f32[256,3584]{1,0:T(8,128)} fusion(f32[256,3584]{1,0:T(8,128)} %convolution_add_fusion.7, bf16[32,3584]{1,0:T(8,128)(2,1)S(1)} %copy-done, f32[256,32]{0,1:T(8,128)S(1)} %fusion.160, bf16[256,3584]{1,0:T(8,128)(2,1)S(1)} %constant_dynamic-update-slice_fusion, bf16[32,3584]{1,0:T(8,128)(2,1)S(1)} %get-tuple-element.26), kind=kOutput, calls=%fused_computation.13 | convolution fusion | flops 118407168 | bytes 9666560 | tf_op jit(solution)/shard_map/dot_general | solution.py:91
  121.1 2.5 slice.369
  124.2 4.5 %fusion.28 = f32[256,512]{1,0:T(8,128)} fusion(bf16[2,2,3584,512]{3,2,1,0:T(8,128)(2,1)} %param.14, bf16[128,3584]{1,0:T(8,128)(2,1)} %collective-permute-done.27, bf16[64,3584]{1,0:T(8,128)(2,1)} %bitcast.209, bf16[64,3584]{1,0:T(8,128)(2,1)} %bitcast.202), kind=kOutput, calls=%fused_computation.43 | convolution fusion | flops 945029120 | bytes 6029312 | tf_op jit(solution)/shard_map/dot_general | solution.py:84
  128.7 3.4 %fusion.4 = f32[256,512]{1,0:T(8,128)S(1)} fusion(bf16[2,2,3584,512]{3,2,1,0:T(8,128)(2,1)} %param.14, bf16[128,3584]{1,0:T(8,128)(2,1)} %collective-permute-done.27, bf16[64,3584]{1,0:T(8,128)(2,1)S(1)} %bitcast.210, bf16[64,3584]{1,0:T(8,128)(2,1)S(1)} %bitcast.203), kind=kOutput, calls=%fused_computation.19 | convolution fusion | flops 945029120 | bytes 6029312 | tf_op jit(solution)/shard_map/dot_general | solution.py:84
  132.2 7.8 %fusion.20 = f32[256,3584]{1,0:T(8,128)} fusion(bf16[2,512,3584]{2,1,0:T(8,128)(2,1)} %param.15, f32[256,512]{1,0:T(8,128)} %fusion.28, bf16[2,2,3584,512]{3,2,1,0:T(8,128)(2,1)} %param.14, f32[256]{0:T(256)S(1)} %bitcast.233, bf16[128,3584]{1,0:T(8,128)(2,1)} %collective-permute-done.27, bf16[64,3584]{1,0:T(8,128)(2,1)S(1)} %bitcast.211, ...), kind=kOutput, calls=%fused_computation.35 | convolution fusion | flops 1885470720 | bytes 13370368 | tf_op jit(solution)/shard_map/dot_general | solution.py:86
  140.0 8.5 %convolution_add_fusion.1 = f32[256,3584]{1,0:T(8,128)} fusion(f32[256,3584]{1,0:T(8,128)} %fusion.20, bf16[2,512,3584]{2,1,0:T(8,128)(2,1)} %param.15, f32[256,512]{1,0:T(8,128)S(1)} %fusion.4, bf16[2,2,3584,512]{3,2,1,0:T(8,128)(2,1)} %param.14, f32[256]{0:T(256)S(1)} %bitcast.232, bf16[128,3584]{1,0:T(8,128)(2,1)} %collective-permute-done.27, ...), kind=kOutput, calls=%fused_computation.8 | convolution fusion | flops 1886388224 | bytes 17040384 | tf_op jit(solution)/shard_map/dot_general | solution.py:86
  148.5 1.8 fusion.146
  150.3 6.4 %convolution_add_fusion = f32[256,3584]{1,0:T(8,128)} fusion(f32[256,3584]{1,0:T(8,128)} %convolution_add_fusion.1, bf16[32,3584]{1,0:T(8,128)(2,1)S(1)} %copy-done, f32[256,32]{0,1:T(8,128)S(1)} %fusion.146, bf16[32,3584]{1,0:T(8,128)(2,1)S(1)} %get-tuple-element.27, bf16[128,3584]{1,0:T(8,128)(2,1)} %collective-permute-done.27, ...), kind=kOutput, calls=%fused_computation.7 | convolution fusion | flops 123912192 | bytes 9666560 | tf_op jit(solution)/shard_map/dot_general | solution.py:91
  156.7 2.5 slice.366
  159.3 4.3 %fusion.30 = f32[256,512]{1,0:T(8,128)} fusion(bf16[2,2,3584,512]{3,2,1,0:T(8,128)(2,1)} %param.14, bf16[128,3584]{1,0:T(8,128)(2,1)} %collective-permute-done.18, bf16[64,3584]{1,0:T(8,128)(2,1)S(1)} %bitcast.195, bf16[64,3584]{1,0:T(8,128)(2,1)S(1)} %bitcast.188), kind=kOutput, calls=%fused_computation.45 | convolution fusion | flops 945029120 | bytes 6029312 | tf_op jit(solution)/shard_map/dot_general | solution.py:84
  163.5 4.2 %fusion.6 = f32[256,512]{1,0:T(8,128)} fusion(bf16[2,2,3584,512]{3,2,1,0:T(8,128)(2,1)} %param.14, bf16[128,3584]{1,0:T(8,128)(2,1)} %collective-permute-done.18, bf16[64,3584]{1,0:T(8,128)(2,1)S(1)} %bitcast.196, bf16[64,3584]{1,0:T(8,128)(2,1)S(1)} %bitcast.189), kind=kOutput, calls=%fused_computation.21 | convolution fusion | flops 945029120 | bytes 6029312 | tf_op jit(solution)/shard_map/dot_general | solution.py:84
  167.8 7.6 %fusion.22 = f32[256,3584]{1,0:T(8,128)} fusion(bf16[2,512,3584]{2,1,0:T(8,128)(2,1)} %param.15, f32[256,512]{1,0:T(8,128)} %fusion.30, bf16[2,2,3584,512]{3,2,1,0:T(8,128)(2,1)} %param.14, f32[256]{0:T(256)S(1)} %bitcast.231, bf16[128,3584]{1,0:T(8,128)(2,1)} %collective-permute-done.18, bf16[64,3584]{1,0:T(8,128)(2,1)S(1)} %bitcast.197, ...), kind=kOutput, calls=%fused_computation.37 | convolution fusion | flops 1885470720 | bytes 13370368 | tf_op jit(solution)/shard_map/dot_general | solution.py:86
  175.4 8.6 %convolution_add_fusion.3 = f32[256,3584]{1,0:T(8,128)} fusion(f32[256,3584]{1,0:T(8,128)} %fusion.22, bf16[2,512,3584]{2,1,0:T(8,128)(2,1)} %param.15, f32[256,512]{1,0:T(8,128)} %fusion.6, bf16[2,2,3584,512]{3,2,1,0:T(8,128)(2,1)} %param.14, f32[256]{0:T(256)S(1)} %bitcast.230, bf16[128,3584]{1,0:T(8,128)(2,1)} %collective-permute-done.18, ...), kind=kOutput, calls=%fused_computation.10 | convolution fusion | flops 1886388224 | bytes 17040384 | tf_op jit(solution)/shard_map/dot_general | solution.py:86
  184.0 1.8 fusion.148
  185.8 6.4 %convolution_add_fusion.2 = f32[256,3584]{1,0:T(8,128)} fusion(f32[256,3584]{1,0:T(8,128)} %convolution_add_fusion.3, bf16[32,3584]{1,0:T(8,128)(2,1)S(1)} %copy-done, f32[256,32]{0,1:T(8,128)S(1)} %fusion.148, bf16[32,3584]{1,0:T(8,128)(2,1)S(1)} %get-tuple-element.27, bf16[128,3584]{1,0:T(8,128)(2,1)} %collective-permute-done.18, ...), kind=kOutput, calls=%fused_computation.9 | convolution fusion | flops 123912192 | bytes 9666560 | tf_op jit(solution)/shard_map/dot_general | solution.py:91
  192.1 2.5 slice.367
  195.1 4.2 %fusion.32 = f32[256,512]{1,0:T(8,128)} fusion(bf16[2,2,3584,512]{3,2,1,0:T(8,128)(2,1)} %param.14, bf16[128,3584]{1,0:T(8,128)(2,1)} %collective-permute-done.9, bf16[64,3584]{1,0:T(8,128)(2,1)S(1)} %bitcast.181, bf16[64,3584]{1,0:T(8,128)(2,1)S(1)} %bitcast.174), kind=kOutput, calls=%fused_computation.47 | convolution fusion | flops 945029120 | bytes 6029312 | tf_op jit(solution)/shard_map/dot_general | solution.py:84
  199.4 4.2 %fusion.8 = f32[256,512]{1,0:T(8,128)} fusion(bf16[2,2,3584,512]{3,2,1,0:T(8,128)(2,1)} %param.14, bf16[128,3584]{1,0:T(8,128)(2,1)} %collective-permute-done.9, bf16[64,3584]{1,0:T(8,128)(2,1)S(1)} %bitcast.182, bf16[64,3584]{1,0:T(8,128)(2,1)S(1)} %bitcast.175), kind=kOutput, calls=%fused_computation.23 | convolution fusion | flops 945029120 | bytes 6029312 | tf_op jit(solution)/shard_map/dot_general | solution.py:84
  203.6 7.7 %fusion.24 = f32[256,3584]{1,0:T(8,128)} fusion(bf16[2,512,3584]{2,1,0:T(8,128)(2,1)} %param.15, f32[256,512]{1,0:T(8,128)} %fusion.32, bf16[2,2,3584,512]{3,2,1,0:T(8,128)(2,1)} %param.14, f32[256]{0:T(256)S(1)} %bitcast.229, bf16[128,3584]{1,0:T(8,128)(2,1)} %collective-permute-done.9, bf16[64,3584]{1,0:T(8,128)(2,1)S(1)} %bitcast.183, ...), kind=kOutput, calls=%fused_computation.39 | convolution fusion | flops 1885470720 | bytes 13370368 | tf_op jit(solution)/shard_map/dot_general | solution.py:86
  211.3 9.0 %convolution_add_fusion.5 = f32[256,3584]{1,0:T(8,128)} fusion(f32[256,3584]{1,0:T(8,128)} %fusion.24, bf16[2,512,3584]{2,1,0:T(8,128)(2,1)} %param.15, f32[256,512]{1,0:T(8,128)} %fusion.8, bf16[2,2,3584,512]{3,2,1,0:T(8,128)(2,1)} %param.14, f32[256]{0:T(256)S(1)} %bitcast.228, bf16[128,3584]{1,0:T(8,128)(2,1)} %collective-permute-done.9, ...), kind=kOutput, calls=%fused_computation.12 | convolution fusion | flops 1886388224 | bytes 17040384 | tf_op jit(solution)/shard_map/dot_general | solution.py:86
  220.3 1.8 fusion.150
  222.0 6.5 %convolution_add_fusion.4 = f32[256,3584]{1,0:T(8,128)} fusion(f32[256,3584]{1,0:T(8,128)} %convolution_add_fusion.5, bf16[32,3584]{1,0:T(8,128)(2,1)S(1)} %copy-done, f32[256,32]{0,1:T(8,128)S(1)} %fusion.150, bf16[32,3584]{1,0:T(8,128)(2,1)S(1)} %get-tuple-element.27, bf16[128,3584]{1,0:T(8,128)(2,1)} %collective-permute-done.9, ...), kind=kOutput, calls=%fused_computation.11 | convolution fusion | flops 123912192 | bytes 9666560 | tf_op jit(solution)/shard_map/dot_general | solution.py:91
  228.5 1.7 slice.368
  230.4 1.9 fusion.71
  235.9 1.5 collective-permute-start.11
  237.4 8.3 %collective-permute-done.3 = bf16[64,3584]{1,0:T(8,128)(2,1)S(1)} collective-permute-done((bf16[64,3584]{1,0:T(8,128)(2,1)S(1)}, bf16[64,3584]{1,0:T(8,128)(2,1)S(1)}, u32[]{:S(2)}, u32[]{:S(2)}) %collective-permute-start.3) | collective-permute-done | bytes 458784 | tf_op jit(solution)/shard_map/ppermute | solution.py:31
  247.0 1.4 collective-permute-start.30
  248.3 7.2 %collective-permute-done.20 = bf16[64,3584]{1,0:T(8,128)(2,1)S(1)} collective-permute-done((bf16[64,3584]{1,0:T(8,128)(2,1)S(1)}, bf16[64,3584]{1,0:T(8,128)(2,1)S(1)}, u32[]{:S(2)}, u32[]{:S(2)}) %collective-permute-start.20) | collective-permute-done | bytes 458784 | tf_op jit(solution)/shard_map/ppermute | solution.py:31
  256.8 1.4 collective-permute-start.12
  258.2 2.3 collective-permute-done.30
  260.5 3.9 %collective-permute-start.31 = (bf16[64,1792]{1,0:T(8,128)(2,1)S(1)}, bf16[64,1792]{1,0:T(8,128)(2,1)S(1)}, u32[]{:S(2)}, u32[]{:S(2)}) collective-permute-start(bf16[64,1792]{1,0:T(8,128)(2,1)S(1)} %fusion.72), channel_id=1, source_target_pairs={{0,12},{1,13},{2,14},{3,15},{4,8},{5,9},{6,10},{7,11},{8,4},{9,5},... | collective-permute-start | bytes 688136 | tf_op jit(solution)/shard_map/ppermute | solution.py:31
  264.4 1.3 collective-permute-done.21
  265.8 4.9 %collective-permute-start.22 = (bf16[64,1792]{1,0:T(8,128)(2,1)S(1)}, bf16[64,1792]{1,0:T(8,128)(2,1)S(1)}, u32[]{:S(2)}, u32[]{:S(2)}) collective-permute-start(bf16[64,1792]{1,0:T(8,128)(2,1)S(1)} %add_convert_fusion.5), channel_id=1, source_target_pairs={{0,8},{1,9},{2,10},{3,11},{4,12},{5,13},{6,14},{7,15},{8,0},{9,1},... | collective-permute-start | bytes 688136 | tf_op jit(solution)/shard_map/ppermute | solution.py:31
  271.4 12.8 %collective-permute-done.22 = bf16[64,1792]{1,0:T(8,128)(2,1)S(1)} collective-permute-done((bf16[64,1792]{1,0:T(8,128)(2,1)S(1)}, bf16[64,1792]{1,0:T(8,128)(2,1)S(1)}, u32[]{:S(2)}, u32[]{:S(2)}) %collective-permute-start.22) | collective-permute-done | bytes 229408 | tf_op jit(solution)/shard_map/ppermute | solution.py:31
  (126 shorter events, 26.8 us)
Async XLA Ops:
  0.0 115.0 %copy-start = (bf16[32,3584]{1,0:T(8,128)(2,1)S(1)}, bf16[32,3584]{1,0:T(8,128)(2,1)}, u32[]{:S(2)}) copy-start(bf16[32,3584]{1,0:T(8,128)(2,1)} %param.17) | copy-start | bytes 688132
  0.0 47.0 %copy-start.12 = (bf16[64,3584]{1,0:T(8,128)(2,1)S(1)}, bf16[64,3584]{1,0:T(8,128)(2,1)}, u32[]{:S(2)}) copy-start(bf16[64,3584]{1,0:T(8,128)(2,1)} %param.10) | copy-start | bytes 1376260
  1.7 39.7 %collective-permute-start.5 = (bf16[32,3584]{1,0:T(8,128)(2,1)}, bf16[32,3584]{1,0:T(8,128)(2,1)}, u32[]{:S(2)}, u32[]{:S(2)}) collective-permute-start(bf16[32,3584]{1,0:T(8,128)(2,1)} %constant_dynamic-slice_fusion.3), channel_id=1, source_target_pairs={{0,4},{1,5},{2,6},{3,7},{4,0},{5,1},{6,2},{7,3},{8,12},{9,13},{10,... | collective-permute-start | bytes 688136 | tf_op jit(solution)/shard_map/ppermute | solution.py:31
  4.7 39.0 %collective-permute-start.14 = (bf16[32,3584]{1,0:T(8,128)(2,1)}, bf16[32,3584]{1,0:T(8,128)(2,1)}, u32[]{:S(2)}, u32[]{:S(2)}) collective-permute-start(bf16[32,3584]{1,0:T(8,128)(2,1)} %constant_dynamic-slice_fusion.3), channel_id=1, source_target_pairs={{0,8},{1,9},{2,10},{3,11},{4,12},{5,13},{6,14},{7,15},{8,0},{9,1},... | collective-permute-start | bytes 688136 | tf_op jit(solution)/shard_map/ppermute | solution.py:31
  7.3 36.9 %collective-permute-start.23 = (bf16[32,3584]{1,0:T(8,128)(2,1)}, bf16[32,3584]{1,0:T(8,128)(2,1)}, u32[]{:S(2)}, u32[]{:S(2)}) collective-permute-start(bf16[32,3584]{1,0:T(8,128)(2,1)} %constant_dynamic-slice_fusion.3), channel_id=1, source_target_pairs={{0,12},{1,13},{2,14},{3,15},{4,8},{5,9},{6,10},{7,11},{8,4},{9,5},... | collective-permute-start | bytes 688136 | tf_op jit(solution)/shard_map/ppermute | solution.py:31
  7.3 38.2 %collective-permute-start = (bf16[64,3584]{1,0:T(8,128)(2,1)}, bf16[64,3584]{1,0:T(8,128)(2,1)S(1)}, u32[]{:S(2)}, u32[]{:S(2)}) collective-permute-start(bf16[64,3584]{1,0:T(8,128)(2,1)} %param.10), channel_id=1, source_target_pairs={{0,2},{1,3},{2,0},{3,1},{4,6},{5,7},{6,4},{7,5},{8,10},{9,11},{10,... | collective-permute-start | bytes 1376264 | tf_op jit(solution)/shard_map/ppermute | solution.py:31
  41.4 8.7 %collective-permute-start.6 = (bf16[32,3584]{1,0:T(8,128)(2,1)}, bf16[32,3584]{1,0:T(8,128)(2,1)S(1)}, u32[]{:S(2)}, u32[]{:S(2)}) collective-permute-start(bf16[32,3584]{1,0:T(8,128)(2,1)} %collective-permute-done.5), channel_id=1, source_target_pairs={{0,16},{16,0},{1,17},{17,1},{2,18},{18,2},{3,19},{19,3},{4,20},{20... | collective-permute-start | bytes 688136 | tf_op jit(solution)/shard_map/ppermute | solution.py:35
  42.9 18.2 %collective-permute-start.7 = (bf16[32,3584]{1,0:T(8,128)(2,1)}, bf16[32,3584]{1,0:T(8,128)(2,1)}, u32[]{:S(2)}, u32[]{:S(2)}) collective-permute-start(bf16[32,3584]{1,0:T(8,128)(2,1)} %collective-permute-done.5), channel_id=1, source_target_pairs={{0,2},{1,3},{2,0},{3,1},{4,6},{5,7},{6,4},{7,5},{8,10},{9,11},{10,... | collective-permute-start | bytes 688136 | tf_op jit(solution)/shard_map/ppermute | solution.py:31
  43.7 11.3 %collective-permute-start.15 = (bf16[32,3584]{1,0:T(8,128)(2,1)}, bf16[32,3584]{1,0:T(8,128)(2,1)S(1)}, u32[]{:S(2)}, u32[]{:S(2)}) collective-permute-start(bf16[32,3584]{1,0:T(8,128)(2,1)} %collective-permute-done.14), channel_id=1, source_target_pairs={{0,16},{16,0},{1,17},{17,1},{2,18},{18,2},{3,19},{19,3},{4,20},{20... | collective-permute-start | bytes 688136 | tf_op jit(solution)/shard_map/ppermute | solution.py:35
  44.2 24.4 %collective-permute-start.16 = (bf16[32,3584]{1,0:T(8,128)(2,1)}, bf16[32,3584]{1,0:T(8,128)(2,1)}, u32[]{:S(2)}, u32[]{:S(2)}) collective-permute-start(bf16[32,3584]{1,0:T(8,128)(2,1)} %collective-permute-done.14), channel_id=1, source_target_pairs={{0,2},{1,3},{2,0},{3,1},{4,6},{5,7},{6,4},{7,5},{8,10},{9,11},{10,... | collective-permute-start | bytes 688136 | tf_op jit(solution)/shard_map/ppermute | solution.py:31
  45.5 13.8 %collective-permute-start.24 = (bf16[32,3584]{1,0:T(8,128)(2,1)}, bf16[32,3584]{1,0:T(8,128)(2,1)S(1)}, u32[]{:S(2)}, u32[]{:S(2)}) collective-permute-start(bf16[32,3584]{1,0:T(8,128)(2,1)} %collective-permute-done.23), channel_id=1, source_target_pairs={{0,16},{16,0},{1,17},{17,1},{2,18},{18,2},{3,19},{19,3},{4,20},{20... | collective-permute-start | bytes 688136 | tf_op jit(solution)/shard_map/ppermute | solution.py:35
  50.1 19.2 %collective-permute-start.25 = (bf16[32,3584]{1,0:T(8,128)(2,1)}, bf16[32,3584]{1,0:T(8,128)(2,1)}, u32[]{:S(2)}, u32[]{:S(2)}) collective-permute-start(bf16[32,3584]{1,0:T(8,128)(2,1)} %collective-permute-done.23), channel_id=1, source_target_pairs={{0,2},{1,3},{2,0},{3,1},{4,6},{5,7},{6,4},{7,5},{8,10},{9,11},{10,... | collective-permute-start | bytes 688136 | tf_op jit(solution)/shard_map/ppermute | solution.py:31
  55.0 34.3 %collective-permute-start.1 = (bf16[128,3584]{1,0:T(8,128)(2,1)}, bf16[128,3584]{1,0:T(8,128)(2,1)}, u32[]{:S(2)}, u32[]{:S(2)}) collective-permute-start(bf16[128,3584]{1,0:T(8,128)(2,1)} %pad_maximum_fusion.3), channel_id=1, source_target_pairs={{0,1},{1,0},{2,3},{3,2},{4,5},{5,4},{6,7},{7,6},{8,9},{9,8},{10,11... | collective-permute-start | bytes 2752520 | tf_op jit(solution)/shard_map/ppermute | solution.py:31
  61.1 9.6 %collective-permute-start.8 = (bf16[32,3584]{1,0:T(8,128)(2,1)}, bf16[32,3584]{1,0:T(8,128)(2,1)}, u32[]{:S(2)}, u32[]{:S(2)}) collective-permute-start(bf16[32,3584]{1,0:T(8,128)(2,1)} %collective-permute-done.7), channel_id=1, source_target_pairs={{0,16},{16,0},{1,17},{17,1},{2,18},{18,2},{3,19},{19,3},{4,20},{20... | collective-permute-start | bytes 688136 | tf_op jit(solution)/shard_map/ppermute | solution.py:35
  68.7 8.8 %collective-permute-start.17 = (bf16[32,3584]{1,0:T(8,128)(2,1)}, bf16[32,3584]{1,0:T(8,128)(2,1)S(1)}, u32[]{:S(2)}, u32[]{:S(2)}) collective-permute-start(bf16[32,3584]{1,0:T(8,128)(2,1)} %collective-permute-done.16), channel_id=1, source_target_pairs={{0,16},{16,0},{1,17},{17,1},{2,18},{18,2},{3,19},{19,3},{4,20},{20... | collective-permute-start | bytes 688136 | tf_op jit(solution)/shard_map/ppermute | solution.py:35
  69.2 11.9 %collective-permute-start.26 = (bf16[32,3584]{1,0:T(8,128)(2,1)}, bf16[32,3584]{1,0:T(8,128)(2,1)}, u32[]{:S(2)}, u32[]{:S(2)}) collective-permute-start(bf16[32,3584]{1,0:T(8,128)(2,1)} %collective-permute-done.25), channel_id=1, source_target_pairs={{0,16},{16,0},{1,17},{17,1},{2,18},{18,2},{3,19},{19,3},{4,20},{20... | collective-permute-start | bytes 688136 | tf_op jit(solution)/shard_map/ppermute | solution.py:35
  85.6 5.0 %copy-start.4 = (bf16[2,32,3584]{2,1,0:T(8,128)(2,1)}, bf16[2,32,3584]{2,1,0:T(8,128)(2,1)S(1)}, u32[]{:S(2)}) copy-start(bf16[2,32,3584]{2,1,0:T(8,128)(2,1)S(1)} %get-tuple-element.22) | copy-start | bytes 1376260
  85.6 5.0 %copy-start.6 = (bf16[2,32,3584]{2,1,0:T(8,128)(2,1)}, bf16[2,32,3584]{2,1,0:T(8,128)(2,1)S(1)}, u32[]{:S(2)}) copy-start(bf16[2,32,3584]{2,1,0:T(8,128)(2,1)S(1)} %get-tuple-element.23) | copy-start | bytes 1376260
  85.6 5.0 %copy-start.8 = (bf16[2,32,3584]{2,1,0:T(8,128)(2,1)}, bf16[2,32,3584]{2,1,0:T(8,128)(2,1)S(1)}, u32[]{:S(2)}) copy-start(bf16[2,32,3584]{2,1,0:T(8,128)(2,1)S(1)} %get-tuple-element.24) | copy-start | bytes 1376260
  85.6 5.0 %copy-start.10 = (bf16[2,32,3584]{2,1,0:T(8,128)(2,1)}, bf16[2,32,3584]{2,1,0:T(8,128)(2,1)S(1)}, u32[]{:S(2)}) copy-start(bf16[2,32,3584]{2,1,0:T(8,128)(2,1)S(1)} %get-tuple-element.25) | copy-start | bytes 1376260
  86.7 37.5 %collective-permute-start.27 = (bf16[128,3584]{1,0:T(8,128)(2,1)}, bf16[128,3584]{1,0:T(8,128)(2,1)}, u32[]{:S(2)}, u32[]{:S(2)}) collective-permute-start(bf16[128,3584]{1,0:T(8,128)(2,1)} %pad_maximum_fusion.6), channel_id=1, source_target_pairs={{0,1},{1,0},{2,3},{3,2},{4,5},{5,4},{6,7},{7,6},{8,9},{9,8},{10,11... | collective-permute-start | bytes 2752520 | tf_op jit(solution)/shard_map/ppermute | solution.py:31
  87.7 71.6 %collective-permute-start.18 = (bf16[128,3584]{1,0:T(8,128)(2,1)}, bf16[128,3584]{1,0:T(8,128)(2,1)}, u32[]{:S(2)}, u32[]{:S(2)}) collective-permute-start(bf16[128,3584]{1,0:T(8,128)(2,1)} %pad_maximum_fusion.5), channel_id=1, source_target_pairs={{0,1},{1,0},{2,3},{3,2},{4,5},{5,4},{6,7},{7,6},{8,9},{9,8},{10,11... | collective-permute-start | bytes 2752520 | tf_op jit(solution)/shard_map/ppermute | solution.py:31
  89.3 105.8 %collective-permute-start.9 = (bf16[128,3584]{1,0:T(8,128)(2,1)}, bf16[128,3584]{1,0:T(8,128)(2,1)}, u32[]{:S(2)}, u32[]{:S(2)}) collective-permute-start(bf16[128,3584]{1,0:T(8,128)(2,1)} %pad_maximum_fusion.4), channel_id=1, source_target_pairs={{0,1},{1,0},{2,3},{3,2},{4,5},{5,4},{6,7},{7,6},{8,9},{9,8},{10,11... | collective-permute-start | bytes 2752520 | tf_op jit(solution)/shard_map/ppermute | solution.py:31
  123.7 5.1 %copy-start.9 = (bf16[2,32,3584]{2,1,0:T(8,128)(2,1)S(1)}, bf16[2,32,3584]{2,1,0:T(8,128)(2,1)}, u32[]{:S(2)}) copy-start(bf16[2,32,3584]{2,1,0:T(8,128)(2,1)} %copy-done.8) | copy-start | bytes 1376260
  123.7 5.1 %copy-start.11 = (bf16[2,32,3584]{2,1,0:T(8,128)(2,1)S(1)}, bf16[2,32,3584]{2,1,0:T(8,128)(2,1)}, u32[]{:S(2)}) copy-start(bf16[2,32,3584]{2,1,0:T(8,128)(2,1)} %copy-done.10) | copy-start | bytes 1376260
  123.7 106.7 %collective-permute-start.2 = (bf16[128,3584]{1,0:T(8,128)(2,1)}, bf16[128,3584]{1,0:T(8,128)(2,1)}, u32[]{:S(2)}, u32[]{:S(2)}) collective-permute-start(bf16[128,3584]{1,0:T(8,128)(2,1)} %slice.369), channel_id=1, source_target_pairs={{0,1},{1,0},{2,3},{3,2},{4,5},{5,4},{6,7},{7,6},{8,9},{9,8},{10,11... | collective-permute-start | bytes 2752520 | tf_op jit(solution)/shard_map/ppermute | solution.py:31
  150.3 9.0 %copy-start.5 = (bf16[2,32,3584]{2,1,0:T(8,128)(2,1)S(1)}, bf16[2,32,3584]{2,1,0:T(8,128)(2,1)}, u32[]{:S(2)}) copy-start(bf16[2,32,3584]{2,1,0:T(8,128)(2,1)} %copy-done.4) | copy-start | bytes 1376260
  150.3 9.0 %copy-start.7 = (bf16[2,32,3584]{2,1,0:T(8,128)(2,1)S(1)}, bf16[2,32,3584]{2,1,0:T(8,128)(2,1)}, u32[]{:S(2)}) copy-start(bf16[2,32,3584]{2,1,0:T(8,128)(2,1)} %copy-done.6) | copy-start | bytes 1376260
  159.2 73.9 %collective-permute-start.28 = (bf16[128,3584]{1,0:T(8,128)(2,1)}, bf16[128,3584]{1,0:T(8,128)(2,1)S(1)}, u32[]{:S(2)}, u32[]{:S(2)}) collective-permute-start(bf16[128,3584]{1,0:T(8,128)(2,1)} %slice.366), channel_id=1, source_target_pairs={{0,1},{1,0},{2,3},{3,2},{4,5},{5,4},{6,7},{7,6},{8,9},{9,8},{10,11... | collective-permute-start | bytes 2752520 | tf_op jit(solution)/shard_map/ppermute | solution.py:31
  194.7 39.3 %collective-permute-start.19 = (bf16[128,3584]{1,0:T(8,128)(2,1)}, bf16[128,3584]{1,0:T(8,128)(2,1)S(1)}, u32[]{:S(2)}, u32[]{:S(2)}) collective-permute-start(bf16[128,3584]{1,0:T(8,128)(2,1)} %slice.367), channel_id=1, source_target_pairs={{0,1},{1,0},{2,3},{3,2},{4,5},{5,4},{6,7},{7,6},{8,9},{9,8},{10,11... | collective-permute-start | bytes 2752520 | tf_op jit(solution)/shard_map/ppermute | solution.py:31
  228.5 4.6 %copy-start.1 = (f32[256,3584]{1,0:T(8,128)S(1)}, f32[256,3584]{1,0:T(8,128)}, u32[]{:S(2)}) copy-start(f32[256,3584]{1,0:T(8,128)} %convolution_add_fusion) | copy-start | bytes 11010052
  230.3 5.4 %collective-permute-start.10 = (bf16[128,3584]{1,0:T(8,128)(2,1)S(1)}, bf16[128,3584]{1,0:T(8,128)(2,1)S(1)}, u32[]{:S(2)}, u32[]{:S(2)}) collective-permute-start(bf16[128,3584]{1,0:T(8,128)(2,1)S(1)} %slice.368), channel_id=1, source_target_pairs={{0,1},{1,0},{2,3},{3,2},{4,5},{5,4},{6,7},{7,6},{8,9},{9,8},{10,11... | collective-permute-start | bytes 2752520 | tf_op jit(solution)/shard_map/ppermute | solution.py:31
  232.3 2.0 copy-start.2
  232.3 13.4 %collective-permute-start.3 = (bf16[64,3584]{1,0:T(8,128)(2,1)S(1)}, bf16[64,3584]{1,0:T(8,128)(2,1)S(1)}, u32[]{:S(2)}, u32[]{:S(2)}) collective-permute-start(bf16[64,3584]{1,0:T(8,128)(2,1)S(1)} %slice.190), channel_id=1, source_target_pairs={{0,2},{1,3},{2,0},{3,1},{4,6},{5,7},{6,4},{7,5},{8,10},{9,11},{10,... | collective-permute-start | bytes 1376264 | tf_op jit(solution)/shard_map/ppermute | solution.py:31
  233.4 2.3 copy-start.3
  233.4 13.4 %collective-permute-start.29 = (bf16[2,64,1792]{2,1,0:T(8,128)(2,1)S(1)}, bf16[2,64,1792]{2,1,0:T(8,128)(2,1)S(1)}, u32[]{:S(2)}, u32[]{:S(2)}) collective-permute-start(bf16[2,64,1792]{2,1,0:T(8,128)(2,1)S(1)} %constant_dynamic-slice_fusion), channel_id=1, source_target_pairs={{0,16},{16,0},{1,17},{17,1},{2,18},{18,2},{3,19},{19,3},{4,20},{20... | collective-permute-start | bytes 1376264 | tf_op jit(solution)/shard_map/ppermute | solution.py:35
  234.6 21.0 %collective-permute-start.20 = (bf16[64,3584]{1,0:T(8,128)(2,1)S(1)}, bf16[64,3584]{1,0:T(8,128)(2,1)S(1)}, u32[]{:S(2)}, u32[]{:S(2)}) collective-permute-start(bf16[64,3584]{1,0:T(8,128)(2,1)S(1)} %slice.204), channel_id=1, source_target_pairs={{0,2},{1,3},{2,0},{3,1},{4,6},{5,7},{6,4},{7,5},{8,10},{9,11},{10,... | collective-permute-start | bytes 1376264 | tf_op jit(solution)/shard_map/ppermute | solution.py:31
  235.9 20.8 %collective-permute-start.11 = (bf16[2,64,1792]{2,1,0:T(8,128)(2,1)S(1)}, bf16[2,64,1792]{2,1,0:T(8,128)(2,1)S(1)}, u32[]{:S(2)}, u32[]{:S(2)}) collective-permute-start(bf16[2,64,1792]{2,1,0:T(8,128)(2,1)S(1)} %constant_dynamic-slice_fusion.2), channel_id=1, source_target_pairs={{0,16},{16,0},{1,17},{17,1},{2,18},{18,2},{3,19},{19,3},{4,20},{20... | collective-permute-start | bytes 1376264 | tf_op jit(solution)/shard_map/ppermute | solution.py:35
  245.9 25.6 %collective-permute-start.4 = (bf16[64,1792]{1,0:T(8,128)(2,1)S(1)}, bf16[64,1792]{1,0:T(8,128)(2,1)S(1)}, u32[]{:S(2)}, u32[]{:S(2)}) collective-permute-start(bf16[64,1792]{1,0:T(8,128)(2,1)S(1)} %constant_dynamic-slice_fusion.4), channel_id=1, source_target_pairs={{0,16},{16,0},{1,17},{17,1},{2,18},{18,2},{3,19},{19,3},{4,20},{20... | collective-permute-start | bytes 688136 | tf_op jit(solution)/shard_map/ppermute | solution.py:35
  247.0 13.5 %collective-permute-start.30 = (bf16[64,1792]{1,0:T(8,128)(2,1)S(1)}, bf16[64,1792]{1,0:T(8,128)(2,1)S(1)}, u32[]{:S(2)}, u32[]{:S(2)}) collective-permute-start(bf16[64,1792]{1,0:T(8,128)(2,1)S(1)} %slice_bitcast_fusion), channel_id=1, source_target_pairs={{0,2},{1,3},{2,0},{3,1},{4,6},{5,7},{6,4},{7,5},{8,10},{9,11},{10,... | collective-permute-start | bytes 688136 | tf_op jit(solution)/shard_map/ppermute | solution.py:31
  255.7 10.0 %collective-permute-start.21 = (bf16[64,1792]{1,0:T(8,128)(2,1)S(1)}, bf16[64,1792]{1,0:T(8,128)(2,1)S(1)}, u32[]{:S(2)}, u32[]{:S(2)}) collective-permute-start(bf16[64,1792]{1,0:T(8,128)(2,1)S(1)} %constant_dynamic-slice_fusion.1), channel_id=1, source_target_pairs={{0,16},{16,0},{1,17},{17,1},{2,18},{18,2},{3,19},{19,3},{4,20},{20... | collective-permute-start | bytes 688136 | tf_op jit(solution)/shard_map/ppermute | solution.py:35
  256.8 13.9 %collective-permute-start.12 = (bf16[64,1792]{1,0:T(8,128)(2,1)S(1)}, bf16[64,1792]{1,0:T(8,128)(2,1)S(1)}, u32[]{:S(2)}, u32[]{:S(2)}) collective-permute-start(bf16[64,1792]{1,0:T(8,128)(2,1)S(1)} %slice_bitcast_fusion.2), channel_id=1, source_target_pairs={{0,2},{1,3},{2,0},{3,1},{4,6},{5,7},{6,4},{7,5},{8,10},{9,11},{10,... | collective-permute-start | bytes 688136 | tf_op jit(solution)/shard_map/ppermute | solution.py:31
  260.5 10.9 %collective-permute-start.31 = (bf16[64,1792]{1,0:T(8,128)(2,1)S(1)}, bf16[64,1792]{1,0:T(8,128)(2,1)S(1)}, u32[]{:S(2)}, u32[]{:S(2)}) collective-permute-start(bf16[64,1792]{1,0:T(8,128)(2,1)S(1)} %fusion.72), channel_id=1, source_target_pairs={{0,12},{1,13},{2,14},{3,15},{4,8},{5,9},{6,10},{7,11},{8,4},{9,5},... | collective-permute-start | bytes 688136 | tf_op jit(solution)/shard_map/ppermute | solution.py:31
  265.8 18.4 %collective-permute-start.22 = (bf16[64,1792]{1,0:T(8,128)(2,1)S(1)}, bf16[64,1792]{1,0:T(8,128)(2,1)S(1)}, u32[]{:S(2)}, u32[]{:S(2)}) collective-permute-start(bf16[64,1792]{1,0:T(8,128)(2,1)S(1)} %add_convert_fusion.5), channel_id=1, source_target_pairs={{0,8},{1,9},{2,10},{3,11},{4,12},{5,13},{6,14},{7,15},{8,0},{9,1},... | collective-permute-start | bytes 688136 | tf_op jit(solution)/shard_map/ppermute | solution.py:31
  270.8 13.5 %collective-permute-start.13 = (bf16[64,1792]{1,0:T(8,128)(2,1)S(1)}, bf16[64,1792]{1,0:T(8,128)(2,1)S(1)}, u32[]{:S(2)}, u32[]{:S(2)}) collective-permute-start(bf16[64,1792]{1,0:T(8,128)(2,1)S(1)} %fusion.73), channel_id=1, source_target_pairs={{0,4},{1,5},{2,6},{3,7},{4,0},{5,1},{6,2},{7,3},{8,12},{9,13},{10,... | collective-permute-start | bytes 688136 | tf_op jit(solution)/shard_map/ppermute | solution.py:31

commit v3 on v2

v3 whole, which is shorter than its diff:
```python
import functools

import jax
import jax.numpy as jnp
from jax import lax
from jax.experimental import pallas as pl
from jax.experimental.pallas import tpu as pltpu
from jax.sharding import PartitionSpec as P

routed_scale = 2.5
lanes = 128
f32 = jnp.float32
bf16 = jnp.bfloat16


def remapped(routes, swap_codes, per_device, half_width):
    owner = routes // per_device
    slot = routes % per_device
    pair_ids = jnp.arange(half_width, dtype=jnp.int32)
    code = jnp.sum(
        jnp.where((owner % half_width)[..., None] == pair_ids, swap_codes, 0), axis=-1
    )
    lower = owner < half_width
    low_slot = (code - 1) // per_device
    high_slot = (code - 1) % per_device
    traded = (code > 0) & (slot == jnp.where(lower, low_slot, high_slot))
    partner = jnp.where(
        lower,
        (owner + half_width) * per_device + high_slot,
        (owner - half_width) * per_device + low_slot,
    )
    return jnp.where(traded, partner, routes)


def hop(x, by):
    return lax.ppermute(x, "expert", [(i, i ^ by) for i in range(lax.axis_size("expert"))])


def hop_x(x, by):
    return lax.ppermute(x, "dp", [(i, i ^ by) for i in range(lax.axis_size("dp"))])


def ffn_kernel(
    levels, x_first, nx, ny, tok_rows, top_count, model_dim, hid_tile, out_tile, n_units, *refs
):
    slots = refs[0]
    units = refs[1 : 1 + n_units]
    sh_gu, sh_dn, gu_own, gu_sib, dn_own, dn_sib = refs[1 + n_units : 7 + n_units]
    refs = refs[7 + n_units :]
    outs = [refs[i * nx : (i + 1) * nx] for i in range(len(levels))]
    rows_in, shared_w, wgu, wdn, act, scale, sem_x, sem_s, sem_gu, sem_dn = refs[len(levels) * nx :]
    mx = lax.axis_index("dp")
    part = tok_rows // nx
    width = model_dim // nx
    per_device, _, _, hidden = gu_own.shape
    tiles = hidden // hid_tile
    n_slots = 2 * per_device
    experts_k = n_slots * hidden
    sp = sh_dn.shape[0]

    copies = []
    at = 0
    for i, level in enumerate(levels):
        for j in range(ny):
            base = (i * ny + j) * tok_rows
            for h in range(1 if level == 0 else nx):
                if level == 0:
                    dst = rows_in.at[pl.ds(base, tok_rows)]
                else:
                    start = pl.multiple_of(base + (mx ^ h) * part, part)
                    dst = rows_in.at[pl.ds(start, part)]
                copies.append(pltpu.make_async_copy(units[at], dst, sem_x.at[at]))
                at += 1
    shared_copy = pltpu.make_async_copy(sh_gu, shared_w, sem_s.at[0])

    def gu_copy(src, e, t, i):
        return pltpu.make_async_copy(
            src.at[e, :, :, pl.ds(t * hid_tile, hid_tile)], wgu.at[i], sem_gu.at[i]
        )

    def dn_copy(src, e, h, s):
        column = pl.multiple_of((mx ^ h) * width, lanes)
        return pltpu.make_async_copy(
            src.at[e, :, pl.ds(column, width)],
            wdn.at[h, pl.ds(s * hidden, hidden)],
            sem_dn.at[h, s],
        )

    def sh_copy(h):
        column = pl.multiple_of((mx ^ h) * width, lanes)
        return pltpu.make_async_copy(
            sh_dn.at[:, pl.ds(column, width)],
            wdn.at[h, pl.ds(experts_k, sp)],
            sem_dn.at[h, n_slots],
        )

    for copy in copies:
        copy.start()
    shared_copy.start()
    for s in range(n_slots):
        src = gu_own if s < per_device else gu_sib
        for t in range(tiles):
            gu_copy(src, s % per_device, t, s * tiles + t).start()
    order = list(range(1, nx)) + [0]
    dn_waits = {h: [] for h in order}
    for h in order:
        for s in range(n_slots):
            src = dn_own if s < per_device else dn_sib
            dn_waits[h].append(dn_copy(src, s % per_device, h, s))
        dn_waits[h].append(sh_copy(h))
        for copy in dn_waits[h]:
            copy.start()

    for copy in copies:
        copy.wait()
    extra = rows_in[:, model_dim:].astype(f32)
    named = extra[:, :top_count]
    quant = extra[:, top_count : 2 * top_count] * 256.0 + extra[:, 2 * top_count : 3 * top_count]
    gates = routed_scale * quant / jnp.sum(quant, axis=1, keepdims=True)
    n_rows = rows_in.shape[0]
    for s in range(n_slots):
        mine = jnp.where(named == slots[s].astype(f32), gates, 0.0)
        column = jnp.sum(mine, axis=1, keepdims=True)
        scale[s] = jnp.broadcast_to(column, (n_rows, lanes))

    def silu(v):
        return v / (1.0 + jnp.exp(-v))

    shared_copy.wait()
    both = lax.dot_general(
        rows_in[:, :model_dim],
        shared_w[...],
        (((1,), (1,)), ((), ())),
        preferred_element_type=f32,
    )
    act[:, experts_k : experts_k + sp] = (silu(both[:, :sp]) * both[:, sp:]).astype(bf16)

    @pl.loop(0, n_slots * tiles)
    def _(i):
        pltpu.make_async_copy(
            gu_own.at[0, :, :, pl.ds(0, hid_tile)], wgu.at[i], sem_gu.at[i]
        ).wait()
        g = jnp.dot(rows_in[:, :model_dim], wgu[i, 0], preferred_element_type=f32)
        u = jnp.dot(rows_in[:, :model_dim], wgu[i, 1], preferred_element_type=f32)
        by = scale[i // tiles]
        by = jnp.concatenate([by] * (hid_tile // lanes), axis=1)
        column = pl.multiple_of(i * hid_tile, hid_tile)
        act[:, pl.ds(column, hid_tile)] = (silu(g) * u * by).astype(bf16)

    level_rows = ny * tok_rows
    for h in order:
        for copy in dn_waits[h]:
            copy.wait()

        @pl.loop(0, width // out_tile)
        def _(n):
            column = pl.multiple_of(n * out_tile, out_tile)
            value = jnp.dot(
                act[...], wdn[h, :, pl.ds(column, out_tile)], preferred_element_type=f32
            ).astype(bf16)
            for i in range(len(levels)):
                if x_first[i]:
                    outs[i][h][:, pl.ds(column, out_tile)] = value[
                        i * level_rows : (i + 1) * level_rows
                    ]
                else:
                    for j in range(ny):
                        base = i * level_rows + j * tok_rows
                        outs[i][j][h, :, pl.ds(column, out_tile)] = value[base : base + tok_rows]


def local(
    tokens, routes, gate_quant, swap_codes, expert_gate_up, expert_down, shared_gate_up, shared_down
):
    axis_width = lax.axis_size("expert")
    nx = lax.axis_size("dp")
    ny = nx
    nz = axis_width // (2 * ny)
    zs = 2 * ny
    per_device, hidden, model_dim = expert_down.shape
    tok_rows = tokens.shape[0]
    top_count = routes.shape[1]
    me = lax.axis_index("expert")
    mx = lax.axis_index("dp")
    part = tok_rows // nx
    width = model_dim // nx
    hid_tile = 256 if hidden % 256 == 0 else 128
    out_tile = 256 if width % 256 == 0 else 128

    pad = -3 * top_count % lanes
    wide = jnp.concatenate(
        [
            tokens,
            routes.astype(bf16),
            (gate_quant // 256).astype(bf16),
            (gate_quant % 256).astype(bf16),
            jnp.zeros((tok_rows, pad), bf16),
        ],
        axis=1,
    )
    wide_dim = wide.shape[1]

    gu_sib = hop(expert_gate_up, 1)
    dn_sib = hop(expert_down, 1)
    shared_rows = shared_down.shape[0]
    shared_own = jnp.concatenate(
        [shared_gate_up[:, 0, :], shared_gate_up[:, 1, :], shared_down], axis=0
    )
    shared_both = jnp.stack([shared_own, hop(shared_own, 1)])
    shared_both = shared_both.reshape(2, 3, shared_rows, model_dim).transpose(1, 0, 2, 3)
    shared_both = shared_both.reshape(3, 2 * shared_rows, model_dim)
    shared_both = jnp.pad(shared_both, ((0, 0), (0, -2 * shared_rows % 16), (0, 0)))
    sp = shared_both.shape[1]
    sh_gu = shared_both[:2].reshape(2 * sp, model_dim)
    sh_dn = shared_both[2]

    my_experts = jnp.concatenate(
        [owner * per_device + jnp.arange(per_device, dtype=jnp.int32) for owner in (me, me ^ 1)]
    )
    slots = remapped(my_experts, swap_codes, per_device, axis_width // 2)

    own_part = lax.dynamic_slice_in_dim(wide, mx * part, part, axis=0)
    units = {(0, 0): [wide]}
    for j in range(1, ny):
        units[0, j] = [hop(wide, 2 * j)]
    for k in range(1, nz):
        from_z = hop(own_part, k * zs)
        for j in range(ny):
            first = from_z if j == 0 else hop(from_z, 2 * j)
            units[k, j] = [first] + [hop_x(first, h) for h in range(1, nx)]

    def added(own, others):
        total = own.astype(f32)
        for other in others:
            total = total + other.astype(f32)
        return total

    done = {}
    n_slots = 2 * per_device
    tiles = hidden // hid_tile
    half = nz // 2
    for levels in (list(range(half)), list(range(half, nz))):
        x_first = [k % 2 == 1 for k in levels]
        chunk = [u for k in levels for j in range(ny) for u in units[k, j]]
        n_rows = len(levels) * ny * tok_rows
        out_shape = []
        for first in x_first:
            shape = (ny * tok_rows, width) if first else (nx, tok_rows, width)
            out_shape += [jax.ShapeDtypeStruct(shape, bf16)] * nx
        k_total = n_slots * hidden + sp
        flops = 2 * n_rows * model_dim * (3 * n_slots * hidden + 3 * sp)
        outs = pl.pallas_call(
            functools.partial(
                ffn_kernel,
                levels,
                x_first,
                nx,
                ny,
                tok_rows,
                top_count,
                model_dim,
                hid_tile,
                out_tile,
                len(chunk),
            ),
            out_shape=out_shape,
            in_specs=[pl.BlockSpec(memory_space=pltpu.SMEM)]
            + [pl.BlockSpec(memory_space=pl.ANY)] * (len(chunk) + 6),
            out_specs=[pl.BlockSpec(memory_space=pltpu.VMEM)] * len(out_shape),
            scratch_shapes=[
                pltpu.VMEM((n_rows, wide_dim), bf16),
                pltpu.VMEM((2 * sp, model_dim), bf16),
                pltpu.VMEM((n_slots * tiles, 2, model_dim, hid_tile), bf16),
                pltpu.VMEM((nx, k_total, width), bf16),
                pltpu.VMEM((n_rows, k_total), bf16),
                pltpu.VMEM((n_slots, n_rows, lanes), f32),
                pltpu.SemaphoreType.DMA((len(chunk),)),
                pltpu.SemaphoreType.DMA((1,)),
                pltpu.SemaphoreType.DMA((n_slots * tiles,)),
                pltpu.SemaphoreType.DMA((nx, n_slots + 1)),
            ],
            compiler_params=pltpu.CompilerParams(vmem_limit_bytes=60 * 1024 * 1024),
            cost_estimate=pl.CostEstimate(
                flops=flops,
                bytes_accessed=3 * 2 * n_slots * hidden * model_dim + 6 * n_rows * model_dim,
                transcendentals=0,
            ),
        )(slots, *chunk, sh_gu, sh_dn, expert_gate_up, gu_sib, expert_down, dn_sib)
        for i, k in enumerate(levels):
            sent = outs[i * nx : (i + 1) * nx]
            if x_first[i]:
                got = [hop_x(sent[h], h) for h in range(1, nx)]
                row = added(sent[0], got).astype(bf16).reshape(ny, tok_rows, width)
                got = [hop(row[j], 2 * j) for j in range(1, ny)]
            else:
                got = [hop(sent[j], 2 * j) for j in range(1, ny)]
                row = added(sent[0], got).astype(bf16)
                got = [hop_x(row[h], h) for h in range(1, nx)]
            plane = added(row[0], got)
            done[k] = plane if k == 0 else hop(plane.astype(bf16), k * zs)
    return added(done[0], [done[k] for k in range(1, nz)]).astype(bf16)


def solution(mesh):
    in_specs = (
        P("expert", None),
        P("expert", None),
        P("expert", None),
        P(),
        P("expert", None, None, "dp"),
        P("expert", "dp", None),
        P(("dp", "expert"), None, None),
        P(("dp", "expert"), None),
    )
    out_specs = P("expert", "dp")
    return jax.shard_map(local, mesh=mesh, in_specs=in_specs, out_specs=out_specs, check_vma=False)
```

time: 286 us -> 158 us (0.55)
  matrix products: 129 us -> 0 us
  Pallas kernels: 0 us -> 66.3 us
  local copies, waits for them, and re-layouts: 29.2 us -> 6.22 us
  blocking collectives: 22.4 us -> 0 us
  other arithmetic: 21.4 us -> 3.2 us
    dot_general x24 -> x0, matrix products: 129 us -> none  [the longest x8 65.2 us: layer(): out = jnp.dot(act, expert_down[e], preferred_element_type=f32)]
    pallas_call x0 -> x2, Pallas kernels: none -> 66.3 us  [local(): pl.pallas_call(functools.partial(ffn_kernel, levels, x_first, nx, ny, tok...]
    all_gather x1 -> x0, blocking collectives: 22.4 us -> none  [local(): every = lax.all_gather(table, 'expert', axis=0, tiled=False)]
    gather x7 -> x0, local copies, waits for them, and re-layouts: 10.7 us -> none  [the longest x6 10.1 us: canonical(): jnp.take(stacked, jnp.arange(nx) ^ mx, axis=0).reshape(tok_rows, model_dim)]
    slice x12 -> x5, local copies, waits for them, and re-layouts: 12.3 us -> 2.5 us  [the longest x1 1.01 us: local(): sh_gu = shared_both[:2].reshape(2 * sp, model_dim)]
    another operation x6 -> x0, other arithmetic: 7.64 us -> none  [canonical(): stacked = jnp.stack(parts)]
    ppermute x22 -> x17, waiting for transfers between devices: 30.6 us -> 24.1 us  [hop(): lax.ppermute(x, 'expert', [(i, i ^ by) for i in range(lax.axis_size('expe...]
    ppermute x10, waiting for transfers between devices: 15.5 us -> 21.2 us  [hop_x(): lax.ppermute(x, 'dp', [(i, i ^ by) for i in range(lax.axis_size('dp'))])]
  transfers between devices with their start and end apart: 32 -> 27, of which waited for: 11 -> 10; matrix products, arithmetic and copies ran while one was open for 62% -> 4% of each run, Pallas kernels for 0% -> 42%
where the time goes in v3:
time: 158 us
  Pallas kernels  66.3 us (42%)
  waiting for transfers between devices  45.3 us (29%)
  starting transfers between devices  36.4 us (23%)
  local copies, waits for them, and re-layouts  6.22 us (4%)
  other arithmetic  3.2 us (2%)
    pallas_call x2, Pallas kernels, local(): pl.pallas_call(functools.partial(ffn_kernel, levels, x_first, nx, ny, tok...  66.3 us
    ppermute x17, waiting for transfers between devices, hop(): lax.ppermute(x, 'expert', [(i, i ^ by) for i in range(lax.axis_size('expe...  24.1 us
    ppermute x17, starting transfers between devices, hop(): lax.ppermute(x, 'expert', [(i, i ^ by) for i in range(lax.axis_size('expe...  23.7 us
    ppermute x10, waiting for transfers between devices, hop_x(): lax.ppermute(x, 'dp', [(i, i ^ by) for i in range(lax.axis_size('dp'))])  21.2 us
    ppermute x10, starting transfers between devices, hop_x(): lax.ppermute(x, 'dp', [(i, i ^ by) for i in range(lax.axis_size('dp'))])  12.7 us
  transfers between devices with their start and end apart: 27, of which 10 were waited for; matrix products, arithmetic and copies ran while one was open for 4% of the time, Pallas kernels for 42%

profile of v3, /device:TPU:0, one launch (start us, length us, event | category | flops | bytes accessed | tf_op | source)
XLA Modules:
  0.0 157.8 jit_solution(7488567420596625294)
XLA Ops:
  0.0 0.5 collective-permute-start.6
  0.5 0.1 collective-permute-start.7
  0.5 0.7 convert_element_type.96
  1.2 0.1 copy.22
  1.3 0.8 copy.18
  2.1 1.1 concatenate.24.refs_1_
  3.3 0.0 copy-start.19
  3.3 4.1 %collective-permute-start.13 = (bf16[32,3712]{1,0:T(8,128)(2,1)S(1)}, bf16[32,3712]{1,0:T(8,128)(2,1)S(1)}, u32[]{:S(2)}, u32[]{:S(2)}) collective-permute-start(bf16[32,3712]{1,0:T(8,128)(2,1)S(1)} %constant_dynamic-slice_fusion), channel_id=1, source_target_pairs={{0,8},{1,9},{2,10},{3,11},{4,12},{5,13},{6,14},{7,15},{8,0},{9,1},... | collective-permute-start | bytes 712712 | tf_op jit(solution)/shard_map/ppermute | solution.py:36
  7.4 1.3 collective-permute-start.17
  8.8 0.2 collective-permute-start.1
  9.0 0.6 fusion.10
  9.6 0.0 copy-start.20
  9.6 0.1 copy_bitcast_fusion
  9.8 14.4 %collective-permute-done.13.refs_1_ = bf16[32,3712]{1,0:T(8,128)(2,1)S(1)} collective-permute-done((bf16[32,3712]{1,0:T(8,128)(2,1)S(1)}, bf16[32,3712]{1,0:T(8,128)(2,1)S(1)}, u32[]{:S(2)}, u32[]{:S(2)}) %collective-permute-start.13) | collective-permute-done | bytes 237600 | tf_op jit(solution)/shard_map/ppermute | solution.py:36
  24.2 0.0 collective-permute-start.5
  24.2 1.9 %collective-permute-start.14 = (bf16[32,3712]{1,0:T(8,128)(2,1)S(1)}, bf16[32,3712]{1,0:T(8,128)(2,1)S(1)}, u32[]{:S(2)}, u32[]{:S(2)}) collective-permute-start(bf16[32,3712]{1,0:T(8,128)(2,1)S(1)} %collective-permute-done.13.refs_1_), channel_id=1, source_target_pairs={{0,16},{16,0},{1,17},{17,1},{2,18},{18,2},{3,19},{19,3},{4,20},{20... | collective-permute-start | bytes 712712 | tf_op jit(solution)/shard_map/ppermute | solution.py:40
  26.2 1.5 collective-permute-start.15
  27.7 0.1 and_select_fusion.4
  27.8 4.8 %collective-permute-done.14.refs_2_ = bf16[32,3712]{1,0:T(8,128)(2,1)S(1)} collective-permute-done((bf16[32,3712]{1,0:T(8,128)(2,1)S(1)}, bf16[32,3712]{1,0:T(8,128)(2,1)S(1)}, u32[]{:S(2)}, u32[]{:S(2)}) %collective-permute-start.14) | collective-permute-done | bytes 237600 | tf_op jit(solution)/shard_map/ppermute | solution.py:40
  32.5 1.8 %collective-permute-start.18 = (bf16[32,3712]{1,0:T(8,128)(2,1)S(1)}, bf16[32,3712]{1,0:T(8,128)(2,1)S(1)}, u32[]{:S(2)}, u32[]{:S(2)}) collective-permute-start(bf16[32,3712]{1,0:T(8,128)(2,1)S(1)} %collective-permute-done.17.refs_5_), channel_id=1, source_target_pairs={{0,16},{16,0},{1,17},{17,1},{2,18},{18,2},{3,19},{19,3},{4,20},{20... | collective-permute-start | bytes 712712 | tf_op jit(solution)/shard_map/ppermute | solution.py:40
  34.3 1.5 collective-permute-start.19
  35.8 0.2 select_reduce_fusion
  36.0 0.6 and_select_fusion.refs_0_
  36.6 3.4 %collective-permute-done.18.refs_6_ = bf16[32,3712]{1,0:T(8,128)(2,1)S(1)} collective-permute-done((bf16[32,3712]{1,0:T(8,128)(2,1)S(1)}, bf16[32,3712]{1,0:T(8,128)(2,1)S(1)}, u32[]{:S(2)}, u32[]{:S(2)}) %collective-permute-start.18) | collective-permute-done | bytes 237600 | tf_op jit(solution)/shard_map/ppermute | solution.py:40
  40.0 1.7 %collective-permute-start.3 = (bf16[32,3712]{1,0:T(8,128)(2,1)S(1)}, bf16[32,3712]{1,0:T(8,128)(2,1)S(1)}, u32[]{:S(2)}, u32[]{:S(2)}) collective-permute-start(bf16[32,3712]{1,0:T(8,128)(2,1)S(1)} %collective-permute-done.1.refs_3_), channel_id=1, source_target_pairs={{0,2},{1,3},{2,0},{3,1},{4,6},{5,7},{6,4},{7,5},{8,10},{9,11},{10,... | collective-permute-start | bytes 712712 | tf_op jit(solution)/shard_map/ppermute | solution.py:36
  41.7 1.5 collective-permute-start.16
  43.2 0.5 collective-permute-start.20
  43.7 0.1 maximum_bitcast_fusion
  43.9 1.0 slice.54
  44.9 0.8 slice.55
  45.7 0.9 collective-permute-done.3.refs_5_
  46.6 1.5 collective-permute-start
  48.1 2.3 %collective-permute-done.16.refs_4_ = bf16[32,3712]{1,0:T(8,128)(2,1)S(1)} collective-permute-done((bf16[32,3712]{1,0:T(8,128)(2,1)S(1)}, bf16[32,3712]{1,0:T(8,128)(2,1)S(1)}, u32[]{:S(2)}, u32[]{:S(2)}) %collective-permute-start.16) | collective-permute-done | bytes 237600 | tf_op jit(solution)/shard_map/ppermute | solution.py:40
  50.4 1.5 collective-permute-start.2
  51.9 3.6 %collective-permute-done.20.refs_8_ = bf16[32,3712]{1,0:T(8,128)(2,1)S(1)} collective-permute-done((bf16[32,3712]{1,0:T(8,128)(2,1)S(1)}, bf16[32,3712]{1,0:T(8,128)(2,1)S(1)}, u32[]{:S(2)}, u32[]{:S(2)}) %collective-permute-start.20) | collective-permute-done | bytes 237600 | tf_op jit(solution)/shard_map/ppermute | solution.py:40
  55.5 1.5 collective-permute-start.4
  57.0 33.2 %shard_map.83 = (bf16[2,64,1792]{2,1,0:T(8,128)(2,1)}, bf16[2,64,1792]{2,1,0:T(8,128)(2,1)}, bf16[128,1792]{1,0:T(8,128)(2,1)}, bf16[128,1792]{1,0:T(8,128)(2,1)}) custom-call(s32[4]{0:T(128)} %and_select_fusion.refs_0_, bf16[32,3712]{1,0:T(8,128)(2,1)} %copy-done.8, bf16[32,3712]{1,0:T(8,128)(2,1)} %copy-done.10, bf16[32,3712]{1,0:T(8,128)(2,1)} %copy-done.11, ...), custom_call_target="tpu_custom_call" | custom-call | flops 11626610688 | bytes 49545216 | tf_op jit(solution)/shard_map/pallas_call | solution.py:252
  90.2 0.8 collective-permute-start.24
  91.0 1.1 collective-permute-start.21
  92.1 0.7 copy-done.2
  92.8 0.1 copy-done.15
  93.0 0.7 copy-done.17
  93.6 33.1 %shard_map.82 = (bf16[2,64,1792]{2,1,0:T(8,128)(2,1)}, bf16[2,64,1792]{2,1,0:T(8,128)(2,1)}, bf16[128,1792]{1,0:T(8,128)(2,1)}, bf16[128,1792]{1,0:T(8,128)(2,1)}) custom-call(s32[4]{0:T(128)} %and_select_fusion.refs_0_, bf16[64,3712]{1,0:T(8,128)(2,1)} %copy-done, bf16[64,3712]{1,0:T(8,128)(2,1)} %copy-done.2, bf16[32,3712]{1,0:T(8,128)(2,1)} %copy-done.7, ...), custom_call_target="tpu_custom_call" | custom-call | flops 11626610688 | bytes 49545216 | tf_op jit(solution)/shard_map/pallas_call | solution.py:252
  126.8 0.8 collective-permute-start.10
  127.6 1.5 collective-permute-start.8
  129.1 0.1 add_convert_fusion
  129.3 0.6 collective-permute-start.25
  129.9 0.1 add_convert_fusion.1
  130.0 1.3 collective-permute-start.22
  131.3 7.2 %collective-permute-done.10 = bf16[128,1792]{1,0:T(8,128)(2,1)S(1)} collective-permute-done((bf16[128,1792]{1,0:T(8,128)(2,1)}, bf16[128,1792]{1,0:T(8,128)(2,1)S(1)}, u32[]{:S(2)}, u32[]{:S(2)}) %collective-permute-start.10) | collective-permute-done | bytes 458784 | tf_op jit(solution)/shard_map/ppermute | solution.py:40
  138.5 0.1 add_convert_fusion.2
  138.6 1.4 collective-permute-start.11
  140.0 0.1 add_convert_fusion.3
  140.1 1.1 collective-permute-start.9
  141.3 0.4 collective-permute-done.25
  141.6 0.1 add_convert_fusion.4
  141.7 2.8 %collective-permute-start.26 = (bf16[64,1792]{1,0:T(8,128)(2,1)S(1)}, bf16[64,1792]{1,0:T(8,128)(2,1)S(1)}, u32[]{:S(2)}, u32[]{:S(2)}) collective-permute-start(bf16[64,1792]{1,0:T(8,128)(2,1)S(1)} %add_convert_fusion.4), channel_id=1, source_target_pairs={{0,12},{1,13},{2,14},{3,15},{4,8},{5,9},{6,10},{7,11},{8,4},{9,5},... | collective-permute-start | bytes 688136 | tf_op jit(solution)/shard_map/ppermute | solution.py:36
  144.5 0.1 fusion
  144.5 2.3 %collective-permute-start.23 = (bf16[64,1792]{1,0:T(8,128)(2,1)S(1)}, bf16[64,1792]{1,0:T(8,128)(2,1)S(1)}, u32[]{:S(2)}, u32[]{:S(2)}) collective-permute-start(bf16[64,1792]{1,0:T(8,128)(2,1)S(1)} %fusion), channel_id=1, source_target_pairs={{0,8},{1,9},{2,10},{3,11},{4,12},{5,13},{6,14},{7,15},{8,0},{9,1},... | collective-permute-start | bytes 688136 | tf_op jit(solution)/shard_map/ppermute | solution.py:36
  146.8 0.1 add_convert_fusion.5
  146.8 1.7 %collective-permute-start.12 = (bf16[64,1792]{1,0:T(8,128)(2,1)S(1)}, bf16[64,1792]{1,0:T(8,128)(2,1)S(1)}, u32[]{:S(2)}, u32[]{:S(2)}) collective-permute-start(bf16[64,1792]{1,0:T(8,128)(2,1)S(1)} %add_convert_fusion.5), channel_id=1, source_target_pairs={{0,4},{1,5},{2,6},{3,7},{4,0},{5,1},{6,2},{7,3},{8,12},{9,13},{10,... | collective-permute-start | bytes 688136 | tf_op jit(solution)/shard_map/ppermute | solution.py:36
  148.5 1.2 collective-permute-done.26
  149.7 7.3 %collective-permute-done.23 = bf16[64,1792]{1,0:T(8,128)(2,1)S(1)} collective-permute-done((bf16[64,1792]{1,0:T(8,128)(2,1)S(1)}, bf16[64,1792]{1,0:T(8,128)(2,1)S(1)}, u32[]{:S(2)}, u32[]{:S(2)}) %collective-permute-start.23) | collective-permute-done | bytes 229408 | tf_op jit(solution)/shard_map/ppermute | solution.py:36
  157.0 0.8 fusion.4
  (63 shorter events, 0.3 us)
Async XLA Ops:
  0.0 9.0 %copy-start.1 = (bf16[32,2,3584]{2,1,0:T(2,128)(2,1)S(1)}, bf16[32,2,3584]{2,1,0:T(2,128)(2,1)}, u32[]{:S(2)}) copy-start(bf16[32,2,3584]{2,1,0:T(2,128)(2,1)} %param.14) | copy-start | bytes 1376260
  0.0 57.0 %collective-permute-start.6 = (bf16[2,2,3584,512]{3,2,1,0:T(8,128)(2,1)}, bf16[2,2,3584,512]{3,2,1,0:T(8,128)(2,1)}, u32[]{:S(2)}, u32[]{:S(2)}) collective-permute-start(bf16[2,2,3584,512]{3,2,1,0:T(8,128)(2,1)} %refs_11_.3), channel_id=1, source_target_pairs={{0,1},{1,0},{2,3},{3,2},{4,5},{5,4},{6,7},{7,6},{8,9},{9,8},{10,11... | collective-permute-start | bytes 44040200 | tf_op jit(solution)/shard_map/ppermute | solution.py:36
  0.5 56.5 %collective-permute-start.7 = (bf16[2,512,3584]{2,1,0:T(8,128)(2,1)}, bf16[2,512,3584]{2,1,0:T(8,128)(2,1)}, u32[]{:S(2)}, u32[]{:S(2)}) collective-permute-start(bf16[2,512,3584]{2,1,0:T(8,128)(2,1)} %refs_13_.1), channel_id=1, source_target_pairs={{0,1},{1,0},{2,3},{3,2},{4,5},{5,4},{6,7},{7,6},{8,9},{9,8},{10,11... | collective-permute-start | bytes 22020104 | tf_op jit(solution)/shard_map/ppermute | solution.py:36
  3.3 43.3 %copy-start = (bf16[64,3712]{1,0:T(8,128)(2,1)}, bf16[64,3712]{1,0:T(8,128)(2,1)S(1)}, u32[]{:S(2)}) copy-start(bf16[64,3712]{1,0:T(8,128)(2,1)S(1)} %concatenate.24.refs_1_) | copy-start | bytes 1425412
  3.3 6.4 %copy-start.19 = (bf16[32,3584]{1,0:T(8,128)(2,1)S(1)}, bf16[32,3584]{1,0:T(8,128)(2,1)}, u32[]{:S(2)}) copy-start(bf16[32,3584]{1,0:T(8,128)(2,1)} %param.15) | copy-start | bytes 688132
  3.3 20.9 %collective-permute-start.13 = (bf16[32,3712]{1,0:T(8,128)(2,1)S(1)}, bf16[32,3712]{1,0:T(8,128)(2,1)S(1)}, u32[]{:S(2)}, u32[]{:S(2)}) collective-permute-start(bf16[32,3712]{1,0:T(8,128)(2,1)S(1)} %constant_dynamic-slice_fusion), channel_id=1, source_target_pairs={{0,8},{1,9},{2,10},{3,11},{4,12},{5,13},{6,14},{7,15},{8,0},{9,1},... | collective-permute-start | bytes 712712 | tf_op jit(solution)/shard_map/ppermute | solution.py:36
  7.4 16.8 %collective-permute-start.17 = (bf16[32,3712]{1,0:T(8,128)(2,1)S(1)}, bf16[32,3712]{1,0:T(8,128)(2,1)S(1)}, u32[]{:S(2)}, u32[]{:S(2)}) collective-permute-start(bf16[32,3712]{1,0:T(8,128)(2,1)S(1)} %constant_dynamic-slice_fusion), channel_id=1, source_target_pairs={{0,12},{1,13},{2,14},{3,15},{4,8},{5,9},{6,10},{7,11},{8,4},{9,5},... | collective-permute-start | bytes 712712 | tf_op jit(solution)/shard_map/ppermute | solution.py:36
  8.8 17.4 %collective-permute-start.1 = (bf16[32,3712]{1,0:T(8,128)(2,1)S(1)}, bf16[32,3712]{1,0:T(8,128)(2,1)S(1)}, u32[]{:S(2)}, u32[]{:S(2)}) collective-permute-start(bf16[32,3712]{1,0:T(8,128)(2,1)S(1)} %constant_dynamic-slice_fusion), channel_id=1, source_target_pairs={{0,4},{1,5},{2,6},{3,7},{4,0},{5,1},{6,2},{7,3},{8,12},{9,13},{10,... | collective-permute-start | bytes 712712 | tf_op jit(solution)/shard_map/ppermute | solution.py:36
  9.6 26.2 %copy-start.20 = (s32[8]{0:T(128)S(1)}, s32[8]{0:T(128)}, u32[]{:S(2)}) copy-start(s32[8]{0:T(128)} %param.11) | copy-start | bytes 100
  24.2 19.6 %copy-start.8 = (bf16[32,3712]{1,0:T(8,128)(2,1)}, bf16[32,3712]{1,0:T(8,128)(2,1)S(1)}, u32[]{:S(2)}) copy-start(bf16[32,3712]{1,0:T(8,128)(2,1)S(1)} %collective-permute-done.13.refs_1_) | copy-start | bytes 712708
  24.2 19.0 %collective-permute-start.5 = (bf16[96,3584]{1,0:T(8,128)(2,1)S(1)}, bf16[96,3584]{1,0:T(8,128)(2,1)S(1)}, u32[]{:S(2)}, u32[]{:S(2)}) collective-permute-start(bf16[96,3584]{1,0:T(8,128)(2,1)S(1)} %pad_maximum_fusion), channel_id=1, source_target_pairs={{0,1},{1,0},{2,3},{3,2},{4,5},{5,4},{6,7},{7,6},{8,9},{9,8},{10,11... | collective-permute-start | bytes 2064392 | tf_op jit(solution)/shard_map/ppermute | solution.py:36
  24.2 19.6 %copy-start.9 = (bf16[32,3712]{1,0:T(8,128)(2,1)}, bf16[32,3712]{1,0:T(8,128)(2,1)S(1)}, u32[]{:S(2)}) copy-start(bf16[32,3712]{1,0:T(8,128)(2,1)S(1)} %collective-permute-done.17.refs_5_) | copy-start | bytes 712708
  24.2 8.3 %collective-permute-start.14 = (bf16[32,3712]{1,0:T(8,128)(2,1)S(1)}, bf16[32,3712]{1,0:T(8,128)(2,1)S(1)}, u32[]{:S(2)}, u32[]{:S(2)}) collective-permute-start(bf16[32,3712]{1,0:T(8,128)(2,1)S(1)} %collective-permute-done.13.refs_1_), channel_id=1, source_target_pairs={{0,16},{16,0},{1,17},{17,1},{2,18},{18,2},{3,19},{19,3},{4,20},{20... | collective-permute-start | bytes 712712 | tf_op jit(solution)/shard_map/ppermute | solution.py:40
  26.2 24.2 %copy-start.7 = (bf16[32,3712]{1,0:T(8,128)(2,1)}, bf16[32,3712]{1,0:T(8,128)(2,1)S(1)}, u32[]{:S(2)}) copy-start(bf16[32,3712]{1,0:T(8,128)(2,1)S(1)} %collective-permute-done.1.refs_3_) | copy-start | bytes 712708
  26.2 8.1 %collective-permute-start.15 = (bf16[32,3712]{1,0:T(8,128)(2,1)S(1)}, bf16[32,3712]{1,0:T(8,128)(2,1)S(1)}, u32[]{:S(2)}, u32[]{:S(2)}) collective-permute-start(bf16[32,3712]{1,0:T(8,128)(2,1)S(1)} %collective-permute-done.13.refs_1_), channel_id=1, source_target_pairs={{0,2},{1,3},{2,0},{3,1},{4,6},{5,7},{6,4},{7,5},{8,10},{9,11},{10,... | collective-permute-start | bytes 712712 | tf_op jit(solution)/shard_map/ppermute | solution.py:36
  32.5 11.3 %copy-start.10 = (bf16[32,3712]{1,0:T(8,128)(2,1)}, bf16[32,3712]{1,0:T(8,128)(2,1)S(1)}, u32[]{:S(2)}) copy-start(bf16[32,3712]{1,0:T(8,128)(2,1)S(1)} %collective-permute-done.14.refs_2_) | copy-start | bytes 712708
  32.5 7.5 %collective-permute-start.18 = (bf16[32,3712]{1,0:T(8,128)(2,1)S(1)}, bf16[32,3712]{1,0:T(8,128)(2,1)S(1)}, u32[]{:S(2)}, u32[]{:S(2)}) collective-permute-start(bf16[32,3712]{1,0:T(8,128)(2,1)S(1)} %collective-permute-done.17.refs_5_), channel_id=1, source_target_pairs={{0,16},{16,0},{1,17},{17,1},{2,18},{18,2},{3,19},{19,3},{4,20},{20... | collective-permute-start | bytes 712712 | tf_op jit(solution)/shard_map/ppermute | solution.py:40
  34.3 9.6 %copy-start.11 = (bf16[32,3712]{1,0:T(8,128)(2,1)}, bf16[32,3712]{1,0:T(8,128)(2,1)S(1)}, u32[]{:S(2)}) copy-start(bf16[32,3712]{1,0:T(8,128)(2,1)S(1)} %collective-permute-done.15.refs_3_) | copy-start | bytes 712708
  34.3 7.4 %collective-permute-start.19 = (bf16[32,3712]{1,0:T(8,128)(2,1)S(1)}, bf16[32,3712]{1,0:T(8,128)(2,1)S(1)}, u32[]{:S(2)}, u32[]{:S(2)}) collective-permute-start(bf16[32,3712]{1,0:T(8,128)(2,1)S(1)} %collective-permute-done.17.refs_5_), channel_id=1, source_target_pairs={{0,2},{1,3},{2,0},{3,1},{4,6},{5,7},{6,4},{7,5},{8,10},{9,11},{10,... | collective-permute-start | bytes 712712 | tf_op jit(solution)/shard_map/ppermute | solution.py:36
  40.0 3.9 %copy-start.13 = (bf16[32,3712]{1,0:T(8,128)(2,1)}, bf16[32,3712]{1,0:T(8,128)(2,1)S(1)}, u32[]{:S(2)}) copy-start(bf16[32,3712]{1,0:T(8,128)(2,1)S(1)} %collective-permute-done.18.refs_6_) | copy-start | bytes 712708
  40.0 6.6 %collective-permute-start.3 = (bf16[32,3712]{1,0:T(8,128)(2,1)S(1)}, bf16[32,3712]{1,0:T(8,128)(2,1)S(1)}, u32[]{:S(2)}, u32[]{:S(2)}) collective-permute-start(bf16[32,3712]{1,0:T(8,128)(2,1)S(1)} %collective-permute-done.1.refs_3_), channel_id=1, source_target_pairs={{0,2},{1,3},{2,0},{3,1},{4,6},{5,7},{6,4},{7,5},{8,10},{9,11},{10,... | collective-permute-start | bytes 712712 | tf_op jit(solution)/shard_map/ppermute | solution.py:36
  41.7 2.2 %copy-start.14 = (bf16[32,3712]{1,0:T(8,128)(2,1)}, bf16[32,3712]{1,0:T(8,128)(2,1)S(1)}, u32[]{:S(2)}) copy-start(bf16[32,3712]{1,0:T(8,128)(2,1)S(1)} %collective-permute-done.19.refs_7_) | copy-start | bytes 712708
  41.7 8.7 %collective-permute-start.16 = (bf16[32,3712]{1,0:T(8,128)(2,1)S(1)}, bf16[32,3712]{1,0:T(8,128)(2,1)S(1)}, u32[]{:S(2)}, u32[]{:S(2)}) collective-permute-start(bf16[32,3712]{1,0:T(8,128)(2,1)S(1)} %collective-permute-done.15.refs_3_), channel_id=1, source_target_pairs={{0,16},{16,0},{1,17},{17,1},{2,18},{18,2},{3,19},{19,3},{4,20},{20... | collective-permute-start | bytes 712712 | tf_op jit(solution)/shard_map/ppermute | solution.py:40
  43.2 12.3 %collective-permute-start.20 = (bf16[32,3712]{1,0:T(8,128)(2,1)S(1)}, bf16[32,3712]{1,0:T(8,128)(2,1)S(1)}, u32[]{:S(2)}, u32[]{:S(2)}) collective-permute-start(bf16[32,3712]{1,0:T(8,128)(2,1)S(1)} %collective-permute-done.19.refs_7_), channel_id=1, source_target_pairs={{0,16},{16,0},{1,17},{17,1},{2,18},{18,2},{3,19},{19,3},{4,20},{20... | collective-permute-start | bytes 712712 | tf_op jit(solution)/shard_map/ppermute | solution.py:40
  46.6 43.7 %copy-start.12 = (bf16[32,3712]{1,0:T(8,128)(2,1)}, bf16[32,3712]{1,0:T(8,128)(2,1)S(1)}, u32[]{:S(2)}) copy-start(bf16[32,3712]{1,0:T(8,128)(2,1)S(1)} %collective-permute-done.3.refs_5_) | copy-start | bytes 712708
  46.6 45.5 %collective-permute-start = (bf16[64,3712]{1,0:T(8,128)(2,1)S(1)}, bf16[64,3712]{1,0:T(8,128)(2,1)S(1)}, u32[]{:S(2)}, u32[]{:S(2)}) collective-permute-start(bf16[64,3712]{1,0:T(8,128)(2,1)S(1)} %concatenate.24.refs_1_), channel_id=1, source_target_pairs={{0,2},{1,3},{2,0},{3,1},{4,6},{5,7},{6,4},{7,5},{8,10},{9,11},{10,... | collective-permute-start | bytes 1425416 | tf_op jit(solution)/shard_map/ppermute | solution.py:36
  50.4 5.1 %copy-start.16 = (bf16[32,3712]{1,0:T(8,128)(2,1)}, bf16[32,3712]{1,0:T(8,128)(2,1)S(1)}, u32[]{:S(2)}) copy-start(bf16[32,3712]{1,0:T(8,128)(2,1)S(1)} %collective-permute-done.16.refs_4_) | copy-start | bytes 712708
  50.4 41.7 %collective-permute-start.2 = (bf16[32,3712]{1,0:T(8,128)(2,1)S(1)}, bf16[32,3712]{1,0:T(8,128)(2,1)S(1)}, u32[]{:S(2)}, u32[]{:S(2)}) collective-permute-start(bf16[32,3712]{1,0:T(8,128)(2,1)S(1)} %collective-permute-done.1.refs_3_), channel_id=1, source_target_pairs={{0,16},{16,0},{1,17},{17,1},{2,18},{18,2},{3,19},{19,3},{4,20},{20... | collective-permute-start | bytes 712712 | tf_op jit(solution)/shard_map/ppermute | solution.py:40
  55.5 1.5 copy-start.18
  55.5 36.6 %collective-permute-start.4 = (bf16[32,3712]{1,0:T(8,128)(2,1)S(1)}, bf16[32,3712]{1,0:T(8,128)(2,1)S(1)}, u32[]{:S(2)}, u32[]{:S(2)}) collective-permute-start(bf16[32,3712]{1,0:T(8,128)(2,1)S(1)} %collective-permute-done.3.refs_5_), channel_id=1, source_target_pairs={{0,16},{16,0},{1,17},{17,1},{2,18},{18,2},{3,19},{19,3},{4,20},{20... | collective-permute-start | bytes 712712 | tf_op jit(solution)/shard_map/ppermute | solution.py:40
  90.2 38.9 %collective-permute-start.24 = (bf16[128,1792]{1,0:T(8,128)(2,1)}, bf16[128,1792]{1,0:T(8,128)(2,1)S(1)}, u32[]{:S(2)}, u32[]{:S(2)}) collective-permute-start(bf16[128,1792]{1,0:T(8,128)(2,1)} %get-tuple-element.20), channel_id=1, source_target_pairs={{0,16},{16,0},{1,17},{17,1},{2,18},{18,2},{3,19},{19,3},{4,20},{20... | collective-permute-start | bytes 1376264 | tf_op jit(solution)/shard_map/ppermute | solution.py:40
  91.0 38.1 %copy-start.5 = (bf16[128,1792]{1,0:T(8,128)(2,1)S(1)}, bf16[128,1792]{1,0:T(8,128)(2,1)}, u32[]{:S(2)}) copy-start(bf16[128,1792]{1,0:T(8,128)(2,1)} %get-tuple-element.19) | copy-start | bytes 1376260
  91.0 38.8 %collective-permute-start.21 = (bf16[2,64,1792]{2,1,0:T(8,128)(2,1)}, bf16[2,64,1792]{2,1,0:T(8,128)(2,1)S(1)}, u32[]{:S(2)}, u32[]{:S(2)}) collective-permute-start(bf16[2,64,1792]{2,1,0:T(8,128)(2,1)} %get-tuple-element.18), channel_id=1, source_target_pairs={{0,2},{1,3},{2,0},{3,1},{4,6},{5,7},{6,4},{7,5},{8,10},{9,11},{10,... | collective-permute-start | bytes 1376264 | tf_op jit(solution)/shard_map/ppermute | solution.py:36
  92.1 0.8 copy-start.2
  92.1 0.9 copy-start.15
  93.0 0.7 copy-start.17
  126.8 3.1 %copy-start.3 = (bf16[2,64,1792]{2,1,0:T(8,128)(2,1)S(1)}, bf16[2,64,1792]{2,1,0:T(8,128)(2,1)}, u32[]{:S(2)}) copy-start(bf16[2,64,1792]{2,1,0:T(8,128)(2,1)} %get-tuple-element.17) | copy-start | bytes 1376260
  126.8 11.7 %collective-permute-start.10 = (bf16[128,1792]{1,0:T(8,128)(2,1)}, bf16[128,1792]{1,0:T(8,128)(2,1)S(1)}, u32[]{:S(2)}, u32[]{:S(2)}) collective-permute-start(bf16[128,1792]{1,0:T(8,128)(2,1)} %get-tuple-element.16), channel_id=1, source_target_pairs={{0,16},{16,0},{1,17},{17,1},{2,18},{18,2},{3,19},{19,3},{4,20},{20... | collective-permute-start | bytes 1376264 | tf_op jit(solution)/shard_map/ppermute | solution.py:40
  127.6 12.4 %collective-permute-start.8 = (bf16[2,64,1792]{2,1,0:T(8,128)(2,1)}, bf16[2,64,1792]{2,1,0:T(8,128)(2,1)S(1)}, u32[]{:S(2)}, u32[]{:S(2)}) collective-permute-start(bf16[2,64,1792]{2,1,0:T(8,128)(2,1)} %get-tuple-element.14), channel_id=1, source_target_pairs={{0,2},{1,3},{2,0},{3,1},{4,6},{5,7},{6,4},{7,5},{8,10},{9,11},{10,... | collective-permute-start | bytes 1376264 | tf_op jit(solution)/shard_map/ppermute | solution.py:36
  129.2 9.3 %copy-start.6 = (bf16[128,1792]{1,0:T(8,128)(2,1)S(1)}, bf16[128,1792]{1,0:T(8,128)(2,1)}, u32[]{:S(2)}) copy-start(bf16[128,1792]{1,0:T(8,128)(2,1)} %get-tuple-element.15) | copy-start | bytes 1376260
  129.3 12.4 %collective-permute-start.25 = (bf16[64,1792]{1,0:T(8,128)(2,1)S(1)}, bf16[64,1792]{1,0:T(8,128)(2,1)S(1)}, u32[]{:S(2)}, u32[]{:S(2)}) collective-permute-start(bf16[64,1792]{1,0:T(8,128)(2,1)S(1)} %slice.63), channel_id=1, source_target_pairs={{0,2},{1,3},{2,0},{3,1},{4,6},{5,7},{6,4},{7,5},{8,10},{9,11},{10,... | collective-permute-start | bytes 688136 | tf_op jit(solution)/shard_map/ppermute | solution.py:36
  130.0 10.0 %copy-start.4 = (bf16[2,64,1792]{2,1,0:T(8,128)(2,1)S(1)}, bf16[2,64,1792]{2,1,0:T(8,128)(2,1)}, u32[]{:S(2)}) copy-start(bf16[2,64,1792]{2,1,0:T(8,128)(2,1)} %get-tuple-element.13) | copy-start | bytes 1376260
  130.0 14.4 %collective-permute-start.22 = (bf16[64,1792]{1,0:T(8,128)(2,1)S(1)}, bf16[64,1792]{1,0:T(8,128)(2,1)S(1)}, u32[]{:S(2)}, u32[]{:S(2)}) collective-permute-start(bf16[64,1792]{1,0:T(8,128)(2,1)S(1)} %slice_bitcast_fusion), channel_id=1, source_target_pairs={{0,16},{16,0},{1,17},{17,1},{2,18},{18,2},{3,19},{19,3},{4,20},{20... | collective-permute-start | bytes 688136 | tf_op jit(solution)/shard_map/ppermute | solution.py:40
  138.6 8.1 %collective-permute-start.11 = (bf16[64,1792]{1,0:T(8,128)(2,1)S(1)}, bf16[64,1792]{1,0:T(8,128)(2,1)S(1)}, u32[]{:S(2)}, u32[]{:S(2)}) collective-permute-start(bf16[64,1792]{1,0:T(8,128)(2,1)S(1)} %slice.59), channel_id=1, source_target_pairs={{0,2},{1,3},{2,0},{3,1},{4,6},{5,7},{6,4},{7,5},{8,10},{9,11},{10,... | collective-permute-start | bytes 688136 | tf_op jit(solution)/shard_map/ppermute | solution.py:36
  140.1 8.4 %collective-permute-start.9 = (bf16[64,1792]{1,0:T(8,128)(2,1)S(1)}, bf16[64,1792]{1,0:T(8,128)(2,1)S(1)}, u32[]{:S(2)}, u32[]{:S(2)}) collective-permute-start(bf16[64,1792]{1,0:T(8,128)(2,1)S(1)} %slice_bitcast_fusion.2), channel_id=1, source_target_pairs={{0,16},{16,0},{1,17},{17,1},{2,18},{18,2},{3,19},{19,3},{4,20},{20... | collective-permute-start | bytes 688136 | tf_op jit(solution)/shard_map/ppermute | solution.py:40
  141.7 8.0 %collective-permute-start.26 = (bf16[64,1792]{1,0:T(8,128)(2,1)S(1)}, bf16[64,1792]{1,0:T(8,128)(2,1)S(1)}, u32[]{:S(2)}, u32[]{:S(2)}) collective-permute-start(bf16[64,1792]{1,0:T(8,128)(2,1)S(1)} %add_convert_fusion.4), channel_id=1, source_target_pairs={{0,12},{1,13},{2,14},{3,15},{4,8},{5,9},{6,10},{7,11},{8,4},{9,5},... | collective-permute-start | bytes 688136 | tf_op jit(solution)/shard_map/ppermute | solution.py:36
  144.5 12.4 %collective-permute-start.23 = (bf16[64,1792]{1,0:T(8,128)(2,1)S(1)}, bf16[64,1792]{1,0:T(8,128)(2,1)S(1)}, u32[]{:S(2)}, u32[]{:S(2)}) collective-permute-start(bf16[64,1792]{1,0:T(8,128)(2,1)S(1)} %fusion), channel_id=1, source_target_pairs={{0,8},{1,9},{2,10},{3,11},{4,12},{5,13},{6,14},{7,15},{8,0},{9,1},... | collective-permute-start | bytes 688136 | tf_op jit(solution)/shard_map/ppermute | solution.py:36
  146.8 10.1 %collective-permute-start.12 = (bf16[64,1792]{1,0:T(8,128)(2,1)S(1)}, bf16[64,1792]{1,0:T(8,128)(2,1)S(1)}, u32[]{:S(2)}, u32[]{:S(2)}) collective-permute-start(bf16[64,1792]{1,0:T(8,128)(2,1)S(1)} %add_convert_fusion.5), channel_id=1, source_target_pairs={{0,4},{1,5},{2,6},{3,7},{4,0},{5,1},{6,2},{7,3},{8,12},{9,13},{10,... | collective-permute-start | bytes 688136 | tf_op jit(solution)/shard_map/ppermute | solution.py:36

commit v4 on v3

v4 whole, which is shorter than its diff:
```python
import functools

import jax
import jax.numpy as jnp
from jax import lax
from jax.experimental import pallas as pl
from jax.experimental.pallas import tpu as pltpu
from jax.sharding import PartitionSpec as P

routed_scale = 2.5
lanes = 128
in_flight = 6
cut = 2048
f32 = jnp.float32
bf16 = jnp.bfloat16


def remapped(routes, swap_codes, per_device, half_width):
    owner = routes // per_device
    slot = routes % per_device
    pair_ids = jnp.arange(half_width, dtype=jnp.int32)
    code = jnp.sum(
        jnp.where((owner % half_width)[..., None] == pair_ids, swap_codes, 0), axis=-1
    )
    lower = owner < half_width
    low_slot = (code - 1) // per_device
    high_slot = (code - 1) % per_device
    traded = (code > 0) & (slot == jnp.where(lower, low_slot, high_slot))
    partner = jnp.where(
        lower,
        (owner + half_width) * per_device + high_slot,
        (owner - half_width) * per_device + low_slot,
    )
    return jnp.where(traded, partner, routes)


def hop(x, by, by_x=0):
    ne = lax.axis_size("expert")
    count = ne * lax.axis_size("dp")
    return lax.ppermute(x, ("dp", "expert"), [(i, i ^ (by_x * ne + by)) for i in range(count)])


def ffn_kernel(
    levels, x_first, nx, ny, tok_rows, top_count, model_dim, hid_tile, n_units, n_after, *refs
):
    slots = refs[0]
    units = refs[1 : 1 + n_units]
    sh_gu, sh_dn, gu_own, gu_sib, dn_own, dn_sib = refs[1 + n_units : 7 + n_units]
    refs = refs[7 + n_units + n_after :]
    outs = [refs[i * nx : (i + 1) * nx] for i in range(len(levels))]
    rows_in, shared_w, wgu, wdn, act, scale, sem_x, sem_s, sem_gu, sem_dn = refs[len(levels) * nx :]
    mx = lax.axis_index("dp")
    part = tok_rows // nx
    width = model_dim // nx
    per_device, _, _, hidden = gu_own.shape
    tiles = hidden // hid_tile
    n_slots = 2 * per_device
    experts_k = n_slots * hidden
    sp = sh_dn.shape[0]

    copies = []

    def take(unit, start, size, row):
        dst = rows_in.at[pl.ds(row, size)]
        copies.append(
            pltpu.make_async_copy(unit.at[pl.ds(start, size)], dst, sem_x.at[len(copies)])
        )

    at = 0
    for j in range(ny):
        if levels[0] == 0:
            take(units[at], 0, tok_rows, j * tok_rows)
            at += 1
        for h in range(nx):
            for n, i in enumerate(i for i in range(len(levels)) if levels[i]):
                row = (i * ny + j) * tok_rows + (mx ^ h) * part
                take(units[at], n * part, part, pl.multiple_of(row, part))
            at += 1
    shared_copy = pltpu.make_async_copy(sh_gu, shared_w, sem_s.at[0])

    def gu_copy(src, e, t, i, g):
        return pltpu.make_async_copy(
            src.at[e, g, :, pl.ds(t * hid_tile, hid_tile)], wgu.at[i, g], sem_gu.at[i, g]
        )

    cuts = [(at, min(cut, width - at)) for at in range(0, width, cut)]

    def dn_copy(src, e, h, s, n):
        at, size = cuts[n]
        column = pl.multiple_of((mx ^ h) * width + at, lanes)
        return pltpu.make_async_copy(
            src.at[e, :, pl.ds(column, size)],
            wdn.at[h, pl.ds(s * hidden, hidden), pl.ds(at, size)],
            sem_dn.at[h, n, s],
        )

    def sh_copy(h, n):
        at, size = cuts[n]
        column = pl.multiple_of((mx ^ h) * width + at, lanes)
        return pltpu.make_async_copy(
            sh_dn.at[:, pl.ds(column, size)],
            wdn.at[h, pl.ds(experts_k, sp), pl.ds(at, size)],
            sem_dn.at[h, n, n_slots],
        )

    order = list(range(1, nx)) + [0]
    gu_copies = []
    for s in range(n_slots):
        src = gu_own if s < per_device else gu_sib
        for t in range(tiles):
            for g in range(2):
                gu_copies.append(gu_copy(src, s % per_device, t, s * tiles + t, g))
    dn_copies = []
    for h in order:
        for n in range(len(cuts)):
            group = [sh_copy(h, n)]
            for s in range(n_slots):
                src = dn_own if s < per_device else dn_sib
                group.append(dn_copy(src, s % per_device, h, s, n))
            dn_copies.append((h, n, group))

    queue = gu_copies[:4] + [shared_copy] + gu_copies[4:]
    queue += [copy for _, _, group in dn_copies for copy in group]
    started = [0]

    def start_next(count):
        for copy in queue[started[0] : started[0] + count]:
            copy.start()
        started[0] += count

    def arrived(copy):
        copy.wait()
        start_next(1)

    for copy in copies:
        copy.start()
    start_next(in_flight)
    for copy in copies:
        copy.wait()
    extra = rows_in[:, model_dim:].astype(f32)
    named = extra[:, :top_count]
    quant = extra[:, top_count : 2 * top_count] * 256.0 + extra[:, 2 * top_count : 3 * top_count]
    gates = routed_scale * quant / jnp.sum(quant, axis=1, keepdims=True)
    n_rows = rows_in.shape[0]
    for s in range(n_slots):
        mine = jnp.where(named == slots[s].astype(f32), gates, 0.0)
        column = jnp.sum(mine, axis=1, keepdims=True)
        scale[s] = jnp.broadcast_to(column, (n_rows, lanes))

    def silu(v):
        return v / (1.0 + jnp.exp(-v))

    for i in range(n_slots * tiles):
        if i == 2:
            arrived(shared_copy)
            both = jnp.dot(rows_in[:, :model_dim], shared_w[...], preferred_element_type=f32)
            shared_act = (silu(both[:, :sp]) * both[:, sp:]).astype(bf16)
            act[:, experts_k : experts_k + sp] = shared_act
        for copy in gu_copies[2 * i : 2 * i + 2]:
            arrived(copy)
        g = jnp.dot(rows_in[:, :model_dim], wgu[i, 0], preferred_element_type=f32)
        u = jnp.dot(rows_in[:, :model_dim], wgu[i, 1], preferred_element_type=f32)
        by = jnp.concatenate([scale[i // tiles]] * (hid_tile // lanes), axis=1)
        act[:, i * hid_tile : (i + 1) * hid_tile] = (silu(g) * u * by).astype(bf16)

    level_rows = ny * tok_rows
    for h, n, group in dn_copies:
        for copy in group:
            arrived(copy)
        columns = pl.ds(*cuts[n])
        value = jnp.dot(act[...], wdn[h, :, columns], preferred_element_type=f32).astype(bf16)
        for i in range(len(levels)):
            if x_first[i]:
                outs[i][h][:, columns] = value[i * level_rows : (i + 1) * level_rows]
            else:
                for j in range(ny):
                    base = i * level_rows + j * tok_rows
                    outs[i][j][h, :, columns] = value[base : base + tok_rows]


def local(
    tokens, routes, gate_quant, swap_codes, expert_gate_up, expert_down, shared_gate_up, shared_down
):
    axis_width = lax.axis_size("expert")
    nx = lax.axis_size("dp")
    ny = nx
    nz = axis_width // (2 * ny)
    zs = 2 * ny
    per_device, hidden, model_dim = expert_down.shape
    tok_rows = tokens.shape[0]
    top_count = routes.shape[1]
    me = lax.axis_index("expert")
    mx = lax.axis_index("dp")
    part = tok_rows // nx
    width = model_dim // nx
    hid_tile = 256 if hidden % 256 == 0 else 128

    pad = -3 * top_count % lanes
    wide = jnp.concatenate(
        [
            tokens,
            routes.astype(bf16),
            (gate_quant // 256).astype(bf16),
            (gate_quant % 256).astype(bf16),
            jnp.zeros((tok_rows, pad), bf16),
        ],
        axis=1,
    )
    wide_dim = wide.shape[1]

    gu_sib = hop(expert_gate_up, 1)
    dn_sib = hop(expert_down, 1)
    shared_rows = shared_down.shape[0]
    shared_own = jnp.concatenate(
        [shared_gate_up[:, 0, :], shared_gate_up[:, 1, :], shared_down], axis=0
    )
    shared_both = jnp.stack([shared_own, hop(shared_own, 1)])
    shared_both = shared_both.reshape(2, 3, shared_rows, model_dim).transpose(1, 0, 2, 3)
    shared_both = shared_both.reshape(3, 2 * shared_rows, model_dim)
    shared_both = jnp.pad(shared_both, ((0, 0), (0, -2 * shared_rows % 16), (0, 0)))
    sp = shared_both.shape[1]
    sh_gu = shared_both[:2].reshape(2 * sp, model_dim).T
    sh_dn = shared_both[2]

    my_experts = jnp.concatenate(
        [owner * per_device + jnp.arange(per_device, dtype=jnp.int32) for owner in (me, me ^ 1)]
    )
    slots = remapped(my_experts, swap_codes, per_device, axis_width // 2)

    half = nz // 2
    held = lax.dynamic_slice_in_dim(wide, mx * part, part, axis=0)
    own = [wide] + [hop(wide, 2 * j) for j in range(1, ny)]
    bits = [0]
    step = half
    while step > 1:
        held = jnp.concatenate([held, hop(held, step * zs)], axis=0)
        bits = bits + [bit ^ step for bit in bits]
        step //= 2
    far = hop(held, zs)
    bits = bits + [bit ^ 1 for bit in bits]

    def spread(x):
        return [[hop(x, 2 * j, h) if j or h else x for h in range(nx)] for j in range(ny)]

    near_units = spread(held[part:])
    near = [u for j in range(ny) for u in near_units[j]]
    far = lax.optimization_barrier([far] + near)[0]
    far_units = spread(far)
    chunks = [
        [u for j in range(ny) for u in [own[j]] + near_units[j]],
        [u for j in range(ny) for u in far_units[j]],
    ]

    def added(own, others):
        total = own.astype(f32)
        for other in others:
            total = total + other.astype(f32)
        return total

    done = {}
    n_slots = 2 * per_device
    tiles = hidden // hid_tile
    after = []
    for levels in (list(range(half)), list(range(half, nz))):
        x_first = [k % 2 == 1 for k in levels]
        chunk = chunks[levels[0] // half]
        n_rows = len(levels) * ny * tok_rows
        out_shape = []
        for first in x_first:
            shape = (ny * tok_rows, width) if first else (nx, tok_rows, width)
            out_shape += [jax.ShapeDtypeStruct(shape, bf16)] * nx
        k_total = n_slots * hidden + sp
        flops = 2 * n_rows * model_dim * (3 * n_slots * hidden + 3 * sp)
        outs = pl.pallas_call(
            functools.partial(
                ffn_kernel,
                levels,
                x_first,
                nx,
                ny,
                tok_rows,
                top_count,
                model_dim,
                hid_tile,
                len(chunk),
                len(after),
            ),
            out_shape=out_shape,
            in_specs=[pl.BlockSpec(memory_space=pltpu.SMEM)]
            + [pl.BlockSpec(memory_space=pl.ANY)] * (len(chunk) + 6 + len(after)),
            out_specs=[pl.BlockSpec(memory_space=pltpu.VMEM)] * len(out_shape),
            scratch_shapes=[
                pltpu.VMEM((n_rows, wide_dim), bf16),
                pltpu.VMEM((model_dim, 2 * sp), bf16),
                pltpu.VMEM((n_slots * tiles, 2, model_dim, hid_tile), bf16),
                pltpu.VMEM((nx, k_total, width), bf16),
                pltpu.VMEM((n_rows, k_total), bf16),
                pltpu.VMEM((n_slots, n_rows, lanes), f32),
                pltpu.SemaphoreType.DMA((len(levels) * ny * nx,)),
                pltpu.SemaphoreType.DMA((1,)),
                pltpu.SemaphoreType.DMA((n_slots * tiles, 2)),
                pltpu.SemaphoreType.DMA((nx, -(-width // cut), n_slots + 1)),
            ],
            compiler_params=pltpu.CompilerParams(vmem_limit_bytes=60 * 1024 * 1024),
            cost_estimate=pl.CostEstimate(
                flops=flops,
                bytes_accessed=3 * 2 * n_slots * hidden * model_dim + 6 * n_rows * model_dim,
                transcendentals=0,
            ),
        )(slots, *chunk, sh_gu, sh_dn, expert_gate_up, gu_sib, expert_down, dn_sib, *after)
        after = outs[:1]
        for i, k in enumerate(levels):
            sent = outs[i * nx : (i + 1) * nx]
            if x_first[i]:
                got = [hop(sent[h], 0, h) for h in range(1, nx)]
                row = added(sent[0], got).astype(bf16).reshape(ny, tok_rows, width)
                got = [hop(row[j], 2 * j) for j in range(1, ny)]
            else:
                got = [hop(sent[j], 2 * j) for j in range(1, ny)]
                row = added(sent[0], got).astype(bf16)
                got = [hop(row[h], 0, h) for h in range(1, nx)]
            plane = added(row[0], got)
            done[k] = plane if k == 0 else hop(plane.astype(bf16), bits[k] * zs)
    return added(done[0], [done[k] for k in range(1, nz)]).astype(bf16)


def solution(mesh):
    in_specs = (
        P("expert", None),
        P("expert", None),
        P("expert", None),
        P(),
        P("expert", None, None, "dp"),
        P("expert", "dp", None),
        P(("dp", "expert"), None, None),
        P(("dp", "expert"), None),
    )
    out_specs = P("expert", "dp")
    return jax.shard_map(local, mesh=mesh, in_specs=in_specs, out_specs=out_specs, check_vma=False)
```

time: 158 us -> 126 us (0.80)
  Pallas kernels: 66.3 us -> 44 us
  waiting for transfers between devices: 45.3 us -> 39.4 us
  starting transfers between devices: 36.4 us -> 32.5 us
    pallas_call x2, Pallas kernels: 66.3 us -> 44 us  [local(): pl.pallas_call(functools.partial(ffn_kernel, levels, x_first, nx, ny, tok...]
    ppermute x27 -> x23, waiting for transfers between devices: 45.3 us -> 39.4 us  [hop(): lax.ppermute(x, ('dp', 'expert'), [(i, i ^ by_x * ne + by) for i in range...]
    ppermute x27 -> x23, starting transfers between devices: 36.4 us -> 32.5 us  [hop(): lax.ppermute(x, ('dp', 'expert'), [(i, i ^ by_x * ne + by) for i in range...]
  transfers between devices with their start and end apart: 27 -> 23, of which waited for: 10 -> 10; matrix products, arithmetic and copies ran while one was open for 4% -> 6% of each run, Pallas kernels for 42% -> 35%
where the time goes in v4:
time: 126 us
  Pallas kernels  44 us (35%)
  waiting for transfers between devices  39.4 us (31%)
  starting transfers between devices  32.5 us (26%)
  local copies, waits for them, and re-layouts  6.46 us (5%)
  other arithmetic  3.25 us (3%)
    pallas_call x2, Pallas kernels, local(): pl.pallas_call(functools.partial(ffn_kernel, levels, x_first, nx, ny, tok...  44 us
    ppermute x23, waiting for transfers between devices, hop(): lax.ppermute(x, ('dp', 'expert'), [(i, i ^ by_x * ne + by) for i in range...  39.4 us
    ppermute x23, starting transfers between devices, hop(): lax.ppermute(x, ('dp', 'expert'), [(i, i ^ by_x * ne + by) for i in range...  32.5 us
  transfers between devices with their start and end apart: 23, of which 10 were waited for; matrix products, arithmetic and copies ran while one was open for 6% of the time, Pallas kernels for 35%

profile of v4, /device:TPU:0, one launch (start us, length us, event | category | flops | bytes accessed | tf_op | source)
XLA Modules:
  0.0 125.8 jit_solution(4178818572750725561)
XLA Ops:
  0.0 0.5 collective-permute-start.6
  0.5 0.1 collective-permute-start.7
  0.5 0.8 copy.27
  1.3 0.7 convert_element_type.96
  2.0 0.1 copy.31
  2.1 1.1 concatenate.27.refs_1_
  3.3 0.0 copy-start.14
  3.3 4.1 %collective-permute-start = (bf16[32,3712]{1,0:T(8,128)(2,1)S(1)}, bf16[32,3712]{1,0:T(8,128)(2,1)S(1)}, u32[]{:S(2)}, u32[]{:S(2)}) collective-permute-start(bf16[32,3712]{1,0:T(8,128)(2,1)S(1)} %constant_dynamic-slice_fusion), channel_id=1, source_target_pairs={{0,8},{1,9},{2,10},{3,11},{4,12},{5,13},{6,14},{7,15},{8,0},{9,1},... | collective-permute-start | bytes 712712 | tf_op jit(solution)/shard_map/ppermute | solution.py:40
  7.4 0.6 fusion.10
  8.1 0.0 copy-start.15
  8.1 0.1 copy_bitcast_fusion
  8.1 0.1 pad_maximum_fusion
  8.2 0.1 collective-permute-start.5
  8.3 0.1 and_select_fusion.4
  8.4 0.3 copy-done.15
  8.7 0.2 select_reduce_fusion
  8.9 0.6 and_select_fusion.refs_0_
  9.5 9.0 %collective-permute-done.refs_2_ = bf16[32,3712]{1,0:T(8,128)(2,1)S(1)} collective-permute-done((bf16[32,3712]{1,0:T(8,128)(2,1)S(1)}, bf16[32,3712]{1,0:T(8,128)(2,1)S(1)}, u32[]{:S(2)}, u32[]{:S(2)}) %collective-permute-start) | collective-permute-done | bytes 237600 | tf_op jit(solution)/shard_map/ppermute | solution.py:40
  18.5 1.5 %collective-permute-start.1 = (bf16[32,3712]{1,0:T(8,128)(2,1)S(1)}, bf16[32,3712]{1,0:T(8,128)(2,1)S(1)}, u32[]{:S(2)}, u32[]{:S(2)}) collective-permute-start(bf16[32,3712]{1,0:T(8,128)(2,1)S(1)} %collective-permute-done.refs_2_), channel_id=1, source_target_pairs={{0,16},{1,17},{2,18},{3,19},{4,20},{5,21},{6,22},{7,23},{8,24},{9,... | collective-permute-start | bytes 712712 | tf_op jit(solution)/shard_map/ppermute | solution.py:40
  20.1 1.5 %collective-permute-start.3 = (bf16[32,3712]{1,0:T(8,128)(2,1)S(1)}, bf16[32,3712]{1,0:T(8,128)(2,1)S(1)}, u32[]{:S(2)}, u32[]{:S(2)}) collective-permute-start(bf16[32,3712]{1,0:T(8,128)(2,1)S(1)} %collective-permute-done.refs_2_), channel_id=1, source_target_pairs={{0,2},{1,3},{2,0},{3,1},{4,6},{5,7},{6,4},{7,5},{8,10},{9,11},{10,... | collective-permute-start | bytes 712712 | tf_op jit(solution)/shard_map/ppermute | solution.py:40
  21.6 4.1 %collective-permute-done.1.refs_3_ = bf16[32,3712]{1,0:T(8,128)(2,1)S(1)} collective-permute-done((bf16[32,3712]{1,0:T(8,128)(2,1)S(1)}, bf16[32,3712]{1,0:T(8,128)(2,1)S(1)}, u32[]{:S(2)}, u32[]{:S(2)}) %collective-permute-start.1) | collective-permute-done | bytes 237600 | tf_op jit(solution)/shard_map/ppermute | solution.py:40
  25.7 1.3 collective-permute-start.2
  27.0 0.0 collective-permute-done.3.refs_5_
  27.0 1.5 %collective-permute-start.13 = (bf16[64,3712]{1,0:T(8,128)(2,1)S(1)}, bf16[64,3712]{1,0:T(8,128)(2,1)S(1)}, u32[]{:S(2)}, u32[]{:S(2)}) collective-permute-start(bf16[64,3712]{1,0:T(8,128)(2,1)S(1)} %pad_maximum_fusion.1), channel_id=1, source_target_pairs={{0,4},{1,5},{2,6},{3,7},{4,0},{5,1},{6,2},{7,3},{8,12},{9,13},{10,... | collective-permute-start | bytes 1425416 | tf_op jit(solution)/shard_map/ppermute | solution.py:40
  28.5 1.4 %collective-permute-start.4 = (bf16[32,3712]{1,0:T(8,128)(2,1)S(1)}, bf16[32,3712]{1,0:T(8,128)(2,1)S(1)}, u32[]{:S(2)}, u32[]{:S(2)}) collective-permute-start(bf16[32,3712]{1,0:T(8,128)(2,1)S(1)} %collective-permute-done.refs_2_), channel_id=1, source_target_pairs={{0,18},{1,19},{2,16},{3,17},{4,22},{5,23},{6,20},{7,21},{8,26},{9,... | collective-permute-start | bytes 712712 | tf_op jit(solution)/shard_map/ppermute | solution.py:40
  29.9 0.1 maximum_bitcast_fusion
  30.1 0.1 slice.54
  30.1 0.8 slice.55
  31.0 1.3 %copy.34 = bf16[128,3584]{0,1:T(8,128)(2,1)} copy(bf16[128,3584]{1,0:T(8,128)(2,1)S(1)} %bitcast.29) | data formatting | bytes 1835008 | tf_op jit(solution)/shard_map/reshape | solution.py:222
  32.2 3.6 %collective-permute-done.4.refs_6_ = bf16[32,3712]{1,0:T(8,128)(2,1)S(1)} collective-permute-done((bf16[32,3712]{1,0:T(8,128)(2,1)S(1)}, bf16[32,3712]{1,0:T(8,128)(2,1)S(1)}, u32[]{:S(2)}, u32[]{:S(2)}) %collective-permute-start.4) | collective-permute-done | bytes 237600 | tf_op jit(solution)/shard_map/ppermute | solution.py:40
  35.8 2.6 %collective-permute-done.13.refs_1_ = bf16[64,3712]{1,0:T(8,128)(2,1)S(1)} collective-permute-done((bf16[64,3712]{1,0:T(8,128)(2,1)S(1)}, bf16[64,3712]{1,0:T(8,128)(2,1)S(1)}, u32[]{:S(2)}, u32[]{:S(2)}) %collective-permute-start.13) | collective-permute-done | bytes 475168 | tf_op jit(solution)/shard_map/ppermute | solution.py:40
  38.4 1.5 %collective-permute-start.14 = (bf16[64,3712]{1,0:T(8,128)(2,1)S(1)}, bf16[64,3712]{1,0:T(8,128)(2,1)S(1)}, u32[]{:S(2)}, u32[]{:S(2)}) collective-permute-start(bf16[64,3712]{1,0:T(8,128)(2,1)S(1)} %collective-permute-done.13.refs_1_), channel_id=1, source_target_pairs={{0,16},{1,17},{2,18},{3,19},{4,20},{5,21},{6,22},{7,23},{8,24},{9,... | collective-permute-start | bytes 1425416 | tf_op jit(solution)/shard_map/ppermute | solution.py:40
  39.9 0.5 collective-permute-start.15
  40.4 4.0 %collective-permute-done.2.refs_4_ = bf16[64,3712]{1,0:T(8,128)(2,1)} collective-permute-done((bf16[64,3712]{1,0:T(8,128)(2,1)S(1)}, bf16[64,3712]{1,0:T(8,128)(2,1)}, u32[]{:S(2)}, u32[]{:S(2)}) %collective-permute-start.2) | collective-permute-done | bytes 475168 | tf_op jit(solution)/shard_map/ppermute | solution.py:40
  44.5 2.5 %collective-permute-start.16 = (bf16[64,3712]{1,0:T(8,128)(2,1)S(1)}, bf16[64,3712]{1,0:T(8,128)(2,1)S(1)}, u32[]{:S(2)}, u32[]{:S(2)}) collective-permute-start(bf16[64,3712]{1,0:T(8,128)(2,1)S(1)} %collective-permute-done.13.refs_1_), channel_id=1, source_target_pairs={{0,18},{1,19},{2,16},{3,17},{4,22},{5,23},{6,20},{7,21},{8,26},{9,... | collective-permute-start | bytes 1425416 | tf_op jit(solution)/shard_map/ppermute | solution.py:40
  46.9 21.8 %shard_map.82 = (bf16[2,64,1792]{2,1,0:T(8,128)(2,1)}, bf16[2,64,1792]{2,1,0:T(8,128)(2,1)}, bf16[128,1792]{1,0:T(8,128)(2,1)}, bf16[128,1792]{1,0:T(8,128)(2,1)}) custom-call(s32[4]{0:T(128)} %and_select_fusion.refs_0_, bf16[64,3712]{1,0:T(8,128)(2,1)} %copy-done, bf16[32,3712]{1,0:T(8,128)(2,1)} %copy-done.3, bf16[32,3712]{1,0:T(8,128)(2,1)} %copy-done.11, ...), custom_call_target="tpu_custom_call" | custom-call | flops 11626610688 | bytes 49545216 | tf_op jit(solution)/shard_map/pallas_call | solution.py:274
  68.8 0.3 collective-permute-start.8
  69.1 0.8 collective-permute-start.10
  69.9 0.7 copy-done.5
  70.7 0.2 copy-done.6
  70.8 0.2 copy-done.7
  71.1 22.1 %shard_map.83 = (bf16[2,64,1792]{2,1,0:T(8,128)(2,1)}, bf16[2,64,1792]{2,1,0:T(8,128)(2,1)}, bf16[128,1792]{1,0:T(8,128)(2,1)}, bf16[128,1792]{1,0:T(8,128)(2,1)}) custom-call(s32[4]{0:T(128)} %and_select_fusion.refs_0_, bf16[64,3712]{1,0:T(8,128)(2,1)} %copy-done.4, bf16[64,3712]{1,0:T(8,128)(2,1)} %copy-done.5, bf16[64,3712]{1,0:T(8,128)(2,1)} %copy-done.6, ...), custom_call_target="tpu_custom_call" | custom-call | flops 11626610688 | bytes 49545216 | tf_op jit(solution)/shard_map/pallas_call | solution.py:274
  93.2 1.6 %collective-permute-start.17 = (bf16[2,64,1792]{2,1,0:T(8,128)(2,1)}, bf16[2,64,1792]{2,1,0:T(8,128)(2,1)S(1)}, u32[]{:S(2)}, u32[]{:S(2)}) collective-permute-start(bf16[2,64,1792]{2,1,0:T(8,128)(2,1)} %get-tuple-element.20), channel_id=1, source_target_pairs={{0,2},{1,3},{2,0},{3,1},{4,6},{5,7},{6,4},{7,5},{8,10},{9,11},{10,... | collective-permute-start | bytes 1376264 | tf_op jit(solution)/shard_map/ppermute | solution.py:40
  94.8 1.5 %collective-permute-start.20 = (bf16[128,1792]{1,0:T(8,128)(2,1)}, bf16[128,1792]{1,0:T(8,128)(2,1)S(1)}, u32[]{:S(2)}, u32[]{:S(2)}) collective-permute-start(bf16[128,1792]{1,0:T(8,128)(2,1)} %get-tuple-element.22), channel_id=1, source_target_pairs={{0,16},{1,17},{2,18},{3,19},{4,20},{5,21},{6,22},{7,23},{8,24},{9,... | collective-permute-start | bytes 1376264 | tf_op jit(solution)/shard_map/ppermute | solution.py:40
  96.3 0.1 add_convert_fusion.3
  96.4 0.6 collective-permute-start.9
  97.0 0.1 add_convert_fusion.2
  97.2 0.6 collective-permute-start.11
  97.7 7.8 %collective-permute-done.17 = bf16[2,64,1792]{2,1,0:T(8,128)(2,1)S(1)} collective-permute-done((bf16[2,64,1792]{2,1,0:T(8,128)(2,1)}, bf16[2,64,1792]{2,1,0:T(8,128)(2,1)S(1)}, u32[]{:S(2)}, u32[]{:S(2)}) %collective-permute-start.17) | collective-permute-done | bytes 458784 | tf_op jit(solution)/shard_map/ppermute | solution.py:40
  105.6 0.1 add_convert_fusion.1
  105.7 0.6 collective-permute-start.18
  106.3 0.2 collective-permute-done.20
  106.5 0.1 add_convert_fusion
  106.6 1.4 %collective-permute-start.21 = (bf16[64,1792]{1,0:T(8,128)(2,1)S(1)}, bf16[64,1792]{1,0:T(8,128)(2,1)S(1)}, u32[]{:S(2)}, u32[]{:S(2)}) collective-permute-start(bf16[64,1792]{1,0:T(8,128)(2,1)S(1)} %slice.63), channel_id=1, source_target_pairs={{0,2},{1,3},{2,0},{3,1},{4,6},{5,7},{6,4},{7,5},{8,10},{9,11},{10,... | collective-permute-start | bytes 688136 | tf_op jit(solution)/shard_map/ppermute | solution.py:40
  108.1 0.1 add_convert_fusion.5
  108.1 1.6 %collective-permute-start.12 = (bf16[64,1792]{1,0:T(8,128)(2,1)S(1)}, bf16[64,1792]{1,0:T(8,128)(2,1)S(1)}, u32[]{:S(2)}, u32[]{:S(2)}) collective-permute-start(bf16[64,1792]{1,0:T(8,128)(2,1)S(1)} %add_convert_fusion.5), channel_id=1, source_target_pairs={{0,8},{1,9},{2,10},{3,11},{4,12},{5,13},{6,14},{7,15},{8,0},{9,1},... | collective-permute-start | bytes 688136 | tf_op jit(solution)/shard_map/ppermute | solution.py:40
  109.7 2.1 %collective-permute-done.18 = bf16[64,1792]{1,0:T(8,128)(2,1)S(1)} collective-permute-done((bf16[64,1792]{1,0:T(8,128)(2,1)S(1)}, bf16[64,1792]{1,0:T(8,128)(2,1)S(1)}, u32[]{:S(2)}, u32[]{:S(2)}) %collective-permute-start.18) | collective-permute-done | bytes 229408 | tf_op jit(solution)/shard_map/ppermute | solution.py:40
  111.8 0.1 fusion
  111.8 3.2 %collective-permute-start.19 = (bf16[64,1792]{1,0:T(8,128)(2,1)S(1)}, bf16[64,1792]{1,0:T(8,128)(2,1)S(1)}, u32[]{:S(2)}, u32[]{:S(2)}) collective-permute-start(bf16[64,1792]{1,0:T(8,128)(2,1)S(1)} %fusion), channel_id=1, source_target_pairs={{0,4},{1,5},{2,6},{3,7},{4,0},{5,1},{6,2},{7,3},{8,12},{9,13},{10,... | collective-permute-start | bytes 688136 | tf_op jit(solution)/shard_map/ppermute | solution.py:40
  115.1 0.1 add_convert_fusion.4
  115.1 3.9 %collective-permute-start.22 = (bf16[64,1792]{1,0:T(8,128)(2,1)S(1)}, bf16[64,1792]{1,0:T(8,128)(2,1)S(1)}, u32[]{:S(2)}, u32[]{:S(2)}) collective-permute-start(bf16[64,1792]{1,0:T(8,128)(2,1)S(1)} %add_convert_fusion.4), channel_id=1, source_target_pairs={{0,12},{1,13},{2,14},{3,15},{4,8},{5,9},{6,10},{7,11},{8,4},{9,5},... | collective-permute-start | bytes 688136 | tf_op jit(solution)/shard_map/ppermute | solution.py:40
  119.0 3.1 %collective-permute-done.12 = bf16[64,1792]{1,0:T(8,128)(2,1)S(1)} collective-permute-done((bf16[64,1792]{1,0:T(8,128)(2,1)S(1)}, bf16[64,1792]{1,0:T(8,128)(2,1)S(1)}, u32[]{:S(2)}, u32[]{:S(2)}) %collective-permute-start.12) | collective-permute-done | bytes 229408 | tf_op jit(solution)/shard_map/ppermute | solution.py:40
  122.2 2.8 %collective-permute-done.22 = bf16[64,1792]{1,0:T(8,128)(2,1)S(1)} collective-permute-done((bf16[64,1792]{1,0:T(8,128)(2,1)S(1)}, bf16[64,1792]{1,0:T(8,128)(2,1)S(1)}, u32[]{:S(2)}, u32[]{:S(2)}) %collective-permute-start.22) | collective-permute-done | bytes 229408 | tf_op jit(solution)/shard_map/ppermute | solution.py:40
  125.0 0.8 fusion.4
  (47 shorter events, 0.3 us)
Async XLA Ops:
  0.0 7.4 %copy-start.2 = (bf16[32,2,3584]{2,1,0:T(2,128)(2,1)S(1)}, bf16[32,2,3584]{2,1,0:T(2,128)(2,1)}, u32[]{:S(2)}) copy-start(bf16[32,2,3584]{2,1,0:T(2,128)(2,1)} %param.14) | copy-start | bytes 1376260
  0.0 46.9 %collective-permute-start.6 = (bf16[2,2,3584,512]{3,2,1,0:T(8,128)(2,1)}, bf16[2,2,3584,512]{3,2,1,0:T(8,128)(2,1)}, u32[]{:S(2)}, u32[]{:S(2)}) collective-permute-start(bf16[2,2,3584,512]{3,2,1,0:T(8,128)(2,1)} %refs_7_.1), channel_id=1, source_target_pairs={{0,1},{1,0},{2,3},{3,2},{4,5},{5,4},{6,7},{7,6},{8,9},{9,8},{10,11... | collective-permute-start | bytes 44040200 | tf_op jit(solution)/shard_map/ppermute | solution.py:40
  0.5 46.5 %collective-permute-start.7 = (bf16[2,512,3584]{2,1,0:T(8,128)(2,1)}, bf16[2,512,3584]{2,1,0:T(8,128)(2,1)}, u32[]{:S(2)}, u32[]{:S(2)}) collective-permute-start(bf16[2,512,3584]{2,1,0:T(8,128)(2,1)} %refs_9_.3), channel_id=1, source_target_pairs={{0,1},{1,0},{2,3},{3,2},{4,5},{5,4},{6,7},{7,6},{8,9},{9,8},{10,11... | collective-permute-start | bytes 22020104 | tf_op jit(solution)/shard_map/ppermute | solution.py:40
  3.3 22.5 %copy-start = (bf16[64,3712]{1,0:T(8,128)(2,1)}, bf16[64,3712]{1,0:T(8,128)(2,1)S(1)}, u32[]{:S(2)}) copy-start(bf16[64,3712]{1,0:T(8,128)(2,1)S(1)} %concatenate.27.refs_1_) | copy-start | bytes 1425412
  3.3 4.8 %copy-start.14 = (bf16[32,3584]{1,0:T(8,128)(2,1)S(1)}, bf16[32,3584]{1,0:T(8,128)(2,1)}, u32[]{:S(2)}) copy-start(bf16[32,3584]{1,0:T(8,128)(2,1)} %param.15) | copy-start | bytes 688132
  3.3 15.2 %collective-permute-start = (bf16[32,3712]{1,0:T(8,128)(2,1)S(1)}, bf16[32,3712]{1,0:T(8,128)(2,1)S(1)}, u32[]{:S(2)}, u32[]{:S(2)}) collective-permute-start(bf16[32,3712]{1,0:T(8,128)(2,1)S(1)} %constant_dynamic-slice_fusion), channel_id=1, source_target_pairs={{0,8},{1,9},{2,10},{3,11},{4,12},{5,13},{6,14},{7,15},{8,0},{9,1},... | collective-permute-start | bytes 712712 | tf_op jit(solution)/shard_map/ppermute | solution.py:40
  8.1 0.7 copy-start.15
  8.2 20.3 %collective-permute-start.5 = (bf16[96,3584]{1,0:T(8,128)(2,1)S(1)}, bf16[96,3584]{1,0:T(8,128)(2,1)S(1)}, u32[]{:S(2)}, u32[]{:S(2)}) collective-permute-start(bf16[96,3584]{1,0:T(8,128)(2,1)S(1)} %pad_maximum_fusion), channel_id=1, source_target_pairs={{0,1},{1,0},{2,3},{3,2},{4,5},{5,4},{6,7},{7,6},{8,9},{9,8},{10,11... | collective-permute-start | bytes 2064392 | tf_op jit(solution)/shard_map/ppermute | solution.py:40
  18.5 11.5 %copy-start.3 = (bf16[32,3712]{1,0:T(8,128)(2,1)}, bf16[32,3712]{1,0:T(8,128)(2,1)S(1)}, u32[]{:S(2)}) copy-start(bf16[32,3712]{1,0:T(8,128)(2,1)S(1)} %collective-permute-done.refs_2_) | copy-start | bytes 712708
  18.5 7.2 %collective-permute-start.1 = (bf16[32,3712]{1,0:T(8,128)(2,1)S(1)}, bf16[32,3712]{1,0:T(8,128)(2,1)S(1)}, u32[]{:S(2)}, u32[]{:S(2)}) collective-permute-start(bf16[32,3712]{1,0:T(8,128)(2,1)S(1)} %collective-permute-done.refs_2_), channel_id=1, source_target_pairs={{0,16},{1,17},{2,18},{3,19},{4,20},{5,21},{6,22},{7,23},{8,24},{9,... | collective-permute-start | bytes 712712 | tf_op jit(solution)/shard_map/ppermute | solution.py:40
  20.1 6.9 %collective-permute-start.3 = (bf16[32,3712]{1,0:T(8,128)(2,1)S(1)}, bf16[32,3712]{1,0:T(8,128)(2,1)S(1)}, u32[]{:S(2)}, u32[]{:S(2)}) collective-permute-start(bf16[32,3712]{1,0:T(8,128)(2,1)S(1)} %collective-permute-done.refs_2_), channel_id=1, source_target_pairs={{0,2},{1,3},{2,0},{3,1},{4,6},{5,7},{6,4},{7,5},{8,10},{9,11},{10,... | collective-permute-start | bytes 712712 | tf_op jit(solution)/shard_map/ppermute | solution.py:40
  25.7 4.2 %copy-start.11 = (bf16[32,3712]{1,0:T(8,128)(2,1)}, bf16[32,3712]{1,0:T(8,128)(2,1)S(1)}, u32[]{:S(2)}) copy-start(bf16[32,3712]{1,0:T(8,128)(2,1)S(1)} %collective-permute-done.1.refs_3_) | copy-start | bytes 712708
  25.7 18.7 %collective-permute-start.2 = (bf16[64,3712]{1,0:T(8,128)(2,1)S(1)}, bf16[64,3712]{1,0:T(8,128)(2,1)}, u32[]{:S(2)}, u32[]{:S(2)}) collective-permute-start(bf16[64,3712]{1,0:T(8,128)(2,1)S(1)} %concatenate.27.refs_1_), channel_id=1, source_target_pairs={{0,2},{1,3},{2,0},{3,1},{4,6},{5,7},{6,4},{7,5},{8,10},{9,11},{10,... | collective-permute-start | bytes 1425416 | tf_op jit(solution)/shard_map/ppermute | solution.py:40
  27.0 2.9 %copy-start.12 = (bf16[32,3712]{1,0:T(8,128)(2,1)}, bf16[32,3712]{1,0:T(8,128)(2,1)S(1)}, u32[]{:S(2)}) copy-start(bf16[32,3712]{1,0:T(8,128)(2,1)S(1)} %collective-permute-done.3.refs_5_) | copy-start | bytes 712708
  27.0 11.4 %collective-permute-start.13 = (bf16[64,3712]{1,0:T(8,128)(2,1)S(1)}, bf16[64,3712]{1,0:T(8,128)(2,1)S(1)}, u32[]{:S(2)}, u32[]{:S(2)}) collective-permute-start(bf16[64,3712]{1,0:T(8,128)(2,1)S(1)} %pad_maximum_fusion.1), channel_id=1, source_target_pairs={{0,4},{1,5},{2,6},{3,7},{4,0},{5,1},{6,2},{7,3},{8,12},{9,13},{10,... | collective-permute-start | bytes 1425416 | tf_op jit(solution)/shard_map/ppermute | solution.py:40
  28.5 7.3 %collective-permute-start.4 = (bf16[32,3712]{1,0:T(8,128)(2,1)S(1)}, bf16[32,3712]{1,0:T(8,128)(2,1)S(1)}, u32[]{:S(2)}, u32[]{:S(2)}) collective-permute-start(bf16[32,3712]{1,0:T(8,128)(2,1)S(1)} %collective-permute-done.refs_2_), channel_id=1, source_target_pairs={{0,18},{1,19},{2,16},{3,17},{4,22},{5,23},{6,20},{7,21},{8,26},{9,... | collective-permute-start | bytes 712712 | tf_op jit(solution)/shard_map/ppermute | solution.py:40
  35.8 11.1 %copy-start.13 = (bf16[32,3712]{1,0:T(8,128)(2,1)}, bf16[32,3712]{1,0:T(8,128)(2,1)S(1)}, u32[]{:S(2)}) copy-start(bf16[32,3712]{1,0:T(8,128)(2,1)S(1)} %collective-permute-done.4.refs_6_) | copy-start | bytes 712708
  38.4 30.4 %copy-start.4 = (bf16[64,3712]{1,0:T(8,128)(2,1)}, bf16[64,3712]{1,0:T(8,128)(2,1)S(1)}, u32[]{:S(2)}) copy-start(bf16[64,3712]{1,0:T(8,128)(2,1)S(1)} %collective-permute-done.13.refs_1_) | copy-start | bytes 1425412
  38.4 31.5 %collective-permute-start.14 = (bf16[64,3712]{1,0:T(8,128)(2,1)S(1)}, bf16[64,3712]{1,0:T(8,128)(2,1)S(1)}, u32[]{:S(2)}, u32[]{:S(2)}) collective-permute-start(bf16[64,3712]{1,0:T(8,128)(2,1)S(1)} %collective-permute-done.13.refs_1_), channel_id=1, source_target_pairs={{0,16},{1,17},{2,18},{3,19},{4,20},{5,21},{6,22},{7,23},{8,24},{9,... | collective-permute-start | bytes 1425416 | tf_op jit(solution)/shard_map/ppermute | solution.py:40
  39.9 30.0 %collective-permute-start.15 = (bf16[64,3712]{1,0:T(8,128)(2,1)S(1)}, bf16[64,3712]{1,0:T(8,128)(2,1)S(1)}, u32[]{:S(2)}, u32[]{:S(2)}) collective-permute-start(bf16[64,3712]{1,0:T(8,128)(2,1)S(1)} %collective-permute-done.13.refs_1_), channel_id=1, source_target_pairs={{0,2},{1,3},{2,0},{3,1},{4,6},{5,7},{6,4},{7,5},{8,10},{9,11},{10,... | collective-permute-start | bytes 1425416 | tf_op jit(solution)/shard_map/ppermute | solution.py:40
  44.5 25.4 %collective-permute-start.16 = (bf16[64,3712]{1,0:T(8,128)(2,1)S(1)}, bf16[64,3712]{1,0:T(8,128)(2,1)S(1)}, u32[]{:S(2)}, u32[]{:S(2)}) collective-permute-start(bf16[64,3712]{1,0:T(8,128)(2,1)S(1)} %collective-permute-done.13.refs_1_), channel_id=1, source_target_pairs={{0,18},{1,19},{2,16},{3,17},{4,22},{5,23},{6,20},{7,21},{8,26},{9,... | collective-permute-start | bytes 1425416 | tf_op jit(solution)/shard_map/ppermute | solution.py:40
  68.8 27.5 %collective-permute-start.8 = (bf16[2,64,1792]{2,1,0:T(8,128)(2,1)}, bf16[2,64,1792]{2,1,0:T(8,128)(2,1)S(1)}, u32[]{:S(2)}, u32[]{:S(2)}) collective-permute-start(bf16[2,64,1792]{2,1,0:T(8,128)(2,1)} %get-tuple-element.15), channel_id=1, source_target_pairs={{0,2},{1,3},{2,0},{3,1},{4,6},{5,7},{6,4},{7,5},{8,10},{9,11},{10,... | collective-permute-start | bytes 1376264 | tf_op jit(solution)/shard_map/ppermute | solution.py:40
  69.1 27.9 %collective-permute-start.10 = (bf16[128,1792]{1,0:T(8,128)(2,1)}, bf16[128,1792]{1,0:T(8,128)(2,1)S(1)}, u32[]{:S(2)}, u32[]{:S(2)}) collective-permute-start(bf16[128,1792]{1,0:T(8,128)(2,1)} %get-tuple-element.17), channel_id=1, source_target_pairs={{0,16},{1,17},{2,18},{3,19},{4,20},{5,21},{6,22},{7,23},{8,24},{9,... | collective-permute-start | bytes 1376264 | tf_op jit(solution)/shard_map/ppermute | solution.py:40
  69.9 0.8 copy-start.5
  69.9 0.9 copy-start.6
  69.9 1.1 copy-start.7
  71.0 25.2 %copy-start.1 = (bf16[2,64,1792]{2,1,0:T(8,128)(2,1)S(1)}, bf16[2,64,1792]{2,1,0:T(8,128)(2,1)}, u32[]{:S(2)}) copy-start(bf16[2,64,1792]{2,1,0:T(8,128)(2,1)} %get-tuple-element.14.refs_11_) | copy-start | bytes 1376260
  93.2 3.9 %copy-start.8 = (bf16[128,1792]{1,0:T(8,128)(2,1)S(1)}, bf16[128,1792]{1,0:T(8,128)(2,1)}, u32[]{:S(2)}) copy-start(bf16[128,1792]{1,0:T(8,128)(2,1)} %get-tuple-element.16) | copy-start | bytes 1376260
  93.2 12.4 %collective-permute-start.17 = (bf16[2,64,1792]{2,1,0:T(8,128)(2,1)}, bf16[2,64,1792]{2,1,0:T(8,128)(2,1)S(1)}, u32[]{:S(2)}, u32[]{:S(2)}) collective-permute-start(bf16[2,64,1792]{2,1,0:T(8,128)(2,1)} %get-tuple-element.20), channel_id=1, source_target_pairs={{0,2},{1,3},{2,0},{3,1},{4,6},{5,7},{6,4},{7,5},{8,10},{9,11},{10,... | collective-permute-start | bytes 1376264 | tf_op jit(solution)/shard_map/ppermute | solution.py:40
  94.8 11.7 %collective-permute-start.20 = (bf16[128,1792]{1,0:T(8,128)(2,1)}, bf16[128,1792]{1,0:T(8,128)(2,1)S(1)}, u32[]{:S(2)}, u32[]{:S(2)}) collective-permute-start(bf16[128,1792]{1,0:T(8,128)(2,1)} %get-tuple-element.22), channel_id=1, source_target_pairs={{0,16},{1,17},{2,18},{3,19},{4,20},{5,21},{6,22},{7,23},{8,24},{9,... | collective-permute-start | bytes 1376264 | tf_op jit(solution)/shard_map/ppermute | solution.py:40
  96.4 9.1 %copy-start.10 = (bf16[2,64,1792]{2,1,0:T(8,128)(2,1)S(1)}, bf16[2,64,1792]{2,1,0:T(8,128)(2,1)}, u32[]{:S(2)}) copy-start(bf16[2,64,1792]{2,1,0:T(8,128)(2,1)} %get-tuple-element.19) | copy-start | bytes 1376260
  96.4 22.6 %collective-permute-start.9 = (bf16[64,1792]{1,0:T(8,128)(2,1)S(1)}, bf16[64,1792]{1,0:T(8,128)(2,1)S(1)}, u32[]{:S(2)}, u32[]{:S(2)}) collective-permute-start(bf16[64,1792]{1,0:T(8,128)(2,1)S(1)} %slice_bitcast_fusion.2), channel_id=1, source_target_pairs={{0,16},{1,17},{2,18},{3,19},{4,20},{5,21},{6,22},{7,23},{8,24},{9,... | collective-permute-start | bytes 688136 | tf_op jit(solution)/shard_map/ppermute | solution.py:40
  97.2 9.3 %copy-start.9 = (bf16[128,1792]{1,0:T(8,128)(2,1)S(1)}, bf16[128,1792]{1,0:T(8,128)(2,1)}, u32[]{:S(2)}) copy-start(bf16[128,1792]{1,0:T(8,128)(2,1)} %get-tuple-element.21) | copy-start | bytes 1376260
  97.2 10.9 %collective-permute-start.11 = (bf16[64,1792]{1,0:T(8,128)(2,1)S(1)}, bf16[64,1792]{1,0:T(8,128)(2,1)S(1)}, u32[]{:S(2)}, u32[]{:S(2)}) collective-permute-start(bf16[64,1792]{1,0:T(8,128)(2,1)S(1)} %slice.59), channel_id=1, source_target_pairs={{0,2},{1,3},{2,0},{3,1},{4,6},{5,7},{6,4},{7,5},{8,10},{9,11},{10,... | collective-permute-start | bytes 688136 | tf_op jit(solution)/shard_map/ppermute | solution.py:40
  105.7 6.1 %collective-permute-start.18 = (bf16[64,1792]{1,0:T(8,128)(2,1)S(1)}, bf16[64,1792]{1,0:T(8,128)(2,1)S(1)}, u32[]{:S(2)}, u32[]{:S(2)}) collective-permute-start(bf16[64,1792]{1,0:T(8,128)(2,1)S(1)} %slice_bitcast_fusion), channel_id=1, source_target_pairs={{0,16},{1,17},{2,18},{3,19},{4,20},{5,21},{6,22},{7,23},{8,24},{9,... | collective-permute-start | bytes 688136 | tf_op jit(solution)/shard_map/ppermute | solution.py:40
  106.6 8.4 %collective-permute-start.21 = (bf16[64,1792]{1,0:T(8,128)(2,1)S(1)}, bf16[64,1792]{1,0:T(8,128)(2,1)S(1)}, u32[]{:S(2)}, u32[]{:S(2)}) collective-permute-start(bf16[64,1792]{1,0:T(8,128)(2,1)S(1)} %slice.63), channel_id=1, source_target_pairs={{0,2},{1,3},{2,0},{3,1},{4,6},{5,7},{6,4},{7,5},{8,10},{9,11},{10,... | collective-permute-start | bytes 688136 | tf_op jit(solution)/shard_map/ppermute | solution.py:40
  108.1 14.0 %collective-permute-start.12 = (bf16[64,1792]{1,0:T(8,128)(2,1)S(1)}, bf16[64,1792]{1,0:T(8,128)(2,1)S(1)}, u32[]{:S(2)}, u32[]{:S(2)}) collective-permute-start(bf16[64,1792]{1,0:T(8,128)(2,1)S(1)} %add_convert_fusion.5), channel_id=1, source_target_pairs={{0,8},{1,9},{2,10},{3,11},{4,12},{5,13},{6,14},{7,15},{8,0},{9,1},... | collective-permute-start | bytes 688136 | tf_op jit(solution)/shard_map/ppermute | solution.py:40
  111.8 10.3 %collective-permute-start.19 = (bf16[64,1792]{1,0:T(8,128)(2,1)S(1)}, bf16[64,1792]{1,0:T(8,128)(2,1)S(1)}, u32[]{:S(2)}, u32[]{:S(2)}) collective-permute-start(bf16[64,1792]{1,0:T(8,128)(2,1)S(1)} %fusion), channel_id=1, source_target_pairs={{0,4},{1,5},{2,6},{3,7},{4,0},{5,1},{6,2},{7,3},{8,12},{9,13},{10,... | collective-permute-start | bytes 688136 | tf_op jit(solution)/shard_map/ppermute | solution.py:40
  115.1 9.9 %collective-permute-start.22 = (bf16[64,1792]{1,0:T(8,128)(2,1)S(1)}, bf16[64,1792]{1,0:T(8,128)(2,1)S(1)}, u32[]{:S(2)}, u32[]{:S(2)}) collective-permute-start(bf16[64,1792]{1,0:T(8,128)(2,1)S(1)} %add_convert_fusion.4), channel_id=1, source_target_pairs={{0,12},{1,13},{2,14},{3,15},{4,8},{5,9},{6,10},{7,11},{8,4},{9,5},... | collective-permute-start | bytes 688136 | tf_op jit(solution)/shard_map/ppermute | solution.py:40

commit v5 on v4

--- a/solution.py
+++ b/solution.py
@@ -47,8 +47,9 @@
     units = refs[1 : 1 + n_units]
     sh_gu, sh_dn, gu_own, gu_sib, dn_own, dn_sib = refs[1 + n_units : 7 + n_units]
     refs = refs[7 + n_units + n_after :]
-    outs = [refs[i * nx : (i + 1) * nx] for i in range(len(levels))]
-    rows_in, shared_w, wgu, wdn, act, scale, sem_x, sem_s, sem_gu, sem_dn = refs[len(levels) * nx :]
+    groups = ny if x_first is None else len(levels)
+    outs = [refs[i * nx : (i + 1) * nx] for i in range(groups)]
+    rows_in, shared_w, wgu, wdn, act, scale, sem_x, sem_s, sem_gu, sem_dn = refs[groups * nx :]
     mx = lax.axis_index("dp")
     part = tok_rows // nx
     width = model_dim // nx
@@ -169,6 +170,12 @@
             arrived(copy)
         columns = pl.ds(*cuts[n])
         value = jnp.dot(act[...], wdn[h, :, columns], preferred_element_type=f32).astype(bf16)
+        if x_first is None:
+            for i in range(len(levels)):
+                for j in range(ny):
+                    base = i * level_rows + j * tok_rows
+                    outs[j][h][i, :, columns] = value[base : base + tok_rows]
+            continue
         for i in range(len(levels)):
             if x_first[i]:
                 outs[i][h][:, columns] = value[i * level_rows : (i + 1) * level_rows]
@@ -242,7 +249,7 @@
     def spread(x):
         return [[hop(x, 2 * j, h) if j or h else x for h in range(nx)] for j in range(ny)]
 
-    near_units = spread(held[part:])
+    near_units = spread(lax.optimization_barrier([held[part:]] + own[1:])[0])
     near = [u for j in range(ny) for u in near_units[j]]
     far = lax.optimization_barrier([far] + near)[0]
     far_units = spread(far)
@@ -262,11 +269,14 @@
     tiles = hidden // hid_tile
     after = []
     for levels in (list(range(half)), list(range(half, nz))):
-        x_first = [k % 2 == 1 for k in levels]
+        x_first = [k % 2 == 1 for k in levels] if levels[0] else None
         chunk = chunks[levels[0] // half]
         n_rows = len(levels) * ny * tok_rows
         out_shape = []
-        for first in x_first:
+        if x_first is None:
+            shape = (len(levels), tok_rows, width)
+            out_shape = [jax.ShapeDtypeStruct(shape, bf16)] * (ny * nx)
+        for first in x_first or []:
             shape = (ny * tok_rows, width) if first else (nx, tok_rows, width)
             out_shape += [jax.ShapeDtypeStruct(shape, bf16)] * nx
         k_total = n_slots * hidden + sp
@@ -309,6 +319,16 @@
             ),
         )(slots, *chunk, sh_gu, sh_dn, expert_gate_up, gu_sib, expert_down, dn_sib, *after)
         after = outs[:1]
+        if x_first is None:
+            got = [
+                hop(outs[j * nx + h], 2 * j, h) for j in range(ny) for h in range(nx) if j or h
+            ]
+            planes = added(outs[0], got)
+            early = got
+            for i, k in enumerate(levels):
+                done[k] = planes[i] if k == 0 else hop(planes[i].astype(bf16), bits[k] * zs)
+            continue
+        outs = lax.optimization_barrier(list(outs) + early)[: len(outs)]
         for i, k in enumerate(levels):
             sent = outs[i * nx : (i + 1) * nx]
             if x_first[i]:

time: 126 us -> 120 us (0.952)
  waiting for transfers between devices: 39.4 us -> 32.6 us
    ppermute x23 -> x22, waiting for transfers between devices: 39.4 us -> 32.6 us  [hop(): lax.ppermute(x, ('dp', 'expert'), [(i, i ^ by_x * ne + by) for i in range...]
    ppermute x23 -> x22, starting transfers between devices: 32.5 us -> 33.7 us  [hop(): lax.ppermute(x, ('dp', 'expert'), [(i, i ^ by_x * ne + by) for i in range...]
  transfers between devices with their start and end apart: 23 -> 22, of which waited for: 10 -> 9; matrix products, arithmetic and copies ran while one was open for 6% -> 6% of each run, Pallas kernels for 35% -> 37%
where the time goes in v5:
time: 120 us
  Pallas kernels  43.8 us (36%)
  starting transfers between devices  33.7 us (28%)
  waiting for transfers between devices  32.6 us (27%)
  local copies, waits for them, and re-layouts  6.3 us (5%)
  other arithmetic  3.14 us (3%)
    pallas_call x2, Pallas kernels, local(): pl.pallas_call(functools.partial(ffn_kernel, levels, x_first, nx, ny, tok...  43.8 us
    ppermute x22, starting transfers between devices, hop(): lax.ppermute(x, ('dp', 'expert'), [(i, i ^ by_x * ne + by) for i in range...  33.7 us
    ppermute x22, waiting for transfers between devices, hop(): lax.ppermute(x, ('dp', 'expert'), [(i, i ^ by_x * ne + by) for i in range...  32.6 us
  transfers between devices with their start and end apart: 22, of which 9 were waited for; matrix products, arithmetic and copies ran while one was open for 6% of the time, Pallas kernels for 37%

profile of v5, /device:TPU:0, one launch (start us, length us, event | category | flops | bytes accessed | tf_op | source)
XLA Modules:
  0.0 119.9 jit_solution(12939215861303151218)
XLA Ops:
  0.0 0.5 collective-permute-start.6
  0.5 0.1 collective-permute-start.7
  0.5 0.8 copy.27
  1.3 0.7 convert_element_type.76
  2.0 0.1 copy.31
  2.1 1.1 concatenate.27.refs_1_
  3.3 3.0 %collective-permute-start.1 = (bf16[64,3712]{1,0:T(8,128)(2,1)S(1)}, bf16[64,3712]{1,0:T(8,128)(2,1)S(1)}, u32[]{:S(2)}, u32[]{:S(2)}) collective-permute-start(bf16[64,3712]{1,0:T(8,128)(2,1)S(1)} %concatenate.27.refs_1_), channel_id=1, source_target_pairs={{0,2},{1,3},{2,0},{3,1},{4,6},{5,7},{6,4},{7,5},{8,10},{9,11},{10,... | collective-permute-start | bytes 1425416 | tf_op jit(solution)/shard_map/ppermute | solution.py:40
  6.3 0.0 copy-start.13
  6.3 2.7 %collective-permute-start = (bf16[32,3712]{1,0:T(8,128)(2,1)S(1)}, bf16[32,3712]{1,0:T(8,128)(2,1)S(1)}, u32[]{:S(2)}, u32[]{:S(2)}) collective-permute-start(bf16[32,3712]{1,0:T(8,128)(2,1)S(1)} %constant_dynamic-slice_fusion), channel_id=1, source_target_pairs={{0,8},{1,9},{2,10},{3,11},{4,12},{5,13},{6,14},{7,15},{8,0},{9,1},... | collective-permute-start | bytes 712712 | tf_op jit(solution)/shard_map/ppermute | solution.py:40
  9.0 0.6 fusion.11
  9.6 0.0 copy-start.14
  9.6 0.1 copy_bitcast_fusion
  9.8 0.1 collective-permute-start.5
  9.9 0.1 and_select_fusion.4
  10.0 0.3 copy-done.14
  10.3 0.2 select_reduce_fusion
  10.5 0.6 and_select_fusion.refs_0_
  11.1 8.8 %collective-permute-done.refs_2_ = bf16[32,3712]{1,0:T(8,128)(2,1)S(1)} collective-permute-done((bf16[32,3712]{1,0:T(8,128)(2,1)S(1)}, bf16[32,3712]{1,0:T(8,128)(2,1)S(1)}, u32[]{:S(2)}, u32[]{:S(2)}) %collective-permute-start) | collective-permute-done | bytes 237600 | tf_op jit(solution)/shard_map/ppermute | solution.py:40
  19.9 0.0 collective-permute-done.1.refs_4_
  19.9 1.6 %collective-permute-start.2 = (bf16[32,3712]{1,0:T(8,128)(2,1)S(1)}, bf16[32,3712]{1,0:T(8,128)(2,1)S(1)}, u32[]{:S(2)}, u32[]{:S(2)}) collective-permute-start(bf16[32,3712]{1,0:T(8,128)(2,1)S(1)} %collective-permute-done.refs_2_), channel_id=1, source_target_pairs={{0,16},{1,17},{2,18},{3,19},{4,20},{5,21},{6,22},{7,23},{8,24},{9,... | collective-permute-start | bytes 712712 | tf_op jit(solution)/shard_map/ppermute | solution.py:40
  21.5 0.7 collective-permute-start.12
  22.1 2.1 %collective-permute-done.5 = bf16[96,3584]{1,0:T(8,128)(2,1)S(1)} collective-permute-done((bf16[96,3584]{1,0:T(8,128)(2,1)S(1)}, bf16[96,3584]{1,0:T(8,128)(2,1)S(1)}, u32[]{:S(2)}, u32[]{:S(2)}) %collective-permute-start.5) | collective-permute-done | bytes 688160 | tf_op jit(solution)/shard_map/ppermute | solution.py:40
  24.2 2.9 %collective-permute-start.3 = (bf16[32,3712]{1,0:T(8,128)(2,1)S(1)}, bf16[32,3712]{1,0:T(8,128)(2,1)S(1)}, u32[]{:S(2)}, u32[]{:S(2)}) collective-permute-start(bf16[32,3712]{1,0:T(8,128)(2,1)S(1)} %collective-permute-done.refs_2_), channel_id=1, source_target_pairs={{0,2},{1,3},{2,0},{3,1},{4,6},{5,7},{6,4},{7,5},{8,10},{9,11},{10,... | collective-permute-start | bytes 712712 | tf_op jit(solution)/shard_map/ppermute | solution.py:40
  27.1 0.0 collective-permute-done.2.refs_3_
  27.1 1.4 %collective-permute-start.4 = (bf16[32,3712]{1,0:T(8,128)(2,1)S(1)}, bf16[32,3712]{1,0:T(8,128)(2,1)}, u32[]{:S(2)}, u32[]{:S(2)}) collective-permute-start(bf16[32,3712]{1,0:T(8,128)(2,1)S(1)} %collective-permute-done.refs_2_), channel_id=1, source_target_pairs={{0,18},{1,19},{2,16},{3,17},{4,22},{5,23},{6,20},{7,21},{8,26},{9,... | collective-permute-start | bytes 712712 | tf_op jit(solution)/shard_map/ppermute | solution.py:40
  28.5 0.1 maximum_bitcast_fusion
  28.7 0.1 slice.45
  28.8 0.8 slice.46
  29.6 1.3 %copy.34 = bf16[128,3584]{0,1:T(8,128)(2,1)} copy(bf16[128,3584]{1,0:T(8,128)(2,1)S(1)} %bitcast.34) | data formatting | bytes 1835008 | tf_op jit(solution)/shard_map/reshape | solution.py:229
  30.9 7.4 %collective-permute-done.3.refs_5_ = bf16[32,3712]{1,0:T(8,128)(2,1)S(1)} collective-permute-done((bf16[32,3712]{1,0:T(8,128)(2,1)S(1)}, bf16[32,3712]{1,0:T(8,128)(2,1)S(1)}, u32[]{:S(2)}, u32[]{:S(2)}) %collective-permute-start.3) | collective-permute-done | bytes 237600 | tf_op jit(solution)/shard_map/ppermute | solution.py:40
  38.3 1.8 %collective-permute-start.13 = (bf16[64,3712]{1,0:T(8,128)(2,1)S(1)}, bf16[64,3712]{1,0:T(8,128)(2,1)S(1)}, u32[]{:S(2)}, u32[]{:S(2)}) collective-permute-start(bf16[64,3712]{1,0:T(8,128)(2,1)S(1)} %collective-permute-done.12.refs_1_), channel_id=1, source_target_pairs={{0,16},{1,17},{2,18},{3,19},{4,20},{5,21},{6,22},{7,23},{8,24},{9,... | collective-permute-start | bytes 1425416 | tf_op jit(solution)/shard_map/ppermute | solution.py:40
  40.1 1.5 %collective-permute-start.14 = (bf16[64,3712]{1,0:T(8,128)(2,1)S(1)}, bf16[64,3712]{1,0:T(8,128)(2,1)S(1)}, u32[]{:S(2)}, u32[]{:S(2)}) collective-permute-start(bf16[64,3712]{1,0:T(8,128)(2,1)S(1)} %collective-permute-done.12.refs_1_), channel_id=1, source_target_pairs={{0,2},{1,3},{2,0},{3,1},{4,6},{5,7},{6,4},{7,5},{8,10},{9,11},{10,... | collective-permute-start | bytes 1425416 | tf_op jit(solution)/shard_map/ppermute | solution.py:40
  41.6 0.3 collective-permute-start.15
  41.8 0.0 collective-permute-done.7.refs_12_.refs_10_
  41.8 0.0 collective-permute-done.6.refs_10_.refs_8_
  41.9 21.7 %shard_map.82 = (bf16[2,64,1792]{2,1,0:T(8,128)(2,1)}, bf16[2,64,1792]{2,1,0:T(8,128)(2,1)}, bf16[2,64,1792]{2,1,0:T(8,128)(2,1)}, bf16[2,64,1792]{2,1,0:T(8,128)(2,1)}) custom-call(s32[4]{0:T(128)} %and_select_fusion.refs_0_, bf16[64,3712]{1,0:T(8,128)(2,1)} %copy-done, bf16[32,3712]{1,0:T(8,128)(2,1)} %copy-done.3, bf16[32,3712]{1,0:T(8,128)(2,1)} %copy-done.11, ...), custom_call_target="tpu_custom_call" | custom-call | flops 11626610688 | bytes 49545216 | tf_op jit(solution)/shard_map/pallas_call | solution.py:284
  63.5 2.7 %collective-permute-start.10 = (bf16[2,64,1792]{2,1,0:T(8,128)(2,1)}, bf16[2,64,1792]{2,1,0:T(8,128)(2,1)S(1)}, u32[]{:S(2)}, u32[]{:S(2)}) collective-permute-start(bf16[2,64,1792]{2,1,0:T(8,128)(2,1)} %get-tuple-element.23), channel_id=1, source_target_pairs={{0,18},{1,19},{2,16},{3,17},{4,22},{5,23},{6,20},{7,21},{8,26},{9,... | collective-permute-start | bytes 1376264 | tf_op jit(solution)/shard_map/ppermute | solution.py:40
  66.3 0.5 collective-permute-start.8
  66.8 0.3 collective-permute-start.9
  67.1 0.0 collective-permute-done.14.refs_3_
  67.1 0.5 copy-done.6
  67.6 0.3 copy-done.7
  67.9 0.2 copy-done.8
  68.1 22.1 %shard_map.83 = (bf16[2,64,1792]{2,1,0:T(8,128)(2,1)}, bf16[2,64,1792]{2,1,0:T(8,128)(2,1)}, bf16[128,1792]{1,0:T(8,128)(2,1)}, bf16[128,1792]{1,0:T(8,128)(2,1)}) custom-call(s32[4]{0:T(128)} %and_select_fusion.refs_0_, bf16[64,3712]{1,0:T(8,128)(2,1)} %copy-done.5, bf16[64,3712]{1,0:T(8,128)(2,1)} %copy-done.6, bf16[64,3712]{1,0:T(8,128)(2,1)} %copy-done.7, ...), custom_call_target="tpu_custom_call" | custom-call | flops 11626610688 | bytes 49545216 | tf_op jit(solution)/shard_map/pallas_call | solution.py:284
  90.3 0.0 collective-permute-done.10
  90.3 1.8 %collective-permute-start.16 = (bf16[2,64,1792]{2,1,0:T(8,128)(2,1)}, bf16[2,64,1792]{2,1,0:T(8,128)(2,1)S(1)}, u32[]{:S(2)}, u32[]{:S(2)}) collective-permute-start(bf16[2,64,1792]{2,1,0:T(8,128)(2,1)} %get-tuple-element.30), channel_id=1, source_target_pairs={{0,2},{1,3},{2,0},{3,1},{4,6},{5,7},{6,4},{7,5},{8,10},{9,11},{10,... | collective-permute-start | bytes 1376264 | tf_op jit(solution)/shard_map/ppermute | solution.py:40
  92.1 1.5 %collective-permute-start.19 = (bf16[128,1792]{1,0:T(8,128)(2,1)}, bf16[128,1792]{1,0:T(8,128)(2,1)S(1)}, u32[]{:S(2)}, u32[]{:S(2)}) collective-permute-start(bf16[128,1792]{1,0:T(8,128)(2,1)} %get-tuple-element.32), channel_id=1, source_target_pairs={{0,16},{1,17},{2,18},{3,19},{4,20},{5,21},{6,22},{7,23},{8,24},{9,... | collective-permute-start | bytes 1376264 | tf_op jit(solution)/shard_map/ppermute | solution.py:40
  93.6 0.2 convert_add_fusion
  93.9 2.7 %collective-permute-start.11 = (bf16[64,1792]{1,0:T(8,128)(2,1)S(1)}, bf16[64,1792]{1,0:T(8,128)(2,1)S(1)}, u32[]{:S(2)}, u32[]{:S(2)}) collective-permute-start(bf16[64,1792]{1,0:T(8,128)(2,1)S(1)} %fusion.5), channel_id=1, source_target_pairs={{0,8},{1,9},{2,10},{3,11},{4,12},{5,13},{6,14},{7,15},{8,0},{9,1},... | collective-permute-start | bytes 688136 | tf_op jit(solution)/shard_map/ppermute | solution.py:40
  96.5 4.4 %collective-permute-done.16 = bf16[2,64,1792]{2,1,0:T(8,128)(2,1)S(1)} collective-permute-done((bf16[2,64,1792]{2,1,0:T(8,128)(2,1)}, bf16[2,64,1792]{2,1,0:T(8,128)(2,1)S(1)}, u32[]{:S(2)}, u32[]{:S(2)}) %collective-permute-start.16) | collective-permute-done | bytes 458784 | tf_op jit(solution)/shard_map/ppermute | solution.py:40
  101.0 0.1 add_convert_fusion.1
  101.1 1.5 %collective-permute-start.17 = (bf16[64,1792]{1,0:T(8,128)(2,1)S(1)}, bf16[64,1792]{1,0:T(8,128)(2,1)S(1)}, u32[]{:S(2)}, u32[]{:S(2)}) collective-permute-start(bf16[64,1792]{1,0:T(8,128)(2,1)S(1)} %slice_bitcast_fusion.1), channel_id=1, source_target_pairs={{0,16},{1,17},{2,18},{3,19},{4,20},{5,21},{6,22},{7,23},{8,24},{9,... | collective-permute-start | bytes 688136 | tf_op jit(solution)/shard_map/ppermute | solution.py:40
  102.6 0.8 collective-permute-done.19
  103.4 0.1 add_convert_fusion
  103.5 0.8 collective-permute-start.20
  104.3 2.9 %collective-permute-done.17 = bf16[64,1792]{1,0:T(8,128)(2,1)S(1)} collective-permute-done((bf16[64,1792]{1,0:T(8,128)(2,1)S(1)}, bf16[64,1792]{1,0:T(8,128)(2,1)S(1)}, u32[]{:S(2)}, u32[]{:S(2)}) %collective-permute-start.17) | collective-permute-done | bytes 229408 | tf_op jit(solution)/shard_map/ppermute | solution.py:40
  107.2 0.1 fusion.4
  107.2 1.5 %collective-permute-start.18 = (bf16[64,1792]{1,0:T(8,128)(2,1)S(1)}, bf16[64,1792]{1,0:T(8,128)(2,1)S(1)}, u32[]{:S(2)}, u32[]{:S(2)}) collective-permute-start(bf16[64,1792]{1,0:T(8,128)(2,1)S(1)} %fusion.4), channel_id=1, source_target_pairs={{0,4},{1,5},{2,6},{3,7},{4,0},{5,1},{6,2},{7,3},{8,12},{9,13},{10,... | collective-permute-start | bytes 688136 | tf_op jit(solution)/shard_map/ppermute | solution.py:40
  108.8 0.8 collective-permute-done.20
  109.6 0.1 add_convert_fusion.2
  109.6 4.1 %collective-permute-start.21 = (bf16[64,1792]{1,0:T(8,128)(2,1)S(1)}, bf16[64,1792]{1,0:T(8,128)(2,1)S(1)}, u32[]{:S(2)}, u32[]{:S(2)}) collective-permute-start(bf16[64,1792]{1,0:T(8,128)(2,1)S(1)} %add_convert_fusion.2), channel_id=1, source_target_pairs={{0,12},{1,13},{2,14},{3,15},{4,8},{5,9},{6,10},{7,11},{8,4},{9,5},... | collective-permute-start | bytes 688136 | tf_op jit(solution)/shard_map/ppermute | solution.py:40
  113.7 2.1 %collective-permute-done.18 = bf16[64,1792]{1,0:T(8,128)(2,1)S(1)} collective-permute-done((bf16[64,1792]{1,0:T(8,128)(2,1)S(1)}, bf16[64,1792]{1,0:T(8,128)(2,1)S(1)}, u32[]{:S(2)}, u32[]{:S(2)}) %collective-permute-start.18) | collective-permute-done | bytes 229408 | tf_op jit(solution)/shard_map/ppermute | solution.py:40
  115.8 3.3 %collective-permute-done.21 = bf16[64,1792]{1,0:T(8,128)(2,1)S(1)} collective-permute-done((bf16[64,1792]{1,0:T(8,128)(2,1)S(1)}, bf16[64,1792]{1,0:T(8,128)(2,1)S(1)}, u32[]{:S(2)}, u32[]{:S(2)}) %collective-permute-start.21) | collective-permute-done | bytes 229408 | tf_op jit(solution)/shard_map/ppermute | solution.py:40
  119.1 0.8 fusion.3
  (40 shorter events, 0.3 us)
Async XLA Ops:
  0.0 9.0 %copy-start.2 = (bf16[32,2,3584]{2,1,0:T(2,128)(2,1)S(1)}, bf16[32,2,3584]{2,1,0:T(2,128)(2,1)}, u32[]{:S(2)}) copy-start(bf16[32,2,3584]{2,1,0:T(2,128)(2,1)} %param.14) | copy-start | bytes 1376260
  0.0 41.8 %collective-permute-start.6 = (bf16[2,2,3584,512]{3,2,1,0:T(8,128)(2,1)}, bf16[2,2,3584,512]{3,2,1,0:T(8,128)(2,1)}, u32[]{:S(2)}, u32[]{:S(2)}) collective-permute-start(bf16[2,2,3584,512]{3,2,1,0:T(8,128)(2,1)} %refs_7_.1), channel_id=1, source_target_pairs={{0,1},{1,0},{2,3},{3,2},{4,5},{5,4},{6,7},{7,6},{8,9},{9,8},{10,11... | collective-permute-start | bytes 44040200 | tf_op jit(solution)/shard_map/ppermute | solution.py:40
  0.5 41.4 %collective-permute-start.7 = (bf16[2,512,3584]{2,1,0:T(8,128)(2,1)}, bf16[2,512,3584]{2,1,0:T(8,128)(2,1)}, u32[]{:S(2)}, u32[]{:S(2)}) collective-permute-start(bf16[2,512,3584]{2,1,0:T(8,128)(2,1)} %refs_9_.3), channel_id=1, source_target_pairs={{0,1},{1,0},{2,3},{3,2},{4,5},{5,4},{6,7},{7,6},{8,9},{9,8},{10,11... | collective-permute-start | bytes 22020104 | tf_op jit(solution)/shard_map/ppermute | solution.py:40
  3.3 6.4 %copy-start = (bf16[64,3712]{1,0:T(8,128)(2,1)}, bf16[64,3712]{1,0:T(8,128)(2,1)S(1)}, u32[]{:S(2)}) copy-start(bf16[64,3712]{1,0:T(8,128)(2,1)S(1)} %concatenate.27.refs_1_) | copy-start | bytes 1425412
  3.3 16.6 %collective-permute-start.1 = (bf16[64,3712]{1,0:T(8,128)(2,1)S(1)}, bf16[64,3712]{1,0:T(8,128)(2,1)S(1)}, u32[]{:S(2)}, u32[]{:S(2)}) collective-permute-start(bf16[64,3712]{1,0:T(8,128)(2,1)S(1)} %concatenate.27.refs_1_), channel_id=1, source_target_pairs={{0,2},{1,3},{2,0},{3,1},{4,6},{5,7},{6,4},{7,5},{8,10},{9,11},{10,... | collective-permute-start | bytes 1425416 | tf_op jit(solution)/shard_map/ppermute | solution.py:40
  6.3 3.4 %copy-start.13 = (bf16[32,3584]{1,0:T(8,128)(2,1)S(1)}, bf16[32,3584]{1,0:T(8,128)(2,1)}, u32[]{:S(2)}) copy-start(bf16[32,3584]{1,0:T(8,128)(2,1)} %param.15) | copy-start | bytes 688132
  6.3 13.5 %collective-permute-start = (bf16[32,3712]{1,0:T(8,128)(2,1)S(1)}, bf16[32,3712]{1,0:T(8,128)(2,1)S(1)}, u32[]{:S(2)}, u32[]{:S(2)}) collective-permute-start(bf16[32,3712]{1,0:T(8,128)(2,1)S(1)} %constant_dynamic-slice_fusion), channel_id=1, source_target_pairs={{0,8},{1,9},{2,10},{3,11},{4,12},{5,13},{6,14},{7,15},{8,0},{9,1},... | collective-permute-start | bytes 712712 | tf_op jit(solution)/shard_map/ppermute | solution.py:40
  9.6 0.7 copy-start.14
  9.8 14.4 %collective-permute-start.5 = (bf16[96,3584]{1,0:T(8,128)(2,1)S(1)}, bf16[96,3584]{1,0:T(8,128)(2,1)S(1)}, u32[]{:S(2)}, u32[]{:S(2)}) collective-permute-start(bf16[96,3584]{1,0:T(8,128)(2,1)S(1)} %pad_maximum_fusion), channel_id=1, source_target_pairs={{0,1},{1,0},{2,3},{3,2},{4,5},{5,4},{6,7},{7,6},{8,9},{9,8},{10,11... | collective-permute-start | bytes 2064392 | tf_op jit(solution)/shard_map/ppermute | solution.py:40
  19.9 8.8 %copy-start.3 = (bf16[32,3712]{1,0:T(8,128)(2,1)}, bf16[32,3712]{1,0:T(8,128)(2,1)S(1)}, u32[]{:S(2)}) copy-start(bf16[32,3712]{1,0:T(8,128)(2,1)S(1)} %collective-permute-done.refs_2_) | copy-start | bytes 712708
  19.9 8.8 %copy-start.4 = (bf16[64,3712]{1,0:T(8,128)(2,1)}, bf16[64,3712]{1,0:T(8,128)(2,1)S(1)}, u32[]{:S(2)}) copy-start(bf16[64,3712]{1,0:T(8,128)(2,1)S(1)} %collective-permute-done.1.refs_4_) | copy-start | bytes 1425412
  19.9 7.2 %collective-permute-start.2 = (bf16[32,3712]{1,0:T(8,128)(2,1)S(1)}, bf16[32,3712]{1,0:T(8,128)(2,1)S(1)}, u32[]{:S(2)}, u32[]{:S(2)}) collective-permute-start(bf16[32,3712]{1,0:T(8,128)(2,1)S(1)} %collective-permute-done.refs_2_), channel_id=1, source_target_pairs={{0,16},{1,17},{2,18},{3,19},{4,20},{5,21},{6,22},{7,23},{8,24},{9,... | collective-permute-start | bytes 712712 | tf_op jit(solution)/shard_map/ppermute | solution.py:40
  21.5 16.8 %collective-permute-start.12 = (bf16[64,3712]{1,0:T(8,128)(2,1)S(1)}, bf16[64,3712]{1,0:T(8,128)(2,1)S(1)}, u32[]{:S(2)}, u32[]{:S(2)}) collective-permute-start(bf16[64,3712]{1,0:T(8,128)(2,1)S(1)} %pad_maximum_fusion.1), channel_id=1, source_target_pairs={{0,4},{1,5},{2,6},{3,7},{4,0},{5,1},{6,2},{7,3},{8,12},{9,13},{10,... | collective-permute-start | bytes 1425416 | tf_op jit(solution)/shard_map/ppermute | solution.py:40
  24.2 14.1 %collective-permute-start.3 = (bf16[32,3712]{1,0:T(8,128)(2,1)S(1)}, bf16[32,3712]{1,0:T(8,128)(2,1)S(1)}, u32[]{:S(2)}, u32[]{:S(2)}) collective-permute-start(bf16[32,3712]{1,0:T(8,128)(2,1)S(1)} %collective-permute-done.refs_2_), channel_id=1, source_target_pairs={{0,2},{1,3},{2,0},{3,1},{4,6},{5,7},{6,4},{7,5},{8,10},{9,11},{10,... | collective-permute-start | bytes 712712 | tf_op jit(solution)/shard_map/ppermute | solution.py:40
  27.1 1.4 %copy-start.11 = (bf16[32,3712]{1,0:T(8,128)(2,1)}, bf16[32,3712]{1,0:T(8,128)(2,1)S(1)}, u32[]{:S(2)}) copy-start(bf16[32,3712]{1,0:T(8,128)(2,1)S(1)} %collective-permute-done.2.refs_3_) | copy-start | bytes 712708
  27.1 11.2 %collective-permute-start.4 = (bf16[32,3712]{1,0:T(8,128)(2,1)S(1)}, bf16[32,3712]{1,0:T(8,128)(2,1)}, u32[]{:S(2)}, u32[]{:S(2)}) collective-permute-start(bf16[32,3712]{1,0:T(8,128)(2,1)S(1)} %collective-permute-done.refs_2_), channel_id=1, source_target_pairs={{0,18},{1,19},{2,16},{3,17},{4,22},{5,23},{6,20},{7,21},{8,26},{9,... | collective-permute-start | bytes 712712 | tf_op jit(solution)/shard_map/ppermute | solution.py:40
  38.3 3.6 %copy-start.12 = (bf16[32,3712]{1,0:T(8,128)(2,1)}, bf16[32,3712]{1,0:T(8,128)(2,1)S(1)}, u32[]{:S(2)}) copy-start(bf16[32,3712]{1,0:T(8,128)(2,1)S(1)} %collective-permute-done.3.refs_5_) | copy-start | bytes 712708
  38.3 25.3 %copy-start.5 = (bf16[64,3712]{1,0:T(8,128)(2,1)}, bf16[64,3712]{1,0:T(8,128)(2,1)S(1)}, u32[]{:S(2)}) copy-start(bf16[64,3712]{1,0:T(8,128)(2,1)S(1)} %collective-permute-done.12.refs_1_) | copy-start | bytes 1425412
  38.3 28.5 %collective-permute-start.13 = (bf16[64,3712]{1,0:T(8,128)(2,1)S(1)}, bf16[64,3712]{1,0:T(8,128)(2,1)S(1)}, u32[]{:S(2)}, u32[]{:S(2)}) collective-permute-start(bf16[64,3712]{1,0:T(8,128)(2,1)S(1)} %collective-permute-done.12.refs_1_), channel_id=1, source_target_pairs={{0,16},{1,17},{2,18},{3,19},{4,20},{5,21},{6,22},{7,23},{8,24},{9,... | collective-permute-start | bytes 1425416 | tf_op jit(solution)/shard_map/ppermute | solution.py:40
  40.1 27.0 %collective-permute-start.14 = (bf16[64,3712]{1,0:T(8,128)(2,1)S(1)}, bf16[64,3712]{1,0:T(8,128)(2,1)S(1)}, u32[]{:S(2)}, u32[]{:S(2)}) collective-permute-start(bf16[64,3712]{1,0:T(8,128)(2,1)S(1)} %collective-permute-done.12.refs_1_), channel_id=1, source_target_pairs={{0,2},{1,3},{2,0},{3,1},{4,6},{5,7},{6,4},{7,5},{8,10},{9,11},{10,... | collective-permute-start | bytes 1425416 | tf_op jit(solution)/shard_map/ppermute | solution.py:40
  41.6 25.5 %collective-permute-start.15 = (bf16[64,3712]{1,0:T(8,128)(2,1)S(1)}, bf16[64,3712]{1,0:T(8,128)(2,1)S(1)}, u32[]{:S(2)}, u32[]{:S(2)}) collective-permute-start(bf16[64,3712]{1,0:T(8,128)(2,1)S(1)} %collective-permute-done.12.refs_1_), channel_id=1, source_target_pairs={{0,18},{1,19},{2,16},{3,17},{4,22},{5,23},{6,20},{7,21},{8,26},{9,... | collective-permute-start | bytes 1425416 | tf_op jit(solution)/shard_map/ppermute | solution.py:40
  63.5 26.7 %collective-permute-start.10 = (bf16[2,64,1792]{2,1,0:T(8,128)(2,1)}, bf16[2,64,1792]{2,1,0:T(8,128)(2,1)S(1)}, u32[]{:S(2)}, u32[]{:S(2)}) collective-permute-start(bf16[2,64,1792]{2,1,0:T(8,128)(2,1)} %get-tuple-element.23), channel_id=1, source_target_pairs={{0,18},{1,19},{2,16},{3,17},{4,22},{5,23},{6,20},{7,21},{8,26},{9,... | collective-permute-start | bytes 1376264 | tf_op jit(solution)/shard_map/ppermute | solution.py:40
  66.3 24.0 %collective-permute-start.8 = (bf16[2,64,1792]{2,1,0:T(8,128)(2,1)}, bf16[2,64,1792]{2,1,0:T(8,128)(2,1)S(1)}, u32[]{:S(2)}, u32[]{:S(2)}) collective-permute-start(bf16[2,64,1792]{2,1,0:T(8,128)(2,1)} %get-tuple-element.21), channel_id=1, source_target_pairs={{0,16},{1,17},{2,18},{3,19},{4,20},{5,21},{6,22},{7,23},{8,24},{9,... | collective-permute-start | bytes 1376264 | tf_op jit(solution)/shard_map/ppermute | solution.py:40
  66.8 0.8 copy-start.6
  66.8 23.5 %collective-permute-start.9 = (bf16[2,64,1792]{2,1,0:T(8,128)(2,1)}, bf16[2,64,1792]{2,1,0:T(8,128)(2,1)S(1)}, u32[]{:S(2)}, u32[]{:S(2)}) collective-permute-start(bf16[2,64,1792]{2,1,0:T(8,128)(2,1)} %get-tuple-element.22), channel_id=1, source_target_pairs={{0,2},{1,3},{2,0},{3,1},{4,6},{5,7},{6,4},{7,5},{8,10},{9,11},{10,... | collective-permute-start | bytes 1376264 | tf_op jit(solution)/shard_map/ppermute | solution.py:40
  67.1 0.8 copy-start.7
  67.1 1.0 copy-start.8
  68.1 25.5 %copy-start.1 = (bf16[2,64,1792]{2,1,0:T(8,128)(2,1)S(1)}, bf16[2,64,1792]{2,1,0:T(8,128)(2,1)}, u32[]{:S(2)}) copy-start(bf16[2,64,1792]{2,1,0:T(8,128)(2,1)} %get-tuple-element.20.refs_11_) | copy-start | bytes 1376260
  90.3 10.7 %copy-start.10 = (bf16[2,64,1792]{2,1,0:T(8,128)(2,1)S(1)}, bf16[2,64,1792]{2,1,0:T(8,128)(2,1)}, u32[]{:S(2)}) copy-start(bf16[2,64,1792]{2,1,0:T(8,128)(2,1)} %get-tuple-element.29) | copy-start | bytes 1376260
  90.3 10.7 %collective-permute-start.16 = (bf16[2,64,1792]{2,1,0:T(8,128)(2,1)}, bf16[2,64,1792]{2,1,0:T(8,128)(2,1)S(1)}, u32[]{:S(2)}, u32[]{:S(2)}) collective-permute-start(bf16[2,64,1792]{2,1,0:T(8,128)(2,1)} %get-tuple-element.30), channel_id=1, source_target_pairs={{0,2},{1,3},{2,0},{3,1},{4,6},{5,7},{6,4},{7,5},{8,10},{9,11},{10,... | collective-permute-start | bytes 1376264 | tf_op jit(solution)/shard_map/ppermute | solution.py:40
  92.1 11.2 %collective-permute-start.19 = (bf16[128,1792]{1,0:T(8,128)(2,1)}, bf16[128,1792]{1,0:T(8,128)(2,1)S(1)}, u32[]{:S(2)}, u32[]{:S(2)}) collective-permute-start(bf16[128,1792]{1,0:T(8,128)(2,1)} %get-tuple-element.32), channel_id=1, source_target_pairs={{0,16},{1,17},{2,18},{3,19},{4,20},{5,21},{6,22},{7,23},{8,24},{9,... | collective-permute-start | bytes 1376264 | tf_op jit(solution)/shard_map/ppermute | solution.py:40
  93.8 9.5 %copy-start.9 = (bf16[128,1792]{1,0:T(8,128)(2,1)S(1)}, bf16[128,1792]{1,0:T(8,128)(2,1)}, u32[]{:S(2)}) copy-start(bf16[128,1792]{1,0:T(8,128)(2,1)} %get-tuple-element.31) | copy-start | bytes 1376260
  93.9 19.8 %collective-permute-start.11 = (bf16[64,1792]{1,0:T(8,128)(2,1)S(1)}, bf16[64,1792]{1,0:T(8,128)(2,1)S(1)}, u32[]{:S(2)}, u32[]{:S(2)}) collective-permute-start(bf16[64,1792]{1,0:T(8,128)(2,1)S(1)} %fusion.5), channel_id=1, source_target_pairs={{0,8},{1,9},{2,10},{3,11},{4,12},{5,13},{6,14},{7,15},{8,0},{9,1},... | collective-permute-start | bytes 688136 | tf_op jit(solution)/shard_map/ppermute | solution.py:40
  101.1 6.1 %collective-permute-start.17 = (bf16[64,1792]{1,0:T(8,128)(2,1)S(1)}, bf16[64,1792]{1,0:T(8,128)(2,1)S(1)}, u32[]{:S(2)}, u32[]{:S(2)}) collective-permute-start(bf16[64,1792]{1,0:T(8,128)(2,1)S(1)} %slice_bitcast_fusion.1), channel_id=1, source_target_pairs={{0,16},{1,17},{2,18},{3,19},{4,20},{5,21},{6,22},{7,23},{8,24},{9,... | collective-permute-start | bytes 688136 | tf_op jit(solution)/shard_map/ppermute | solution.py:40
  103.5 6.1 %collective-permute-start.20 = (bf16[64,1792]{1,0:T(8,128)(2,1)S(1)}, bf16[64,1792]{1,0:T(8,128)(2,1)S(1)}, u32[]{:S(2)}, u32[]{:S(2)}) collective-permute-start(bf16[64,1792]{1,0:T(8,128)(2,1)S(1)} %slice.52), channel_id=1, source_target_pairs={{0,2},{1,3},{2,0},{3,1},{4,6},{5,7},{6,4},{7,5},{8,10},{9,11},{10,... | collective-permute-start | bytes 688136 | tf_op jit(solution)/shard_map/ppermute | solution.py:40
  107.2 8.5 %collective-permute-start.18 = (bf16[64,1792]{1,0:T(8,128)(2,1)S(1)}, bf16[64,1792]{1,0:T(8,128)(2,1)S(1)}, u32[]{:S(2)}, u32[]{:S(2)}) collective-permute-start(bf16[64,1792]{1,0:T(8,128)(2,1)S(1)} %fusion.4), channel_id=1, source_target_pairs={{0,4},{1,5},{2,6},{3,7},{4,0},{5,1},{6,2},{7,3},{8,12},{9,13},{10,... | collective-permute-start | bytes 688136 | tf_op jit(solution)/shard_map/ppermute | solution.py:40
  109.6 9.5 %collective-permute-start.21 = (bf16[64,1792]{1,0:T(8,128)(2,1)S(1)}, bf16[64,1792]{1,0:T(8,128)(2,1)S(1)}, u32[]{:S(2)}, u32[]{:S(2)}) collective-permute-start(bf16[64,1792]{1,0:T(8,128)(2,1)S(1)} %add_convert_fusion.2), channel_id=1, source_target_pairs={{0,12},{1,13},{2,14},{3,15},{4,8},{5,9},{6,10},{7,11},{8,4},{9,5},... | collective-permute-start | bytes 688136 | tf_op jit(solution)/shard_map/ppermute | solution.py:40

commit v6 on v5

--- a/solution.py
+++ b/solution.py
@@ -236,7 +236,7 @@
 
     half = nz // 2
     held = lax.dynamic_slice_in_dim(wide, mx * part, part, axis=0)
-    own = [wide] + [hop(wide, 2 * j) for j in range(1, ny)]
+    own = [wide] + [hop(lax.optimization_barrier((wide, held))[0], 2 * j) for j in range(1, ny)]
     bits = [0]
     step = half
     while step > 1:
@@ -251,7 +251,7 @@
 
     near_units = spread(lax.optimization_barrier([held[part:]] + own[1:])[0])
     near = [u for j in range(ny) for u in near_units[j]]
-    far = lax.optimization_barrier([far] + near)[0]
+    far = lax.optimization_barrier([far, near[1]])[0]
     far_units = spread(far)
     chunks = [
         [u for j in range(ny) for u in [own[j]] + near_units[j]],
@@ -269,7 +269,7 @@
     tiles = hidden // hid_tile
     after = []
     for levels in (list(range(half)), list(range(half, nz))):
-        x_first = [k % 2 == 1 for k in levels] if levels[0] else None
+        x_first = [k % 2 == 0 for k in levels] if levels[0] else None
         chunk = chunks[levels[0] // half]
         n_rows = len(levels) * ny * tok_rows
         out_shape = []

time: 120 us -> 119 us (level)
  waiting for transfers between devices: 32.6 us -> 30.2 us
    ppermute x22, waiting for transfers between devices: 32.6 us -> 30.2 us  [hop(): lax.ppermute(x, ('dp', 'expert'), [(i, i ^ by_x * ne + by) for i in range...]
  transfers between devices with their start and end apart: 22 -> 22, of which waited for: 9 -> 9; matrix products, arithmetic and copies ran while one was open for 6% -> 7% of each run, Pallas kernels for 37% -> 37%
where the time goes in v6:
time: 119 us
  Pallas kernels  43.9 us (37%)
  starting transfers between devices  34.1 us (29%)
  waiting for transfers between devices  30.2 us (25%)
  local copies, waits for them, and re-layouts  6.31 us (5%)
  other arithmetic  4.15 us (3%)
    pallas_call x2, Pallas kernels, local(): pl.pallas_call(functools.partial(ffn_kernel, levels, x_first, nx, ny, tok...  43.9 us
    ppermute x22, starting transfers between devices, hop(): lax.ppermute(x, ('dp', 'expert'), [(i, i ^ by_x * ne + by) for i in range...  34.1 us
    ppermute x22, waiting for transfers between devices, hop(): lax.ppermute(x, ('dp', 'expert'), [(i, i ^ by_x * ne + by) for i in range...  30.2 us
  transfers between devices with their start and end apart: 22, of which 9 were waited for; matrix products, arithmetic and copies ran while one was open for 7% of the time, Pallas kernels for 37%

profile of v6, /device:TPU:0, one launch (start us, length us, event | category | flops | bytes accessed | tf_op | source)
XLA Modules:
  0.0 118.9 jit_solution(1206542322463896176)
XLA Ops:
  0.0 0.5 collective-permute-start.6
  0.5 0.1 collective-permute-start.7
  0.5 0.8 copy.27
  1.3 0.7 convert_element_type.76
  2.0 0.1 copy.31
  2.1 1.1 concatenate.27.refs_1_
  3.3 0.0 copy-start.12
  3.3 4.1 %collective-permute-start = (bf16[32,3712]{1,0:T(8,128)(2,1)S(1)}, bf16[32,3712]{1,0:T(8,128)(2,1)S(1)}, u32[]{:S(2)}, u32[]{:S(2)}) collective-permute-start(bf16[32,3712]{1,0:T(8,128)(2,1)S(1)} %constant_dynamic-slice_fusion), channel_id=1, source_target_pairs={{0,8},{1,9},{2,10},{3,11},{4,12},{5,13},{6,14},{7,15},{8,0},{9,1},... | collective-permute-start | bytes 712712 | tf_op jit(solution)/shard_map/ppermute | solution.py:40
  7.4 1.5 %collective-permute-start.1 = (bf16[64,3712]{1,0:T(8,128)(2,1)S(1)}, bf16[64,3712]{1,0:T(8,128)(2,1)S(1)}, u32[]{:S(2)}, u32[]{:S(2)}) collective-permute-start(bf16[64,3712]{1,0:T(8,128)(2,1)S(1)} %concatenate.27.refs_1_), channel_id=1, source_target_pairs={{0,2},{1,3},{2,0},{3,1},{4,6},{5,7},{6,4},{7,5},{8,10},{9,11},{10,... | collective-permute-start | bytes 1425416 | tf_op jit(solution)/shard_map/ppermute | solution.py:40
  8.9 0.6 fusion.11
  9.6 0.0 copy-start.13
  9.6 0.1 copy_bitcast_fusion
  9.7 0.1 collective-permute-start.5
  9.8 0.1 and_select_fusion.4
  9.9 0.3 copy-done.13
  10.2 0.2 select_reduce_fusion
  10.4 0.6 and_select_fusion.refs_0_
  11.0 7.5 %collective-permute-done.refs_2_ = bf16[32,3712]{1,0:T(8,128)(2,1)S(1)} collective-permute-done((bf16[32,3712]{1,0:T(8,128)(2,1)S(1)}, bf16[32,3712]{1,0:T(8,128)(2,1)S(1)}, u32[]{:S(2)}, u32[]{:S(2)}) %collective-permute-start) | collective-permute-done | bytes 237600 | tf_op jit(solution)/shard_map/ppermute | solution.py:40
  18.5 1.5 %collective-permute-done.1.refs_4_ = bf16[64,3712]{1,0:T(8,128)(2,1)S(1)} collective-permute-done((bf16[64,3712]{1,0:T(8,128)(2,1)S(1)}, bf16[64,3712]{1,0:T(8,128)(2,1)S(1)}, u32[]{:S(2)}, u32[]{:S(2)}) %collective-permute-start.1) | collective-permute-done | bytes 475168 | tf_op jit(solution)/shard_map/ppermute | solution.py:40
  20.0 1.5 %collective-permute-start.2 = (bf16[32,3712]{1,0:T(8,128)(2,1)S(1)}, bf16[32,3712]{1,0:T(8,128)(2,1)S(1)}, u32[]{:S(2)}, u32[]{:S(2)}) collective-permute-start(bf16[32,3712]{1,0:T(8,128)(2,1)S(1)} %collective-permute-done.refs_2_), channel_id=1, source_target_pairs={{0,16},{1,17},{2,18},{3,19},{4,20},{5,21},{6,22},{7,23},{8,24},{9,... | collective-permute-start | bytes 712712 | tf_op jit(solution)/shard_map/ppermute | solution.py:40
  21.5 1.6 %collective-permute-start.12 = (bf16[64,3712]{1,0:T(8,128)(2,1)S(1)}, bf16[64,3712]{1,0:T(8,128)(2,1)S(1)}, u32[]{:S(2)}, u32[]{:S(2)}) collective-permute-start(bf16[64,3712]{1,0:T(8,128)(2,1)S(1)} %pad_maximum_fusion.1), channel_id=1, source_target_pairs={{0,4},{1,5},{2,6},{3,7},{4,0},{5,1},{6,2},{7,3},{8,12},{9,13},{10,... | collective-permute-start | bytes 1425416 | tf_op jit(solution)/shard_map/ppermute | solution.py:40
  23.1 1.1 collective-permute-done.5
  24.2 2.9 %collective-permute-start.3 = (bf16[32,3712]{1,0:T(8,128)(2,1)S(1)}, bf16[32,3712]{1,0:T(8,128)(2,1)}, u32[]{:S(2)}, u32[]{:S(2)}) collective-permute-start(bf16[32,3712]{1,0:T(8,128)(2,1)S(1)} %collective-permute-done.refs_2_), channel_id=1, source_target_pairs={{0,2},{1,3},{2,0},{3,1},{4,6},{5,7},{6,4},{7,5},{8,10},{9,11},{10,... | collective-permute-start | bytes 712712 | tf_op jit(solution)/shard_map/ppermute | solution.py:40
  27.1 1.9 %collective-permute-start.4 = (bf16[32,3712]{1,0:T(8,128)(2,1)S(1)}, bf16[32,3712]{1,0:T(8,128)(2,1)}, u32[]{:S(2)}, u32[]{:S(2)}) collective-permute-start(bf16[32,3712]{1,0:T(8,128)(2,1)S(1)} %collective-permute-done.refs_2_), channel_id=1, source_target_pairs={{0,18},{1,19},{2,16},{3,17},{4,22},{5,23},{6,20},{7,21},{8,26},{9,... | collective-permute-start | bytes 712712 | tf_op jit(solution)/shard_map/ppermute | solution.py:40
  29.0 0.1 maximum_bitcast_fusion
  29.2 0.1 slice.45
  29.2 0.8 slice.46
  30.1 1.3 %copy.34 = bf16[128,3584]{0,1:T(8,128)(2,1)} copy(bf16[128,3584]{1,0:T(8,128)(2,1)S(1)} %bitcast.34) | data formatting | bytes 1835008 | tf_op jit(solution)/shard_map/reshape | solution.py:229
  31.3 1.6 %collective-permute-done.12.refs_1_ = bf16[64,3712]{1,0:T(8,128)(2,1)S(1)} collective-permute-done((bf16[64,3712]{1,0:T(8,128)(2,1)S(1)}, bf16[64,3712]{1,0:T(8,128)(2,1)S(1)}, u32[]{:S(2)}, u32[]{:S(2)}) %collective-permute-start.12) | collective-permute-done | bytes 475168 | tf_op jit(solution)/shard_map/ppermute | solution.py:40
  33.0 0.5 collective-permute-start.13
  33.5 4.9 %collective-permute-done.3.refs_5_ = bf16[32,3712]{1,0:T(8,128)(2,1)} collective-permute-done((bf16[32,3712]{1,0:T(8,128)(2,1)S(1)}, bf16[32,3712]{1,0:T(8,128)(2,1)}, u32[]{:S(2)}, u32[]{:S(2)}) %collective-permute-start.3) | collective-permute-done | bytes 237600 | tf_op jit(solution)/shard_map/ppermute | solution.py:40
  38.4 1.7 %collective-permute-start.14 = (bf16[64,3712]{1,0:T(8,128)(2,1)S(1)}, bf16[64,3712]{1,0:T(8,128)(2,1)S(1)}, u32[]{:S(2)}, u32[]{:S(2)}) collective-permute-start(bf16[64,3712]{1,0:T(8,128)(2,1)S(1)} %collective-permute-done.12.refs_1_), channel_id=1, source_target_pairs={{0,2},{1,3},{2,0},{3,1},{4,6},{5,7},{6,4},{7,5},{8,10},{9,11},{10,... | collective-permute-start | bytes 1425416 | tf_op jit(solution)/shard_map/ppermute | solution.py:40
  40.1 0.0 collective-permute-done.4.refs_6_
  40.1 1.4 %collective-permute-start.15 = (bf16[64,3712]{1,0:T(8,128)(2,1)S(1)}, bf16[64,3712]{1,0:T(8,128)(2,1)S(1)}, u32[]{:S(2)}, u32[]{:S(2)}) collective-permute-start(bf16[64,3712]{1,0:T(8,128)(2,1)S(1)} %collective-permute-done.12.refs_1_), channel_id=1, source_target_pairs={{0,18},{1,19},{2,16},{3,17},{4,22},{5,23},{6,20},{7,21},{8,26},{9,... | collective-permute-start | bytes 1425416 | tf_op jit(solution)/shard_map/ppermute | solution.py:40
  41.5 0.0 collective-permute-done.7.refs_12_.refs_10_
  41.6 0.0 collective-permute-done.6.refs_10_.refs_8_
  41.6 21.7 %shard_map.82 = (bf16[2,64,1792]{2,1,0:T(8,128)(2,1)}, bf16[2,64,1792]{2,1,0:T(8,128)(2,1)}, bf16[2,64,1792]{2,1,0:T(8,128)(2,1)}, bf16[2,64,1792]{2,1,0:T(8,128)(2,1)}) custom-call(s32[4]{0:T(128)} %and_select_fusion.refs_0_, bf16[64,3712]{1,0:T(8,128)(2,1)} %copy-done, bf16[32,3712]{1,0:T(8,128)(2,1)} %copy-done.3, bf16[32,3712]{1,0:T(8,128)(2,1)} %copy-done.11, ...), custom_call_target="tpu_custom_call" | custom-call | flops 11626610688 | bytes 49545216 | tf_op jit(solution)/shard_map/pallas_call | solution.py:284
  63.3 1.6 %collective-permute-start.10 = (bf16[2,64,1792]{2,1,0:T(8,128)(2,1)}, bf16[2,64,1792]{2,1,0:T(8,128)(2,1)S(1)}, u32[]{:S(2)}, u32[]{:S(2)}) collective-permute-start(bf16[2,64,1792]{2,1,0:T(8,128)(2,1)} %get-tuple-element.25), channel_id=1, source_target_pairs={{0,18},{1,19},{2,16},{3,17},{4,22},{5,23},{6,20},{7,21},{8,26},{9,... | collective-permute-start | bytes 1376264 | tf_op jit(solution)/shard_map/ppermute | solution.py:40
  64.8 1.5 %collective-permute-start.8 = (bf16[2,64,1792]{2,1,0:T(8,128)(2,1)}, bf16[2,64,1792]{2,1,0:T(8,128)(2,1)S(1)}, u32[]{:S(2)}, u32[]{:S(2)}) collective-permute-start(bf16[2,64,1792]{2,1,0:T(8,128)(2,1)} %get-tuple-element.23), channel_id=1, source_target_pairs={{0,16},{1,17},{2,18},{3,19},{4,20},{5,21},{6,22},{7,23},{8,24},{9,... | collective-permute-start | bytes 1376264 | tf_op jit(solution)/shard_map/ppermute | solution.py:40
  66.3 0.0 collective-permute-done.13.refs_2_
  66.3 0.5 collective-permute-start.9
  66.8 0.0 collective-permute-done.14.refs_3_
  66.8 0.3 copy-done.6
  67.1 0.5 copy-done.7
  67.6 0.2 copy-done.8
  67.8 22.2 %shard_map.83 = (bf16[128,1792]{1,0:T(8,128)(2,1)}, bf16[128,1792]{1,0:T(8,128)(2,1)}, bf16[2,64,1792]{2,1,0:T(8,128)(2,1)}, bf16[2,64,1792]{2,1,0:T(8,128)(2,1)}) custom-call(s32[4]{0:T(128)} %and_select_fusion.refs_0_, bf16[64,3712]{1,0:T(8,128)(2,1)} %copy-done.5, bf16[64,3712]{1,0:T(8,128)(2,1)} %copy-done.6, bf16[64,3712]{1,0:T(8,128)(2,1)} %copy-done.7, ...), custom_call_target="tpu_custom_call" | custom-call | flops 11626610688 | bytes 49545216 | tf_op jit(solution)/shard_map/pallas_call | solution.py:284
  90.1 0.4 collective-permute-start.16
  90.4 1.7 %collective-permute-start.19 = (bf16[2,64,1792]{2,1,0:T(8,128)(2,1)}, bf16[2,64,1792]{2,1,0:T(8,128)(2,1)S(1)}, u32[]{:S(2)}, u32[]{:S(2)}) collective-permute-start(bf16[2,64,1792]{2,1,0:T(8,128)(2,1)} %get-tuple-element.34), channel_id=1, source_target_pairs={{0,2},{1,3},{2,0},{3,1},{4,6},{5,7},{6,4},{7,5},{8,10},{9,11},{10,... | collective-permute-start | bytes 1376264 | tf_op jit(solution)/shard_map/ppermute | solution.py:40
  92.2 1.2 %convert_add_fusion = f32[2,64,1792]{2,1,0:T(8,128)S(1)} fusion(bf16[2,64,1792]{2,1,0:T(8,128)(2,1)S(1)} %collective-permute-done.10, bf16[2,64,1792]{2,1,0:T(8,128)(2,1)} %collective-permute-done.9, bf16[2,64,1792]{2,1,0:T(8,128)(2,1)S(1)} %collective-permute-done.8, bf16[2,64,1792]{2,1,0:T(8,128)(2,1)S(1)} %copy-done.1), kind=kLoop, calls=%fused_computation.3 | loop fusion | flops 1605632 | bytes 2752512 | tf_op jit(solution)/shard_map/add | solution.py:264
  93.5 2.6 %collective-permute-start.11 = (bf16[64,1792]{1,0:T(8,128)(2,1)S(1)}, bf16[64,1792]{1,0:T(8,128)(2,1)S(1)}, u32[]{:S(2)}, u32[]{:S(2)}) collective-permute-start(bf16[64,1792]{1,0:T(8,128)(2,1)S(1)} %fusion.5), channel_id=1, source_target_pairs={{0,8},{1,9},{2,10},{3,11},{4,12},{5,13},{6,14},{7,15},{8,0},{9,1},... | collective-permute-start | bytes 688136 | tf_op jit(solution)/shard_map/ppermute | solution.py:40
  96.1 4.6 %collective-permute-done.16 = bf16[128,1792]{1,0:T(8,128)(2,1)S(1)} collective-permute-done((bf16[128,1792]{1,0:T(8,128)(2,1)}, bf16[128,1792]{1,0:T(8,128)(2,1)S(1)}, u32[]{:S(2)}, u32[]{:S(2)}) %collective-permute-start.16) | collective-permute-done | bytes 458784 | tf_op jit(solution)/shard_map/ppermute | solution.py:40
  100.7 0.1 add_convert_fusion.1
  100.8 1.6 %collective-permute-start.17 = (bf16[64,1792]{1,0:T(8,128)(2,1)S(1)}, bf16[64,1792]{1,0:T(8,128)(2,1)S(1)}, u32[]{:S(2)}, u32[]{:S(2)}) collective-permute-start(bf16[64,1792]{1,0:T(8,128)(2,1)S(1)} %slice.50), channel_id=1, source_target_pairs={{0,2},{1,3},{2,0},{3,1},{4,6},{5,7},{6,4},{7,5},{8,10},{9,11},{10,... | collective-permute-start | bytes 688136 | tf_op jit(solution)/shard_map/ppermute | solution.py:40
  102.4 0.1 add_convert_fusion
  102.5 1.0 collective-permute-start.20
  103.6 3.3 %collective-permute-done.17 = bf16[64,1792]{1,0:T(8,128)(2,1)S(1)} collective-permute-done((bf16[64,1792]{1,0:T(8,128)(2,1)S(1)}, bf16[64,1792]{1,0:T(8,128)(2,1)S(1)}, u32[]{:S(2)}, u32[]{:S(2)}) %collective-permute-start.17) | collective-permute-done | bytes 229408 | tf_op jit(solution)/shard_map/ppermute | solution.py:40
  106.9 0.1 add_convert_fusion.2
  106.9 1.6 %collective-permute-start.18 = (bf16[64,1792]{1,0:T(8,128)(2,1)S(1)}, bf16[64,1792]{1,0:T(8,128)(2,1)S(1)}, u32[]{:S(2)}, u32[]{:S(2)}) collective-permute-start(bf16[64,1792]{1,0:T(8,128)(2,1)S(1)} %add_convert_fusion.2), channel_id=1, source_target_pairs={{0,4},{1,5},{2,6},{3,7},{4,0},{5,1},{6,2},{7,3},{8,12},{9,13},{10,... | collective-permute-start | bytes 688136 | tf_op jit(solution)/shard_map/ppermute | solution.py:40
  108.6 0.0 collective-permute-done.20
  108.6 0.1 fusion.4
  108.7 3.7 %collective-permute-start.21 = (bf16[64,1792]{1,0:T(8,128)(2,1)S(1)}, bf16[64,1792]{1,0:T(8,128)(2,1)S(1)}, u32[]{:S(2)}, u32[]{:S(2)}) collective-permute-start(bf16[64,1792]{1,0:T(8,128)(2,1)S(1)} %fusion.4), channel_id=1, source_target_pairs={{0,12},{1,13},{2,14},{3,15},{4,8},{5,9},{6,10},{7,11},{8,4},{9,5},... | collective-permute-start | bytes 688136 | tf_op jit(solution)/shard_map/ppermute | solution.py:40
  112.3 3.1 %collective-permute-done.18 = bf16[64,1792]{1,0:T(8,128)(2,1)S(1)} collective-permute-done((bf16[64,1792]{1,0:T(8,128)(2,1)S(1)}, bf16[64,1792]{1,0:T(8,128)(2,1)S(1)}, u32[]{:S(2)}, u32[]{:S(2)}) %collective-permute-start.18) | collective-permute-done | bytes 229408 | tf_op jit(solution)/shard_map/ppermute | solution.py:40
  115.5 2.6 %collective-permute-done.21 = bf16[64,1792]{1,0:T(8,128)(2,1)S(1)} collective-permute-done((bf16[64,1792]{1,0:T(8,128)(2,1)S(1)}, bf16[64,1792]{1,0:T(8,128)(2,1)S(1)}, u32[]{:S(2)}, u32[]{:S(2)}) %collective-permute-start.21) | collective-permute-done | bytes 229408 | tf_op jit(solution)/shard_map/ppermute | solution.py:40
  118.1 0.8 fusion.3
  (38 shorter events, 0.3 us)
Async XLA Ops:
  0.0 8.9 %copy-start.2 = (bf16[32,2,3584]{2,1,0:T(2,128)(2,1)S(1)}, bf16[32,2,3584]{2,1,0:T(2,128)(2,1)}, u32[]{:S(2)}) copy-start(bf16[32,2,3584]{2,1,0:T(2,128)(2,1)} %param.14) | copy-start | bytes 1376260
  0.0 41.6 %collective-permute-start.6 = (bf16[2,2,3584,512]{3,2,1,0:T(8,128)(2,1)}, bf16[2,2,3584,512]{3,2,1,0:T(8,128)(2,1)}, u32[]{:S(2)}, u32[]{:S(2)}) collective-permute-start(bf16[2,2,3584,512]{3,2,1,0:T(8,128)(2,1)} %refs_7_.1), channel_id=1, source_target_pairs={{0,1},{1,0},{2,3},{3,2},{4,5},{5,4},{6,7},{7,6},{8,9},{9,8},{10,11... | collective-permute-start | bytes 44040200 | tf_op jit(solution)/shard_map/ppermute | solution.py:40
  0.5 41.1 %collective-permute-start.7 = (bf16[2,512,3584]{2,1,0:T(8,128)(2,1)}, bf16[2,512,3584]{2,1,0:T(8,128)(2,1)}, u32[]{:S(2)}, u32[]{:S(2)}) collective-permute-start(bf16[2,512,3584]{2,1,0:T(8,128)(2,1)} %refs_9_.3), channel_id=1, source_target_pairs={{0,1},{1,0},{2,3},{3,2},{4,5},{5,4},{6,7},{7,6},{8,9},{9,8},{10,11... | collective-permute-start | bytes 22020104 | tf_op jit(solution)/shard_map/ppermute | solution.py:40
  3.3 6.4 %copy-start = (bf16[64,3712]{1,0:T(8,128)(2,1)}, bf16[64,3712]{1,0:T(8,128)(2,1)S(1)}, u32[]{:S(2)}) copy-start(bf16[64,3712]{1,0:T(8,128)(2,1)S(1)} %concatenate.27.refs_1_) | copy-start | bytes 1425412
  3.3 6.4 %copy-start.12 = (bf16[32,3584]{1,0:T(8,128)(2,1)S(1)}, bf16[32,3584]{1,0:T(8,128)(2,1)}, u32[]{:S(2)}) copy-start(bf16[32,3584]{1,0:T(8,128)(2,1)} %param.15) | copy-start | bytes 688132
  3.3 15.2 %collective-permute-start = (bf16[32,3712]{1,0:T(8,128)(2,1)S(1)}, bf16[32,3712]{1,0:T(8,128)(2,1)S(1)}, u32[]{:S(2)}, u32[]{:S(2)}) collective-permute-start(bf16[32,3712]{1,0:T(8,128)(2,1)S(1)} %constant_dynamic-slice_fusion), channel_id=1, source_target_pairs={{0,8},{1,9},{2,10},{3,11},{4,12},{5,13},{6,14},{7,15},{8,0},{9,1},... | collective-permute-start | bytes 712712 | tf_op jit(solution)/shard_map/ppermute | solution.py:40
  7.4 12.6 %collective-permute-start.1 = (bf16[64,3712]{1,0:T(8,128)(2,1)S(1)}, bf16[64,3712]{1,0:T(8,128)(2,1)S(1)}, u32[]{:S(2)}, u32[]{:S(2)}) collective-permute-start(bf16[64,3712]{1,0:T(8,128)(2,1)S(1)} %concatenate.27.refs_1_), channel_id=1, source_target_pairs={{0,2},{1,3},{2,0},{3,1},{4,6},{5,7},{6,4},{7,5},{8,10},{9,11},{10,... | collective-permute-start | bytes 1425416 | tf_op jit(solution)/shard_map/ppermute | solution.py:40
  9.6 0.7 copy-start.13
  9.7 14.5 %collective-permute-start.5 = (bf16[96,3584]{1,0:T(8,128)(2,1)S(1)}, bf16[96,3584]{1,0:T(8,128)(2,1)S(1)}, u32[]{:S(2)}, u32[]{:S(2)}) collective-permute-start(bf16[96,3584]{1,0:T(8,128)(2,1)S(1)} %pad_maximum_fusion), channel_id=1, source_target_pairs={{0,1},{1,0},{2,3},{3,2},{4,5},{5,4},{6,7},{7,6},{8,9},{9,8},{10,11... | collective-permute-start | bytes 2064392 | tf_op jit(solution)/shard_map/ppermute | solution.py:40
  18.5 10.6 %copy-start.3 = (bf16[32,3712]{1,0:T(8,128)(2,1)}, bf16[32,3712]{1,0:T(8,128)(2,1)S(1)}, u32[]{:S(2)}) copy-start(bf16[32,3712]{1,0:T(8,128)(2,1)S(1)} %collective-permute-done.refs_2_) | copy-start | bytes 712708
  20.0 9.2 %copy-start.4 = (bf16[64,3712]{1,0:T(8,128)(2,1)}, bf16[64,3712]{1,0:T(8,128)(2,1)S(1)}, u32[]{:S(2)}) copy-start(bf16[64,3712]{1,0:T(8,128)(2,1)S(1)} %collective-permute-done.1.refs_4_) | copy-start | bytes 1425412
  20.0 7.1 %collective-permute-start.2 = (bf16[32,3712]{1,0:T(8,128)(2,1)S(1)}, bf16[32,3712]{1,0:T(8,128)(2,1)S(1)}, u32[]{:S(2)}, u32[]{:S(2)}) collective-permute-start(bf16[32,3712]{1,0:T(8,128)(2,1)S(1)} %collective-permute-done.refs_2_), channel_id=1, source_target_pairs={{0,16},{1,17},{2,18},{3,19},{4,20},{5,21},{6,22},{7,23},{8,24},{9,... | collective-permute-start | bytes 712712 | tf_op jit(solution)/shard_map/ppermute | solution.py:40
  21.5 11.5 %collective-permute-start.12 = (bf16[64,3712]{1,0:T(8,128)(2,1)S(1)}, bf16[64,3712]{1,0:T(8,128)(2,1)S(1)}, u32[]{:S(2)}, u32[]{:S(2)}) collective-permute-start(bf16[64,3712]{1,0:T(8,128)(2,1)S(1)} %pad_maximum_fusion.1), channel_id=1, source_target_pairs={{0,4},{1,5},{2,6},{3,7},{4,0},{5,1},{6,2},{7,3},{8,12},{9,13},{10,... | collective-permute-start | bytes 1425416 | tf_op jit(solution)/shard_map/ppermute | solution.py:40
  24.2 14.2 %collective-permute-start.3 = (bf16[32,3712]{1,0:T(8,128)(2,1)S(1)}, bf16[32,3712]{1,0:T(8,128)(2,1)}, u32[]{:S(2)}, u32[]{:S(2)}) collective-permute-start(bf16[32,3712]{1,0:T(8,128)(2,1)S(1)} %collective-permute-done.refs_2_), channel_id=1, source_target_pairs={{0,2},{1,3},{2,0},{3,1},{4,6},{5,7},{6,4},{7,5},{8,10},{9,11},{10,... | collective-permute-start | bytes 712712 | tf_op jit(solution)/shard_map/ppermute | solution.py:40
  27.1 1.9 %copy-start.11 = (bf16[32,3712]{1,0:T(8,128)(2,1)}, bf16[32,3712]{1,0:T(8,128)(2,1)S(1)}, u32[]{:S(2)}) copy-start(bf16[32,3712]{1,0:T(8,128)(2,1)S(1)} %collective-permute-done.2.refs_3_) | copy-start | bytes 712708
  27.1 13.0 %collective-permute-start.4 = (bf16[32,3712]{1,0:T(8,128)(2,1)S(1)}, bf16[32,3712]{1,0:T(8,128)(2,1)}, u32[]{:S(2)}, u32[]{:S(2)}) collective-permute-start(bf16[32,3712]{1,0:T(8,128)(2,1)S(1)} %collective-permute-done.refs_2_), channel_id=1, source_target_pairs={{0,18},{1,19},{2,16},{3,17},{4,22},{5,23},{6,20},{7,21},{8,26},{9,... | collective-permute-start | bytes 712712 | tf_op jit(solution)/shard_map/ppermute | solution.py:40
  33.0 30.3 %copy-start.5 = (bf16[64,3712]{1,0:T(8,128)(2,1)}, bf16[64,3712]{1,0:T(8,128)(2,1)S(1)}, u32[]{:S(2)}) copy-start(bf16[64,3712]{1,0:T(8,128)(2,1)S(1)} %collective-permute-done.12.refs_1_) | copy-start | bytes 1425412
  33.0 33.3 %collective-permute-start.13 = (bf16[64,3712]{1,0:T(8,128)(2,1)S(1)}, bf16[64,3712]{1,0:T(8,128)(2,1)S(1)}, u32[]{:S(2)}, u32[]{:S(2)}) collective-permute-start(bf16[64,3712]{1,0:T(8,128)(2,1)S(1)} %collective-permute-done.12.refs_1_), channel_id=1, source_target_pairs={{0,16},{1,17},{2,18},{3,19},{4,20},{5,21},{6,22},{7,23},{8,24},{9,... | collective-permute-start | bytes 1425416 | tf_op jit(solution)/shard_map/ppermute | solution.py:40
  38.4 28.5 %collective-permute-start.14 = (bf16[64,3712]{1,0:T(8,128)(2,1)S(1)}, bf16[64,3712]{1,0:T(8,128)(2,1)S(1)}, u32[]{:S(2)}, u32[]{:S(2)}) collective-permute-start(bf16[64,3712]{1,0:T(8,128)(2,1)S(1)} %collective-permute-done.12.refs_1_), channel_id=1, source_target_pairs={{0,2},{1,3},{2,0},{3,1},{4,6},{5,7},{6,4},{7,5},{8,10},{9,11},{10,... | collective-permute-start | bytes 1425416 | tf_op jit(solution)/shard_map/ppermute | solution.py:40
  40.1 26.7 %collective-permute-start.15 = (bf16[64,3712]{1,0:T(8,128)(2,1)S(1)}, bf16[64,3712]{1,0:T(8,128)(2,1)S(1)}, u32[]{:S(2)}, u32[]{:S(2)}) collective-permute-start(bf16[64,3712]{1,0:T(8,128)(2,1)S(1)} %collective-permute-done.12.refs_1_), channel_id=1, source_target_pairs={{0,18},{1,19},{2,16},{3,17},{4,22},{5,23},{6,20},{7,21},{8,26},{9,... | collective-permute-start | bytes 1425416 | tf_op jit(solution)/shard_map/ppermute | solution.py:40
  63.3 26.8 %collective-permute-start.10 = (bf16[2,64,1792]{2,1,0:T(8,128)(2,1)}, bf16[2,64,1792]{2,1,0:T(8,128)(2,1)S(1)}, u32[]{:S(2)}, u32[]{:S(2)}) collective-permute-start(bf16[2,64,1792]{2,1,0:T(8,128)(2,1)} %get-tuple-element.25), channel_id=1, source_target_pairs={{0,18},{1,19},{2,16},{3,17},{4,22},{5,23},{6,20},{7,21},{8,26},{9,... | collective-permute-start | bytes 1376264 | tf_op jit(solution)/shard_map/ppermute | solution.py:40
  64.8 25.2 %collective-permute-start.8 = (bf16[2,64,1792]{2,1,0:T(8,128)(2,1)}, bf16[2,64,1792]{2,1,0:T(8,128)(2,1)S(1)}, u32[]{:S(2)}, u32[]{:S(2)}) collective-permute-start(bf16[2,64,1792]{2,1,0:T(8,128)(2,1)} %get-tuple-element.23), channel_id=1, source_target_pairs={{0,16},{1,17},{2,18},{3,19},{4,20},{5,21},{6,22},{7,23},{8,24},{9,... | collective-permute-start | bytes 1376264 | tf_op jit(solution)/shard_map/ppermute | solution.py:40
  66.3 0.8 copy-start.6
  66.3 23.7 %collective-permute-start.9 = (bf16[2,64,1792]{2,1,0:T(8,128)(2,1)}, bf16[2,64,1792]{2,1,0:T(8,128)(2,1)}, u32[]{:S(2)}, u32[]{:S(2)}) collective-permute-start(bf16[2,64,1792]{2,1,0:T(8,128)(2,1)} %get-tuple-element.24), channel_id=1, source_target_pairs={{0,2},{1,3},{2,0},{3,1},{4,6},{5,7},{6,4},{7,5},{8,10},{9,11},{10,... | collective-permute-start | bytes 1376264 | tf_op jit(solution)/shard_map/ppermute | solution.py:40
  66.8 0.8 copy-start.7
  66.8 1.0 copy-start.8
  67.8 24.3 %copy-start.1 = (bf16[2,64,1792]{2,1,0:T(8,128)(2,1)S(1)}, bf16[2,64,1792]{2,1,0:T(8,128)(2,1)}, u32[]{:S(2)}) copy-start(bf16[2,64,1792]{2,1,0:T(8,128)(2,1)} %get-tuple-element.22.refs_11_) | copy-start | bytes 1376260
  90.0 10.6 %copy-start.10 = (bf16[128,1792]{1,0:T(8,128)(2,1)S(1)}, bf16[128,1792]{1,0:T(8,128)(2,1)}, u32[]{:S(2)}) copy-start(bf16[128,1792]{1,0:T(8,128)(2,1)} %get-tuple-element.31) | copy-start | bytes 1376260
  90.1 10.6 %collective-permute-start.16 = (bf16[128,1792]{1,0:T(8,128)(2,1)}, bf16[128,1792]{1,0:T(8,128)(2,1)S(1)}, u32[]{:S(2)}, u32[]{:S(2)}) collective-permute-start(bf16[128,1792]{1,0:T(8,128)(2,1)} %get-tuple-element.32), channel_id=1, source_target_pairs={{0,16},{1,17},{2,18},{3,19},{4,20},{5,21},{6,22},{7,23},{8,24},{9,... | collective-permute-start | bytes 1376264 | tf_op jit(solution)/shard_map/ppermute | solution.py:40
  90.4 12.0 %collective-permute-start.19 = (bf16[2,64,1792]{2,1,0:T(8,128)(2,1)}, bf16[2,64,1792]{2,1,0:T(8,128)(2,1)S(1)}, u32[]{:S(2)}, u32[]{:S(2)}) collective-permute-start(bf16[2,64,1792]{2,1,0:T(8,128)(2,1)} %get-tuple-element.34), channel_id=1, source_target_pairs={{0,2},{1,3},{2,0},{3,1},{4,6},{5,7},{6,4},{7,5},{8,10},{9,11},{10,... | collective-permute-start | bytes 1376264 | tf_op jit(solution)/shard_map/ppermute | solution.py:40
  93.4 9.0 %copy-start.9 = (bf16[2,64,1792]{2,1,0:T(8,128)(2,1)S(1)}, bf16[2,64,1792]{2,1,0:T(8,128)(2,1)}, u32[]{:S(2)}) copy-start(bf16[2,64,1792]{2,1,0:T(8,128)(2,1)} %get-tuple-element.33) | copy-start | bytes 1376260
  93.5 18.9 %collective-permute-start.11 = (bf16[64,1792]{1,0:T(8,128)(2,1)S(1)}, bf16[64,1792]{1,0:T(8,128)(2,1)S(1)}, u32[]{:S(2)}, u32[]{:S(2)}) collective-permute-start(bf16[64,1792]{1,0:T(8,128)(2,1)S(1)} %fusion.5), channel_id=1, source_target_pairs={{0,8},{1,9},{2,10},{3,11},{4,12},{5,13},{6,14},{7,15},{8,0},{9,1},... | collective-permute-start | bytes 688136 | tf_op jit(solution)/shard_map/ppermute | solution.py:40
  100.8 6.1 %collective-permute-start.17 = (bf16[64,1792]{1,0:T(8,128)(2,1)S(1)}, bf16[64,1792]{1,0:T(8,128)(2,1)S(1)}, u32[]{:S(2)}, u32[]{:S(2)}) collective-permute-start(bf16[64,1792]{1,0:T(8,128)(2,1)S(1)} %slice.50), channel_id=1, source_target_pairs={{0,2},{1,3},{2,0},{3,1},{4,6},{5,7},{6,4},{7,5},{8,10},{9,11},{10,... | collective-permute-start | bytes 688136 | tf_op jit(solution)/shard_map/ppermute | solution.py:40
  102.5 6.1 %collective-permute-start.20 = (bf16[64,1792]{1,0:T(8,128)(2,1)S(1)}, bf16[64,1792]{1,0:T(8,128)(2,1)S(1)}, u32[]{:S(2)}, u32[]{:S(2)}) collective-permute-start(bf16[64,1792]{1,0:T(8,128)(2,1)S(1)} %slice_bitcast_fusion.1), channel_id=1, source_target_pairs={{0,16},{1,17},{2,18},{3,19},{4,20},{5,21},{6,22},{7,23},{8,24},{9,... | collective-permute-start | bytes 688136 | tf_op jit(solution)/shard_map/ppermute | solution.py:40
  106.9 8.5 %collective-permute-start.18 = (bf16[64,1792]{1,0:T(8,128)(2,1)S(1)}, bf16[64,1792]{1,0:T(8,128)(2,1)S(1)}, u32[]{:S(2)}, u32[]{:S(2)}) collective-permute-start(bf16[64,1792]{1,0:T(8,128)(2,1)S(1)} %add_convert_fusion.2), channel_id=1, source_target_pairs={{0,4},{1,5},{2,6},{3,7},{4,0},{5,1},{6,2},{7,3},{8,12},{9,13},{10,... | collective-permute-start | bytes 688136 | tf_op jit(solution)/shard_map/ppermute | solution.py:40
  108.7 9.4 %collective-permute-start.21 = (bf16[64,1792]{1,0:T(8,128)(2,1)S(1)}, bf16[64,1792]{1,0:T(8,128)(2,1)S(1)}, u32[]{:S(2)}, u32[]{:S(2)}) collective-permute-start(bf16[64,1792]{1,0:T(8,128)(2,1)S(1)} %fusion.4), channel_id=1, source_target_pairs={{0,12},{1,13},{2,14},{3,15},{4,8},{5,9},{6,10},{7,11},{8,4},{9,5},... | collective-permute-start | bytes 688136 | tf_op jit(solution)/shard_map/ppermute | solution.py:40

commit v7 on v6

--- a/solution.py
+++ b/solution.py
@@ -250,8 +250,6 @@
         return [[hop(x, 2 * j, h) if j or h else x for h in range(nx)] for j in range(ny)]
 
     near_units = spread(lax.optimization_barrier([held[part:]] + own[1:])[0])
-    near = [u for j in range(ny) for u in near_units[j]]
-    far = lax.optimization_barrier([far, near[1]])[0]
     far_units = spread(far)
     chunks = [
         [u for j in range(ny) for u in [own[j]] + near_units[j]],

time: 119 us -> 119 us (level)
  no operation moved by 1% of the time
where the time goes in v7:
time: 119 us
  Pallas kernels  43.9 us (37%)
  starting transfers between devices  34.1 us (29%)
  waiting for transfers between devices  30.2 us (25%)
  local copies, waits for them, and re-layouts  6.31 us (5%)
  other arithmetic  4.15 us (3%)
    pallas_call x2, Pallas kernels, local(): pl.pallas_call(functools.partial(ffn_kernel, levels, x_first, nx, ny, tok...  43.9 us
    ppermute x22, starting transfers between devices, hop(): lax.ppermute(x, ('dp', 'expert'), [(i, i ^ by_x * ne + by) for i in range...  34.1 us
    ppermute x22, waiting for transfers between devices, hop(): lax.ppermute(x, ('dp', 'expert'), [(i, i ^ by_x * ne + by) for i in range...  30.2 us
  transfers between devices with their start and end apart: 22, of which 9 were waited for; matrix products, arithmetic and copies ran while one was open for 7% of the time, Pallas kernels for 37%

profile of v7, /device:TPU:0, one launch (start us, length us, event | category | flops | bytes accessed | tf_op | source)
XLA Modules:
  0.0 118.9 jit_solution(1206542322463896176)
XLA Ops:
  0.0 0.5 collective-permute-start.6
  0.5 0.1 collective-permute-start.7
  0.5 0.8 copy.27
  1.3 0.7 convert_element_type.76
  2.0 0.1 copy.31
  2.1 1.1 concatenate.27.refs_1_
  3.3 0.0 copy-start.12
  3.3 4.1 %collective-permute-start = (bf16[32,3712]{1,0:T(8,128)(2,1)S(1)}, bf16[32,3712]{1,0:T(8,128)(2,1)S(1)}, u32[]{:S(2)}, u32[]{:S(2)}) collective-permute-start(bf16[32,3712]{1,0:T(8,128)(2,1)S(1)} %constant_dynamic-slice_fusion), channel_id=1, source_target_pairs={{0,8},{1,9},{2,10},{3,11},{4,12},{5,13},{6,14},{7,15},{8,0},{9,1},... | collective-permute-start | bytes 712712 | tf_op jit(solution)/shard_map/ppermute | solution.py:40
  7.4 1.5 %collective-permute-start.1 = (bf16[64,3712]{1,0:T(8,128)(2,1)S(1)}, bf16[64,3712]{1,0:T(8,128)(2,1)S(1)}, u32[]{:S(2)}, u32[]{:S(2)}) collective-permute-start(bf16[64,3712]{1,0:T(8,128)(2,1)S(1)} %concatenate.27.refs_1_), channel_id=1, source_target_pairs={{0,2},{1,3},{2,0},{3,1},{4,6},{5,7},{6,4},{7,5},{8,10},{9,11},{10,... | collective-permute-start | bytes 1425416 | tf_op jit(solution)/shard_map/ppermute | solution.py:40
  8.9 0.6 fusion.11
  9.6 0.0 copy-start.13
  9.6 0.1 copy_bitcast_fusion
  9.7 0.1 collective-permute-start.5
  9.8 0.1 and_select_fusion.4
  9.9 0.3 copy-done.13
  10.2 0.2 select_reduce_fusion
  10.4 0.6 and_select_fusion.refs_0_
  11.0 7.5 %collective-permute-done.refs_2_ = bf16[32,3712]{1,0:T(8,128)(2,1)S(1)} collective-permute-done((bf16[32,3712]{1,0:T(8,128)(2,1)S(1)}, bf16[32,3712]{1,0:T(8,128)(2,1)S(1)}, u32[]{:S(2)}, u32[]{:S(2)}) %collective-permute-start) | collective-permute-done | bytes 237600 | tf_op jit(solution)/shard_map/ppermute | solution.py:40
  18.5 1.5 %collective-permute-done.1.refs_4_ = bf16[64,3712]{1,0:T(8,128)(2,1)S(1)} collective-permute-done((bf16[64,3712]{1,0:T(8,128)(2,1)S(1)}, bf16[64,3712]{1,0:T(8,128)(2,1)S(1)}, u32[]{:S(2)}, u32[]{:S(2)}) %collective-permute-start.1) | collective-permute-done | bytes 475168 | tf_op jit(solution)/shard_map/ppermute | solution.py:40
  20.0 1.5 %collective-permute-start.2 = (bf16[32,3712]{1,0:T(8,128)(2,1)S(1)}, bf16[32,3712]{1,0:T(8,128)(2,1)S(1)}, u32[]{:S(2)}, u32[]{:S(2)}) collective-permute-start(bf16[32,3712]{1,0:T(8,128)(2,1)S(1)} %collective-permute-done.refs_2_), channel_id=1, source_target_pairs={{0,16},{1,17},{2,18},{3,19},{4,20},{5,21},{6,22},{7,23},{8,24},{9,... | collective-permute-start | bytes 712712 | tf_op jit(solution)/shard_map/ppermute | solution.py:40
  21.5 1.6 %collective-permute-start.12 = (bf16[64,3712]{1,0:T(8,128)(2,1)S(1)}, bf16[64,3712]{1,0:T(8,128)(2,1)S(1)}, u32[]{:S(2)}, u32[]{:S(2)}) collective-permute-start(bf16[64,3712]{1,0:T(8,128)(2,1)S(1)} %pad_maximum_fusion.1), channel_id=1, source_target_pairs={{0,4},{1,5},{2,6},{3,7},{4,0},{5,1},{6,2},{7,3},{8,12},{9,13},{10,... | collective-permute-start | bytes 1425416 | tf_op jit(solution)/shard_map/ppermute | solution.py:40
  23.1 1.1 collective-permute-done.5
  24.2 2.9 %collective-permute-start.3 = (bf16[32,3712]{1,0:T(8,128)(2,1)S(1)}, bf16[32,3712]{1,0:T(8,128)(2,1)}, u32[]{:S(2)}, u32[]{:S(2)}) collective-permute-start(bf16[32,3712]{1,0:T(8,128)(2,1)S(1)} %collective-permute-done.refs_2_), channel_id=1, source_target_pairs={{0,2},{1,3},{2,0},{3,1},{4,6},{5,7},{6,4},{7,5},{8,10},{9,11},{10,... | collective-permute-start | bytes 712712 | tf_op jit(solution)/shard_map/ppermute | solution.py:40
  27.1 1.9 %collective-permute-start.4 = (bf16[32,3712]{1,0:T(8,128)(2,1)S(1)}, bf16[32,3712]{1,0:T(8,128)(2,1)}, u32[]{:S(2)}, u32[]{:S(2)}) collective-permute-start(bf16[32,3712]{1,0:T(8,128)(2,1)S(1)} %collective-permute-done.refs_2_), channel_id=1, source_target_pairs={{0,18},{1,19},{2,16},{3,17},{4,22},{5,23},{6,20},{7,21},{8,26},{9,... | collective-permute-start | bytes 712712 | tf_op jit(solution)/shard_map/ppermute | solution.py:40
  29.0 0.1 maximum_bitcast_fusion
  29.2 0.1 slice.45
  29.2 0.8 slice.46
  30.1 1.3 %copy.34 = bf16[128,3584]{0,1:T(8,128)(2,1)} copy(bf16[128,3584]{1,0:T(8,128)(2,1)S(1)} %bitcast.34) | data formatting | bytes 1835008 | tf_op jit(solution)/shard_map/reshape | solution.py:229
  31.3 1.6 %collective-permute-done.12.refs_1_ = bf16[64,3712]{1,0:T(8,128)(2,1)S(1)} collective-permute-done((bf16[64,3712]{1,0:T(8,128)(2,1)S(1)}, bf16[64,3712]{1,0:T(8,128)(2,1)S(1)}, u32[]{:S(2)}, u32[]{:S(2)}) %collective-permute-start.12) | collective-permute-done | bytes 475168 | tf_op jit(solution)/shard_map/ppermute | solution.py:40
  33.0 0.5 collective-permute-start.13
  33.5 4.9 %collective-permute-done.3.refs_5_ = bf16[32,3712]{1,0:T(8,128)(2,1)} collective-permute-done((bf16[32,3712]{1,0:T(8,128)(2,1)S(1)}, bf16[32,3712]{1,0:T(8,128)(2,1)}, u32[]{:S(2)}, u32[]{:S(2)}) %collective-permute-start.3) | collective-permute-done | bytes 237600 | tf_op jit(solution)/shard_map/ppermute | solution.py:40
  38.4 1.7 %collective-permute-start.14 = (bf16[64,3712]{1,0:T(8,128)(2,1)S(1)}, bf16[64,3712]{1,0:T(8,128)(2,1)S(1)}, u32[]{:S(2)}, u32[]{:S(2)}) collective-permute-start(bf16[64,3712]{1,0:T(8,128)(2,1)S(1)} %collective-permute-done.12.refs_1_), channel_id=1, source_target_pairs={{0,2},{1,3},{2,0},{3,1},{4,6},{5,7},{6,4},{7,5},{8,10},{9,11},{10,... | collective-permute-start | bytes 1425416 | tf_op jit(solution)/shard_map/ppermute | solution.py:40
  40.1 0.0 collective-permute-done.4.refs_6_
  40.1 1.4 %collective-permute-start.15 = (bf16[64,3712]{1,0:T(8,128)(2,1)S(1)}, bf16[64,3712]{1,0:T(8,128)(2,1)S(1)}, u32[]{:S(2)}, u32[]{:S(2)}) collective-permute-start(bf16[64,3712]{1,0:T(8,128)(2,1)S(1)} %collective-permute-done.12.refs_1_), channel_id=1, source_target_pairs={{0,18},{1,19},{2,16},{3,17},{4,22},{5,23},{6,20},{7,21},{8,26},{9,... | collective-permute-start | bytes 1425416 | tf_op jit(solution)/shard_map/ppermute | solution.py:40
  41.5 0.0 collective-permute-done.7.refs_12_.refs_10_
  41.6 0.0 collective-permute-done.6.refs_10_.refs_8_
  41.6 21.7 %shard_map.82 = (bf16[2,64,1792]{2,1,0:T(8,128)(2,1)}, bf16[2,64,1792]{2,1,0:T(8,128)(2,1)}, bf16[2,64,1792]{2,1,0:T(8,128)(2,1)}, bf16[2,64,1792]{2,1,0:T(8,128)(2,1)}) custom-call(s32[4]{0:T(128)} %and_select_fusion.refs_0_, bf16[64,3712]{1,0:T(8,128)(2,1)} %copy-done, bf16[32,3712]{1,0:T(8,128)(2,1)} %copy-done.3, bf16[32,3712]{1,0:T(8,128)(2,1)} %copy-done.11, ...), custom_call_target="tpu_custom_call" | custom-call | flops 11626610688 | bytes 49545216 | tf_op jit(solution)/shard_map/pallas_call | solution.py:282
  63.3 1.6 %collective-permute-start.10 = (bf16[2,64,1792]{2,1,0:T(8,128)(2,1)}, bf16[2,64,1792]{2,1,0:T(8,128)(2,1)S(1)}, u32[]{:S(2)}, u32[]{:S(2)}) collective-permute-start(bf16[2,64,1792]{2,1,0:T(8,128)(2,1)} %get-tuple-element.24), channel_id=1, source_target_pairs={{0,18},{1,19},{2,16},{3,17},{4,22},{5,23},{6,20},{7,21},{8,26},{9,... | collective-permute-start | bytes 1376264 | tf_op jit(solution)/shard_map/ppermute | solution.py:40
  64.8 1.5 %collective-permute-start.8 = (bf16[2,64,1792]{2,1,0:T(8,128)(2,1)}, bf16[2,64,1792]{2,1,0:T(8,128)(2,1)S(1)}, u32[]{:S(2)}, u32[]{:S(2)}) collective-permute-start(bf16[2,64,1792]{2,1,0:T(8,128)(2,1)} %get-tuple-element.22), channel_id=1, source_target_pairs={{0,16},{1,17},{2,18},{3,19},{4,20},{5,21},{6,22},{7,23},{8,24},{9,... | collective-permute-start | bytes 1376264 | tf_op jit(solution)/shard_map/ppermute | solution.py:40
  66.3 0.0 collective-permute-done.13.refs_2_
  66.3 0.5 collective-permute-start.9
  66.8 0.0 collective-permute-done.14.refs_3_
  66.8 0.3 copy-done.6
  67.1 0.5 copy-done.7
  67.6 0.2 copy-done.8
  67.8 22.2 %shard_map.83 = (bf16[128,1792]{1,0:T(8,128)(2,1)}, bf16[128,1792]{1,0:T(8,128)(2,1)}, bf16[2,64,1792]{2,1,0:T(8,128)(2,1)}, bf16[2,64,1792]{2,1,0:T(8,128)(2,1)}) custom-call(s32[4]{0:T(128)} %and_select_fusion.refs_0_, bf16[64,3712]{1,0:T(8,128)(2,1)} %copy-done.5, bf16[64,3712]{1,0:T(8,128)(2,1)} %copy-done.6, bf16[64,3712]{1,0:T(8,128)(2,1)} %copy-done.7, ...), custom_call_target="tpu_custom_call" | custom-call | flops 11626610688 | bytes 49545216 | tf_op jit(solution)/shard_map/pallas_call | solution.py:282
  90.1 0.4 collective-permute-start.16
  90.4 1.7 %collective-permute-start.19 = (bf16[2,64,1792]{2,1,0:T(8,128)(2,1)}, bf16[2,64,1792]{2,1,0:T(8,128)(2,1)S(1)}, u32[]{:S(2)}, u32[]{:S(2)}) collective-permute-start(bf16[2,64,1792]{2,1,0:T(8,128)(2,1)} %get-tuple-element.32), channel_id=1, source_target_pairs={{0,2},{1,3},{2,0},{3,1},{4,6},{5,7},{6,4},{7,5},{8,10},{9,11},{10,... | collective-permute-start | bytes 1376264 | tf_op jit(solution)/shard_map/ppermute | solution.py:40
  92.2 1.2 %convert_add_fusion = f32[2,64,1792]{2,1,0:T(8,128)S(1)} fusion(bf16[2,64,1792]{2,1,0:T(8,128)(2,1)S(1)} %collective-permute-done.10, bf16[2,64,1792]{2,1,0:T(8,128)(2,1)} %collective-permute-done.9, bf16[2,64,1792]{2,1,0:T(8,128)(2,1)S(1)} %collective-permute-done.8, bf16[2,64,1792]{2,1,0:T(8,128)(2,1)S(1)} %copy-done.1), kind=kLoop, calls=%fused_computation.3 | loop fusion | flops 1605632 | bytes 2752512 | tf_op jit(solution)/shard_map/add | solution.py:262
  93.5 2.6 %collective-permute-start.11 = (bf16[64,1792]{1,0:T(8,128)(2,1)S(1)}, bf16[64,1792]{1,0:T(8,128)(2,1)S(1)}, u32[]{:S(2)}, u32[]{:S(2)}) collective-permute-start(bf16[64,1792]{1,0:T(8,128)(2,1)S(1)} %fusion.5), channel_id=1, source_target_pairs={{0,8},{1,9},{2,10},{3,11},{4,12},{5,13},{6,14},{7,15},{8,0},{9,1},... | collective-permute-start | bytes 688136 | tf_op jit(solution)/shard_map/ppermute | solution.py:40
  96.1 4.6 %collective-permute-done.16 = bf16[128,1792]{1,0:T(8,128)(2,1)S(1)} collective-permute-done((bf16[128,1792]{1,0:T(8,128)(2,1)}, bf16[128,1792]{1,0:T(8,128)(2,1)S(1)}, u32[]{:S(2)}, u32[]{:S(2)}) %collective-permute-start.16) | collective-permute-done | bytes 458784 | tf_op jit(solution)/shard_map/ppermute | solution.py:40
  100.7 0.1 add_convert_fusion.1
  100.8 1.6 %collective-permute-start.17 = (bf16[64,1792]{1,0:T(8,128)(2,1)S(1)}, bf16[64,1792]{1,0:T(8,128)(2,1)S(1)}, u32[]{:S(2)}, u32[]{:S(2)}) collective-permute-start(bf16[64,1792]{1,0:T(8,128)(2,1)S(1)} %slice.50), channel_id=1, source_target_pairs={{0,2},{1,3},{2,0},{3,1},{4,6},{5,7},{6,4},{7,5},{8,10},{9,11},{10,... | collective-permute-start | bytes 688136 | tf_op jit(solution)/shard_map/ppermute | solution.py:40
  102.4 0.1 add_convert_fusion
  102.5 1.0 collective-permute-start.20
  103.6 3.3 %collective-permute-done.17 = bf16[64,1792]{1,0:T(8,128)(2,1)S(1)} collective-permute-done((bf16[64,1792]{1,0:T(8,128)(2,1)S(1)}, bf16[64,1792]{1,0:T(8,128)(2,1)S(1)}, u32[]{:S(2)}, u32[]{:S(2)}) %collective-permute-start.17) | collective-permute-done | bytes 229408 | tf_op jit(solution)/shard_map/ppermute | solution.py:40
  106.9 0.1 add_convert_fusion.2
  106.9 1.6 %collective-permute-start.18 = (bf16[64,1792]{1,0:T(8,128)(2,1)S(1)}, bf16[64,1792]{1,0:T(8,128)(2,1)S(1)}, u32[]{:S(2)}, u32[]{:S(2)}) collective-permute-start(bf16[64,1792]{1,0:T(8,128)(2,1)S(1)} %add_convert_fusion.2), channel_id=1, source_target_pairs={{0,4},{1,5},{2,6},{3,7},{4,0},{5,1},{6,2},{7,3},{8,12},{9,13},{10,... | collective-permute-start | bytes 688136 | tf_op jit(solution)/shard_map/ppermute | solution.py:40
  108.6 0.0 collective-permute-done.20
  108.6 0.1 fusion.4
  108.7 3.7 %collective-permute-start.21 = (bf16[64,1792]{1,0:T(8,128)(2,1)S(1)}, bf16[64,1792]{1,0:T(8,128)(2,1)S(1)}, u32[]{:S(2)}, u32[]{:S(2)}) collective-permute-start(bf16[64,1792]{1,0:T(8,128)(2,1)S(1)} %fusion.4), channel_id=1, source_target_pairs={{0,12},{1,13},{2,14},{3,15},{4,8},{5,9},{6,10},{7,11},{8,4},{9,5},... | collective-permute-start | bytes 688136 | tf_op jit(solution)/shard_map/ppermute | solution.py:40
  112.3 3.1 %collective-permute-done.18 = bf16[64,1792]{1,0:T(8,128)(2,1)S(1)} collective-permute-done((bf16[64,1792]{1,0:T(8,128)(2,1)S(1)}, bf16[64,1792]{1,0:T(8,128)(2,1)S(1)}, u32[]{:S(2)}, u32[]{:S(2)}) %collective-permute-start.18) | collective-permute-done | bytes 229408 | tf_op jit(solution)/shard_map/ppermute | solution.py:40
  115.5 2.6 %collective-permute-done.21 = bf16[64,1792]{1,0:T(8,128)(2,1)S(1)} collective-permute-done((bf16[64,1792]{1,0:T(8,128)(2,1)S(1)}, bf16[64,1792]{1,0:T(8,128)(2,1)S(1)}, u32[]{:S(2)}, u32[]{:S(2)}) %collective-permute-start.21) | collective-permute-done | bytes 229408 | tf_op jit(solution)/shard_map/ppermute | solution.py:40
  118.1 0.8 fusion.3
  (38 shorter events, 0.3 us)
Async XLA Ops:
  0.0 8.9 %copy-start.2 = (bf16[32,2,3584]{2,1,0:T(2,128)(2,1)S(1)}, bf16[32,2,3584]{2,1,0:T(2,128)(2,1)}, u32[]{:S(2)}) copy-start(bf16[32,2,3584]{2,1,0:T(2,128)(2,1)} %param.14) | copy-start | bytes 1376260
  0.0 41.6 %collective-permute-start.6 = (bf16[2,2,3584,512]{3,2,1,0:T(8,128)(2,1)}, bf16[2,2,3584,512]{3,2,1,0:T(8,128)(2,1)}, u32[]{:S(2)}, u32[]{:S(2)}) collective-permute-start(bf16[2,2,3584,512]{3,2,1,0:T(8,128)(2,1)} %refs_7_.1), channel_id=1, source_target_pairs={{0,1},{1,0},{2,3},{3,2},{4,5},{5,4},{6,7},{7,6},{8,9},{9,8},{10,11... | collective-permute-start | bytes 44040200 | tf_op jit(solution)/shard_map/ppermute | solution.py:40
  0.5 41.1 %collective-permute-start.7 = (bf16[2,512,3584]{2,1,0:T(8,128)(2,1)}, bf16[2,512,3584]{2,1,0:T(8,128)(2,1)}, u32[]{:S(2)}, u32[]{:S(2)}) collective-permute-start(bf16[2,512,3584]{2,1,0:T(8,128)(2,1)} %refs_9_.3), channel_id=1, source_target_pairs={{0,1},{1,0},{2,3},{3,2},{4,5},{5,4},{6,7},{7,6},{8,9},{9,8},{10,11... | collective-permute-start | bytes 22020104 | tf_op jit(solution)/shard_map/ppermute | solution.py:40
  3.3 6.4 %copy-start = (bf16[64,3712]{1,0:T(8,128)(2,1)}, bf16[64,3712]{1,0:T(8,128)(2,1)S(1)}, u32[]{:S(2)}) copy-start(bf16[64,3712]{1,0:T(8,128)(2,1)S(1)} %concatenate.27.refs_1_) | copy-start | bytes 1425412
  3.3 6.4 %copy-start.12 = (bf16[32,3584]{1,0:T(8,128)(2,1)S(1)}, bf16[32,3584]{1,0:T(8,128)(2,1)}, u32[]{:S(2)}) copy-start(bf16[32,3584]{1,0:T(8,128)(2,1)} %param.15) | copy-start | bytes 688132
  3.3 15.2 %collective-permute-start = (bf16[32,3712]{1,0:T(8,128)(2,1)S(1)}, bf16[32,3712]{1,0:T(8,128)(2,1)S(1)}, u32[]{:S(2)}, u32[]{:S(2)}) collective-permute-start(bf16[32,3712]{1,0:T(8,128)(2,1)S(1)} %constant_dynamic-slice_fusion), channel_id=1, source_target_pairs={{0,8},{1,9},{2,10},{3,11},{4,12},{5,13},{6,14},{7,15},{8,0},{9,1},... | collective-permute-start | bytes 712712 | tf_op jit(solution)/shard_map/ppermute | solution.py:40
  7.4 12.6 %collective-permute-start.1 = (bf16[64,3712]{1,0:T(8,128)(2,1)S(1)}, bf16[64,3712]{1,0:T(8,128)(2,1)S(1)}, u32[]{:S(2)}, u32[]{:S(2)}) collective-permute-start(bf16[64,3712]{1,0:T(8,128)(2,1)S(1)} %concatenate.27.refs_1_), channel_id=1, source_target_pairs={{0,2},{1,3},{2,0},{3,1},{4,6},{5,7},{6,4},{7,5},{8,10},{9,11},{10,... | collective-permute-start | bytes 1425416 | tf_op jit(solution)/shard_map/ppermute | solution.py:40
  9.6 0.7 copy-start.13
  9.7 14.5 %collective-permute-start.5 = (bf16[96,3584]{1,0:T(8,128)(2,1)S(1)}, bf16[96,3584]{1,0:T(8,128)(2,1)S(1)}, u32[]{:S(2)}, u32[]{:S(2)}) collective-permute-start(bf16[96,3584]{1,0:T(8,128)(2,1)S(1)} %pad_maximum_fusion), channel_id=1, source_target_pairs={{0,1},{1,0},{2,3},{3,2},{4,5},{5,4},{6,7},{7,6},{8,9},{9,8},{10,11... | collective-permute-start | bytes 2064392 | tf_op jit(solution)/shard_map/ppermute | solution.py:40
  18.5 10.6 %copy-start.3 = (bf16[32,3712]{1,0:T(8,128)(2,1)}, bf16[32,3712]{1,0:T(8,128)(2,1)S(1)}, u32[]{:S(2)}) copy-start(bf16[32,3712]{1,0:T(8,128)(2,1)S(1)} %collective-permute-done.refs_2_) | copy-start | bytes 712708
  20.0 9.2 %copy-start.4 = (bf16[64,3712]{1,0:T(8,128)(2,1)}, bf16[64,3712]{1,0:T(8,128)(2,1)S(1)}, u32[]{:S(2)}) copy-start(bf16[64,3712]{1,0:T(8,128)(2,1)S(1)} %collective-permute-done.1.refs_4_) | copy-start | bytes 1425412
  20.0 7.1 %collective-permute-start.2 = (bf16[32,3712]{1,0:T(8,128)(2,1)S(1)}, bf16[32,3712]{1,0:T(8,128)(2,1)S(1)}, u32[]{:S(2)}, u32[]{:S(2)}) collective-permute-start(bf16[32,3712]{1,0:T(8,128)(2,1)S(1)} %collective-permute-done.refs_2_), channel_id=1, source_target_pairs={{0,16},{1,17},{2,18},{3,19},{4,20},{5,21},{6,22},{7,23},{8,24},{9,... | collective-permute-start | bytes 712712 | tf_op jit(solution)/shard_map/ppermute | solution.py:40
  21.5 11.5 %collective-permute-start.12 = (bf16[64,3712]{1,0:T(8,128)(2,1)S(1)}, bf16[64,3712]{1,0:T(8,128)(2,1)S(1)}, u32[]{:S(2)}, u32[]{:S(2)}) collective-permute-start(bf16[64,3712]{1,0:T(8,128)(2,1)S(1)} %pad_maximum_fusion.1), channel_id=1, source_target_pairs={{0,4},{1,5},{2,6},{3,7},{4,0},{5,1},{6,2},{7,3},{8,12},{9,13},{10,... | collective-permute-start | bytes 1425416 | tf_op jit(solution)/shard_map/ppermute | solution.py:40
  24.2 14.2 %collective-permute-start.3 = (bf16[32,3712]{1,0:T(8,128)(2,1)S(1)}, bf16[32,3712]{1,0:T(8,128)(2,1)}, u32[]{:S(2)}, u32[]{:S(2)}) collective-permute-start(bf16[32,3712]{1,0:T(8,128)(2,1)S(1)} %collective-permute-done.refs_2_), channel_id=1, source_target_pairs={{0,2},{1,3},{2,0},{3,1},{4,6},{5,7},{6,4},{7,5},{8,10},{9,11},{10,... | collective-permute-start | bytes 712712 | tf_op jit(solution)/shard_map/ppermute | solution.py:40
  27.1 1.9 %copy-start.11 = (bf16[32,3712]{1,0:T(8,128)(2,1)}, bf16[32,3712]{1,0:T(8,128)(2,1)S(1)}, u32[]{:S(2)}) copy-start(bf16[32,3712]{1,0:T(8,128)(2,1)S(1)} %collective-permute-done.2.refs_3_) | copy-start | bytes 712708
  27.1 13.0 %collective-permute-start.4 = (bf16[32,3712]{1,0:T(8,128)(2,1)S(1)}, bf16[32,3712]{1,0:T(8,128)(2,1)}, u32[]{:S(2)}, u32[]{:S(2)}) collective-permute-start(bf16[32,3712]{1,0:T(8,128)(2,1)S(1)} %collective-permute-done.refs_2_), channel_id=1, source_target_pairs={{0,18},{1,19},{2,16},{3,17},{4,22},{5,23},{6,20},{7,21},{8,26},{9,... | collective-permute-start | bytes 712712 | tf_op jit(solution)/shard_map/ppermute | solution.py:40
  33.0 30.3 %copy-start.5 = (bf16[64,3712]{1,0:T(8,128)(2,1)}, bf16[64,3712]{1,0:T(8,128)(2,1)S(1)}, u32[]{:S(2)}) copy-start(bf16[64,3712]{1,0:T(8,128)(2,1)S(1)} %collective-permute-done.12.refs_1_) | copy-start | bytes 1425412
  33.0 33.3 %collective-permute-start.13 = (bf16[64,3712]{1,0:T(8,128)(2,1)S(1)}, bf16[64,3712]{1,0:T(8,128)(2,1)S(1)}, u32[]{:S(2)}, u32[]{:S(2)}) collective-permute-start(bf16[64,3712]{1,0:T(8,128)(2,1)S(1)} %collective-permute-done.12.refs_1_), channel_id=1, source_target_pairs={{0,16},{1,17},{2,18},{3,19},{4,20},{5,21},{6,22},{7,23},{8,24},{9,... | collective-permute-start | bytes 1425416 | tf_op jit(solution)/shard_map/ppermute | solution.py:40
  38.4 28.5 %collective-permute-start.14 = (bf16[64,3712]{1,0:T(8,128)(2,1)S(1)}, bf16[64,3712]{1,0:T(8,128)(2,1)S(1)}, u32[]{:S(2)}, u32[]{:S(2)}) collective-permute-start(bf16[64,3712]{1,0:T(8,128)(2,1)S(1)} %collective-permute-done.12.refs_1_), channel_id=1, source_target_pairs={{0,2},{1,3},{2,0},{3,1},{4,6},{5,7},{6,4},{7,5},{8,10},{9,11},{10,... | collective-permute-start | bytes 1425416 | tf_op jit(solution)/shard_map/ppermute | solution.py:40
  40.1 26.7 %collective-permute-start.15 = (bf16[64,3712]{1,0:T(8,128)(2,1)S(1)}, bf16[64,3712]{1,0:T(8,128)(2,1)S(1)}, u32[]{:S(2)}, u32[]{:S(2)}) collective-permute-start(bf16[64,3712]{1,0:T(8,128)(2,1)S(1)} %collective-permute-done.12.refs_1_), channel_id=1, source_target_pairs={{0,18},{1,19},{2,16},{3,17},{4,22},{5,23},{6,20},{7,21},{8,26},{9,... | collective-permute-start | bytes 1425416 | tf_op jit(solution)/shard_map/ppermute | solution.py:40
  63.3 26.8 %collective-permute-start.10 = (bf16[2,64,1792]{2,1,0:T(8,128)(2,1)}, bf16[2,64,1792]{2,1,0:T(8,128)(2,1)S(1)}, u32[]{:S(2)}, u32[]{:S(2)}) collective-permute-start(bf16[2,64,1792]{2,1,0:T(8,128)(2,1)} %get-tuple-element.24), channel_id=1, source_target_pairs={{0,18},{1,19},{2,16},{3,17},{4,22},{5,23},{6,20},{7,21},{8,26},{9,... | collective-permute-start | bytes 1376264 | tf_op jit(solution)/shard_map/ppermute | solution.py:40
  64.8 25.2 %collective-permute-start.8 = (bf16[2,64,1792]{2,1,0:T(8,128)(2,1)}, bf16[2,64,1792]{2,1,0:T(8,128)(2,1)S(1)}, u32[]{:S(2)}, u32[]{:S(2)}) collective-permute-start(bf16[2,64,1792]{2,1,0:T(8,128)(2,1)} %get-tuple-element.22), channel_id=1, source_target_pairs={{0,16},{1,17},{2,18},{3,19},{4,20},{5,21},{6,22},{7,23},{8,24},{9,... | collective-permute-start | bytes 1376264 | tf_op jit(solution)/shard_map/ppermute | solution.py:40
  66.3 0.8 copy-start.6
  66.3 23.7 %collective-permute-start.9 = (bf16[2,64,1792]{2,1,0:T(8,128)(2,1)}, bf16[2,64,1792]{2,1,0:T(8,128)(2,1)}, u32[]{:S(2)}, u32[]{:S(2)}) collective-permute-start(bf16[2,64,1792]{2,1,0:T(8,128)(2,1)} %get-tuple-element.23), channel_id=1, source_target_pairs={{0,2},{1,3},{2,0},{3,1},{4,6},{5,7},{6,4},{7,5},{8,10},{9,11},{10,... | collective-permute-start | bytes 1376264 | tf_op jit(solution)/shard_map/ppermute | solution.py:40
  66.8 0.8 copy-start.7
  66.8 1.0 copy-start.8
  67.8 24.3 %copy-start.1 = (bf16[2,64,1792]{2,1,0:T(8,128)(2,1)S(1)}, bf16[2,64,1792]{2,1,0:T(8,128)(2,1)}, u32[]{:S(2)}) copy-start(bf16[2,64,1792]{2,1,0:T(8,128)(2,1)} %get-tuple-element.21.refs_11_) | copy-start | bytes 1376260
  90.0 10.6 %copy-start.10 = (bf16[128,1792]{1,0:T(8,128)(2,1)S(1)}, bf16[128,1792]{1,0:T(8,128)(2,1)}, u32[]{:S(2)}) copy-start(bf16[128,1792]{1,0:T(8,128)(2,1)} %get-tuple-element.29) | copy-start | bytes 1376260
  90.1 10.6 %collective-permute-start.16 = (bf16[128,1792]{1,0:T(8,128)(2,1)}, bf16[128,1792]{1,0:T(8,128)(2,1)S(1)}, u32[]{:S(2)}, u32[]{:S(2)}) collective-permute-start(bf16[128,1792]{1,0:T(8,128)(2,1)} %get-tuple-element.30), channel_id=1, source_target_pairs={{0,16},{1,17},{2,18},{3,19},{4,20},{5,21},{6,22},{7,23},{8,24},{9,... | collective-permute-start | bytes 1376264 | tf_op jit(solution)/shard_map/ppermute | solution.py:40
  90.4 12.0 %collective-permute-start.19 = (bf16[2,64,1792]{2,1,0:T(8,128)(2,1)}, bf16[2,64,1792]{2,1,0:T(8,128)(2,1)S(1)}, u32[]{:S(2)}, u32[]{:S(2)}) collective-permute-start(bf16[2,64,1792]{2,1,0:T(8,128)(2,1)} %get-tuple-element.32), channel_id=1, source_target_pairs={{0,2},{1,3},{2,0},{3,1},{4,6},{5,7},{6,4},{7,5},{8,10},{9,11},{10,... | collective-permute-start | bytes 1376264 | tf_op jit(solution)/shard_map/ppermute | solution.py:40
  93.4 9.0 %copy-start.9 = (bf16[2,64,1792]{2,1,0:T(8,128)(2,1)S(1)}, bf16[2,64,1792]{2,1,0:T(8,128)(2,1)}, u32[]{:S(2)}) copy-start(bf16[2,64,1792]{2,1,0:T(8,128)(2,1)} %get-tuple-element.31) | copy-start | bytes 1376260
  93.5 18.9 %collective-permute-start.11 = (bf16[64,1792]{1,0:T(8,128)(2,1)S(1)}, bf16[64,1792]{1,0:T(8,128)(2,1)S(1)}, u32[]{:S(2)}, u32[]{:S(2)}) collective-permute-start(bf16[64,1792]{1,0:T(8,128)(2,1)S(1)} %fusion.5), channel_id=1, source_target_pairs={{0,8},{1,9},{2,10},{3,11},{4,12},{5,13},{6,14},{7,15},{8,0},{9,1},... | collective-permute-start | bytes 688136 | tf_op jit(solution)/shard_map/ppermute | solution.py:40
  100.8 6.1 %collective-permute-start.17 = (bf16[64,1792]{1,0:T(8,128)(2,1)S(1)}, bf16[64,1792]{1,0:T(8,128)(2,1)S(1)}, u32[]{:S(2)}, u32[]{:S(2)}) collective-permute-start(bf16[64,1792]{1,0:T(8,128)(2,1)S(1)} %slice.50), channel_id=1, source_target_pairs={{0,2},{1,3},{2,0},{3,1},{4,6},{5,7},{6,4},{7,5},{8,10},{9,11},{10,... | collective-permute-start | bytes 688136 | tf_op jit(solution)/shard_map/ppermute | solution.py:40
  102.5 6.1 %collective-permute-start.20 = (bf16[64,1792]{1,0:T(8,128)(2,1)S(1)}, bf16[64,1792]{1,0:T(8,128)(2,1)S(1)}, u32[]{:S(2)}, u32[]{:S(2)}) collective-permute-start(bf16[64,1792]{1,0:T(8,128)(2,1)S(1)} %slice_bitcast_fusion.1), channel_id=1, source_target_pairs={{0,16},{1,17},{2,18},{3,19},{4,20},{5,21},{6,22},{7,23},{8,24},{9,... | collective-permute-start | bytes 688136 | tf_op jit(solution)/shard_map/ppermute | solution.py:40
  106.9 8.5 %collective-permute-start.18 = (bf16[64,1792]{1,0:T(8,128)(2,1)S(1)}, bf16[64,1792]{1,0:T(8,128)(2,1)S(1)}, u32[]{:S(2)}, u32[]{:S(2)}) collective-permute-start(bf16[64,1792]{1,0:T(8,128)(2,1)S(1)} %add_convert_fusion.2), channel_id=1, source_target_pairs={{0,4},{1,5},{2,6},{3,7},{4,0},{5,1},{6,2},{7,3},{8,12},{9,13},{10,... | collective-permute-start | bytes 688136 | tf_op jit(solution)/shard_map/ppermute | solution.py:40
  108.7 9.4 %collective-permute-start.21 = (bf16[64,1792]{1,0:T(8,128)(2,1)S(1)}, bf16[64,1792]{1,0:T(8,128)(2,1)S(1)}, u32[]{:S(2)}, u32[]{:S(2)}) collective-permute-start(bf16[64,1792]{1,0:T(8,128)(2,1)S(1)} %fusion.4), channel_id=1, source_target_pairs={{0,12},{1,13},{2,14},{3,15},{4,8},{5,9},{6,10},{7,11},{8,4},{9,5},... | collective-permute-start | bytes 688136 | tf_op jit(solution)/shard_map/ppermute | solution.py:40
